TPU v7x, 32 devices: a whole 2x2x4 slice. The times are simulated.
32 devices in a mesh: region: 8 (over z, y), sub: 4 (over x, core).
Axes of the slice: x: 2, y: 2, z: 4, core: 2. Of those that a mesh axis runs over, the one named last changes fastest.
Arguments:
- mode_rows: bfloat16 [16384, 4096], P(('region', 'sub')), may hold values from -0.09375 to 0.09375
- input_rows: bfloat16 [512, 4096], P(('region', 'sub')), may hold values from -0.25 to 0.25
- input_factor: bfloat16 [512, 128], P(('region', 'sub')), may hold values from -6 to 6
- mode_freq: float32 [4096], replicated, may hold values from 0.5 to 2
- mode_damping: float32 [4096], replicated, may hold values from 0.02 to 0.2
- line_freq: float32 [2], replicated, may hold values from 0.6 to 1.6
- boundary_rows: int32 [4096], P(('region', 'sub')), may hold values from 0 to 511
- connectivity: int32 [4, 16384], P(None, ('region', 'sub')), may hold values from 0 to 639
- stress_coef: float32 [4, 16384], P(None, ('region', 'sub')), may hold values from -3 to 3
Outputs:
- stress_psd: float32 [2, 16384], P(None, ('region', 'sub'))
Inputs may be any that keep to these rules, and one draw needn't show every extreme that they name: `boundary_rows`: local row numbers of the sending device. `connectivity`: rows of the node table of the element's device.
All inputs are finite; a program needn't handle non-finite values.
Results may differ from a plain program's by a relative error of at most 0.0013.
Values may be sent and summed in bfloat16 or wider, within the bound.
No kernel may reach another device: no remote copies, remote signals or barrier semaphores. Data moves between devices by JAX's collectives and lax.ppermute only.
A program may use at most 64 MiB of HBM per device.

v0:
```python
import functools
import math

import jax
import jax.numpy as jnp
from jax import lax
from jax.experimental import pallas as pl
from jax.experimental.pallas import tpu as pltpu
from jax.sharding import PartitionSpec as P

AXES = ("region", "sub")
LANES = 128
F32 = jnp.float32
BF16 = jnp.bfloat16
VMEM_BYTES = 24 * 1024 * 1024
LONG = 8 * 1024**3
FAST_SHAPE = (8, 4)


def whole(*_):
    return pl.BlockSpec(memory_space=pltpu.VMEM)


def modal_gain(freq, damping, omega):
    detune = freq * freq - omega * omega
    damped = 2.0 * damping * freq * omega
    magnitude = detune * detune + damped * damped
    return detune / magnitude, -damped / magnitude


def slab_of(device):
    return device % 2 * 8 + device // 2 % 8


def ones_kernel(ones_ref):
    ones_ref[...] = jnp.ones_like(ones_ref)


def pack_kernel(ones_ref, line_ref, freq_ref, damping_ref, rows_ref, factor_ref, sent_ref, gain_ref):
    devices, _, width = sent_ref.shape
    rows = rows_ref.shape[0]
    parts = sent_ref.shape[1] // rows - 1
    lines = line_ref.shape[1]
    factor = factor_ref[...]
    for device in range(devices):
        for part in range(parts):
            here = (slab_of(device) * parts + part) * width
            sent_ref[device, part * rows : (part + 1) * rows, :] = rows_ref[:, here : here + width]
        sent_ref[device, parts * rows :, :] = factor
    slab = slab_of(lax.axis_index(AXES))
    one = ones_ref[0:1, :]
    for part in range(parts):
        here = pl.ds(slab * parts + part, 1)
        for line in range(lines):
            omega = line_ref[:, line : line + 1]
            real, imag = modal_gain(freq_ref[here, :], damping_ref[here, :], omega)
            row = 2 * (part * lines + line)
            gain_ref[row : row + 1, :] = real * one
            gain_ref[row + 1 : row + 2, :] = imag * one


def pseudo_kernel(gain_ref, got_ref, pseudo_ref, *, rows, lines):
    devices, tall, width = got_ref.shape
    parts = tall // rows - 1
    factor = got_ref[:, parts * rows :, :].reshape(devices * rows, width)
    columns = width // lines
    half = columns // 2
    for part in range(parts):
        shapes = got_ref[:, part * rows : (part + 1) * rows, :].reshape(devices * rows, width)
        forced = lax.dot_general(
            factor, shapes, (((0,), (0,)), ((), ())), preferred_element_type=F32
        )
        pieces = []
        for line in range(lines):
            row = 2 * (part * lines + line)
            gain_real = gain_ref[row : row + 1, :]
            gain_imag = gain_ref[row + 1 : row + 2, :]
            real = forced[line * columns : line * columns + half]
            imag = forced[line * columns + half : (line + 1) * columns]
            pieces.append(gain_real * real - gain_imag * imag)
            pieces.append(gain_real * imag + gain_imag * real)
        pseudo = jnp.concatenate(pieces, axis=0).T.astype(BF16)
        for copy in range(pseudo_ref.shape[0]):
            pseudo_ref[copy, part * width : (part + 1) * width, :] = pseudo


def first_kernel(boundary_ref, modes_ref, pseudo_ref, total_ref, part_ref, picked_ref):
    rows = modes_ref.shape[0]
    depth = pseudo_ref.shape[0]
    odd = lax.axis_index(AXES) % 2
    mine = pl.ds(pl.multiple_of(odd * depth, depth), depth)
    other = pl.ds(pl.multiple_of((1 - odd) * depth, depth), depth)
    total = jnp.dot(modes_ref[:, mine], pseudo_ref[...], preferred_element_type=F32)
    total_ref[...] = total
    pick = lax.broadcasted_iota(jnp.int32, (rows, boundary_ref.shape[1]), 0) == boundary_ref[...]
    pick = pick.astype(F32).T
    part_ref[...] = jnp.dot(
        pick, total, precision=lax.Precision.HIGHEST, preferred_element_type=F32
    )
    picked_ref[...] = jnp.dot(
        pick.astype(BF16), modes_ref[:, other], preferred_element_type=F32
    ).astype(BF16)


def export_kernel(part_ref, picked_ref, pseudo_ref, far_ref, near_ref):
    export = part_ref[...] + jnp.dot(
        picked_ref[...], pseudo_ref[...], preferred_element_type=F32
    )
    export = export.astype(BF16)
    odd = lax.axis_index(AXES) % 2 == 1
    rim = far_ref.shape[0]
    far_ref[...] = jnp.where(odd, export[rim:], export[:rim])
    near_ref[...] = jnp.where(odd, export[:rim], export[rim:])


def own_kernel(
    connect_ref, coef_ref, modes_ref, pseudo_ref, total_ref, stress_ref, high_ref, low_ref, own_ref
):
    depth = pseudo_ref.shape[0]
    rows = modes_ref.shape[0]
    elems = connect_ref.shape[1]
    rim = high_ref.shape[0] // 2
    odd = lax.axis_index(AXES) % 2

    def matrix(start, tall):
        node = lax.broadcasted_iota(jnp.int32, (tall, elems), 0) + start
        total = jnp.zeros((tall, elems), F32)
        for corner in range(connect_ref.shape[0]):
            hit = node == connect_ref[corner : corner + 1, :]
            total = total + jnp.where(hit, coef_ref[corner : corner + 1, :], 0.0)
        high = total.astype(BF16)
        return high, (total - high.astype(F32)).astype(BF16)

    after = rim + rows
    for place, start in ((0, after * odd), (1, after * (1 - odd))):
        here = slice(place * rim, (place + 1) * rim)
        high_ref[here, :], low_ref[here, :] = matrix(start, rim)
    for start in range(0, rows, rim):
        here = slice(start, start + rim)
        own_ref[0, here, :], own_ref[1, here, :] = matrix(start + rim, rim)
    other = pl.ds(pl.multiple_of((1 - odd) * depth, depth), depth)
    total = total_ref[...] + jnp.dot(
        modes_ref[:, other], pseudo_ref[...], preferred_element_type=F32
    )
    table = total.T.astype(BF16)
    stress = jnp.dot(table, own_ref[0], preferred_element_type=F32)
    stress_ref[...] = stress + jnp.dot(table, own_ref[1], preferred_element_type=F32)


def power_kernel(stress_ref, far_ref, near_ref, high_ref, low_ref, power_ref):
    rows = jnp.concatenate([far_ref[...], near_ref[...]], axis=0)
    stress = stress_ref[...]
    for part in (high_ref, low_ref):
        stress = stress + lax.dot_general(
            rows, part[...], (((0,), (0,)), ((), ())), preferred_element_type=F32
        )
    squares = stress * stress
    lines = power_ref.shape[0]
    columns = squares.shape[0] // lines
    for line in range(lines):
        power_ref[line : line + 1, :] = (
            jnp.sum(squares[line * columns : (line + 1) * columns], axis=0, keepdims=True)
            / columns
        )


def call(kernel, name, out, *operands, flops, scratch=()):
    shapes = [jax.ShapeDtypeStruct(shape, dtype) for shape, dtype in out]
    moved = sum(x.size * x.dtype.itemsize for x in operands)
    moved += sum(math.prod(shape) * jnp.dtype(dtype).itemsize for shape, dtype in out)
    result = pl.pallas_call(
        kernel,
        out_shape=shapes,
        in_specs=[whole()] * len(operands),
        out_specs=[whole()] * len(out),
        scratch_shapes=scratch,
        compiler_params=pltpu.CompilerParams(vmem_limit_bytes=VMEM_BYTES),
        cost_estimate=pl.CostEstimate(flops=flops, bytes_accessed=moved, transcendentals=0),
        name=name,
    )(*operands)
    return result if len(out) > 1 else result[0]


def pseudo_by_sum(input_rows, input_factor, mode_freq, mode_damping, line_freq):
    lines = line_freq.shape[0]
    columns = input_factor.shape[1] // lines
    half = columns // 2
    forced = lax.psum(
        lax.dot_general(
            input_rows, input_factor, (((0,), (0,)), ((), ())), preferred_element_type=F32
        ),
        AXES,
    )
    pieces = []
    for line in range(lines):
        gain_real, gain_imag = modal_gain(mode_freq, mode_damping, line_freq[line])
        gain_real, gain_imag = gain_real[:, None], gain_imag[:, None]
        real = forced[:, line * columns : line * columns + half]
        imag = forced[:, line * columns + half : (line + 1) * columns]
        pieces.append(gain_real * real - gain_imag * imag)
        pieces.append(gain_real * imag + gain_imag * real)
    return jnp.concatenate(pieces, axis=1).astype(BF16)


def own_pseudo(input_rows, input_factor, mode_freq, mode_damping, line_freq, copies):
    devices = math.prod(FAST_SHAPE)
    rows, modes = input_rows.shape
    width = input_factor.shape[1]
    lines = line_freq.shape[0]
    parts = modes // (devices // 2 * width)
    ones = call(ones_kernel, "ones", [((8, width), F32)], flops=LONG)
    sent, gains = call(
        pack_kernel,
        "pack",
        [((devices, (parts + 1) * rows, width), BF16), ((parts * 2 * lines, width), F32)],
        ones,
        line_freq.reshape(1, lines),
        mode_freq.reshape(-1, width),
        mode_damping.reshape(-1, width),
        input_rows,
        input_factor,
        flops=0,
    )
    got = lax.all_to_all(sent, AXES, 0, 0)
    return call(
        functools.partial(pseudo_kernel, rows=rows, lines=lines),
        "pseudo",
        [((copies, parts * width, width), BF16)],
        gains,
        got,
        flops=LONG,
    )


def local(
    shape,
    mode_rows,
    input_rows,
    input_factor,
    mode_freq,
    mode_damping,
    line_freq,
    boundary_rows,
    connectivity,
    stress_coef,
):
    devices = math.prod(shape)
    rows, modes = mode_rows.shape
    width = input_factor.shape[1]
    lines = line_freq.shape[0]
    exports = boundary_rows.shape[0]
    rim = exports // 2
    elems = connectivity.shape[1]
    inputs = (input_rows, input_factor, mode_freq, mode_damping, line_freq)
    if shape == FAST_SHAPE and modes == devices * LANES and input_rows.shape[0] % 16 == 0:
        groups = [[h * 16 + j * 2 + c for j in range(8)] for h in range(2) for c in range(2)]
        got = lax.all_to_all(own_pseudo(*inputs, copies=8), AXES, 0, 0, axis_index_groups=groups)
        mine = got.reshape(modes // 2, width)
        theirs = lax.ppermute(mine, AXES, [(i, i ^ 1) for i in range(devices)])
    else:
        pseudo = pseudo_by_sum(*inputs).reshape(2, modes // 2, width)
        core = lax.axis_index(AXES) % 2
        mine = lax.dynamic_index_in_dim(pseudo, core, 0, keepdims=False)
        theirs = lax.dynamic_index_in_dim(pseudo, 1 - core, 0, keepdims=False)
    total, part, picked = call(
        first_kernel,
        "first",
        [((rows, width), F32), ((exports, width), F32), ((exports, modes // 2), BF16)],
        boundary_rows.reshape(1, exports),
        mode_rows,
        mine,
        flops=rows * modes * (width + exports),
    )
    far, near = call(
        export_kernel,
        "export",
        [((rim, width), BF16)] * 2,
        part,
        picked,
        theirs,
        flops=exports * modes * width,
    )
    inner = [(i, i ^ 1) for i in range(devices)]
    outer = [(i, i + 1) for i in range(1, devices - 1, 2)]
    outer += [(j, i) for i, j in outer]
    near = lax.ppermute(near, AXES, inner)
    far = lax.ppermute(far, AXES, outer)
    stress, high, low = call(
        own_kernel,
        "own",
        [((width, elems), F32)] + [((exports, elems), BF16)] * 2,
        connectivity,
        stress_coef,
        mode_rows,
        theirs,
        total,
        flops=rows * modes * width + 4 * rows * elems * width,
        scratch=[pltpu.VMEM((2, rows, elems), BF16)],
    )
    return call(
        power_kernel,
        "power",
        [((lines, elems), F32)],
        stress,
        far,
        near,
        high,
        low,
        flops=4 * exports * elems * width,
    )


def solution(mesh):
    shape = tuple(mesh.shape[axis] for axis in AXES)
    placed = (
        P(AXES, None),
        P(AXES, None),
        P(AXES, None),
        P(),
        P(),
        P(),
        P(AXES),
        P(None, AXES),
        P(None, AXES),
    )
    return jax.shard_map(
        functools.partial(local, shape),
        mesh=mesh,
        in_specs=placed,
        out_specs=P(None, AXES),
        check_vma=False,
    )
```

profile of v0, /device:TPU:8, one launch (start us, length us, event | category | flops | bytes accessed | tf_op | source)
XLA Modules:
  0.0 41.9 jit_solution(15399676680265734524)
XLA Ops:
  0.0 0.0 copy-start.7
  0.0 0.0 copy-start.3
  0.0 0.0 copy-start.2
  0.0 0.0 copy-start.6
  0.0 0.0 copy-start.1
  0.0 0.6 %copy-done.7 = f32[2]{0:T(128)S(1)} copy-done((f32[2]{0:T(128)S(1)}, f32[2]{0:T(128)}, u32[]{:S(2)}) %copy-start.7) | copy-done | bytes 32
  0.7 0.1 copy-done.3
  0.7 0.0 copy-done.2
  0.8 0.0 copy-done.6
  0.8 0.2 copy-done.1
  1.0 0.1 pack.1
  1.1 18.3 %all_to_all.10.got_ref = bf16[32,48,128]{2,1,0:T(8,128)(2,1)S(1)} all-to-all(bf16[32,48,128]{2,1,0:T(8,128)(2,1)S(1)} %get-tuple-element.16), channel_id=1, replica_groups=mesh['region'=8,'sub'=4] {'region','sub'}, dimensions={0} | all-to-all | bytes 786432 | tf_op jit(solution)/shard_map/all_to_all | solution.py:224
  19.3 0.0 copy-start
  19.3 0.0 copy-start.8
  19.3 0.4 pseudo.1
  19.7 0.0 copy-start.4
  19.7 0.0 copy-start.5
  19.7 11.9 %all_to_all.11 = bf16[8,256,128]{2,1,0:T(8,128)(2,1)S(1)} all-to-all(bf16[8,256,128]{2,1,0:T(8,128)(2,1)S(1)} %pseudo.1), channel_id=1, replica_groups={{0,2,4,6,8,10,12,14},{1,3,5,7,9,11,13,15},{16,18,20,22,24,26,28,30},{17..., dimensions={0} | all-to-all | bytes 1048576 | tf_op jit(solution)/shard_map/all_to_all | solution.py:257
  31.7 0.0 collective-permute-start
  31.7 0.0 copy-done
  31.7 0.0 copy-done.8
  31.7 2.2 %first.1 = (f32[512,128]{1,0:T(8,128)S(1)}, f32[128,128]{1,0:T(8,128)S(1)}, bf16[128,2048]{1,0:T(8,128)(2,1)S(1)}) custom-call(s32[1,128]{1,0:T(1,128)S(1)} %bitcast.10, bf16[512,4096]{1,0:T(8,128)(2,1)S(1)} %copy-done, bf16[2048,128]{1,0:T(8,128)(2,1)S(1)} %bitcast.6), custom_call_target="tpu_custom_call" | custom-call | flops 536870912 | bytes 5571072 | tf_op jit(solution)/shard_map/first/pallas_call | solution.py:171
  33.8 0.0 collective-permute-done.pseudo_ref
  33.8 0.3 export.1
  34.1 3.5 %collective-permute-start.1 = (bf16[64,128]{1,0:T(8,128)(2,1)S(1)}, bf16[64,128]{1,0:T(8,128)(2,1)S(1)}, u32[]{:S(2)}, u32[]{:S(2)}) collective-permute-start(bf16[64,128]{1,0:T(8,128)(2,1)S(1)} %get-tuple-element.21), channel_id=1, source_target_pairs={{1,2},{3,4},{5,6},{7,8},{9,10},{11,12},{13,14},{15,16},{17,18},{19... | collective-permute-start | bytes 49160 | tf_op jit(solution)/shard_map/ppermute | solution.py:287
  37.6 0.1 collective-permute-start.2
  37.7 0.0 copy-done.4
  37.7 0.0 copy-done.5
  37.7 1.5 %own.1 = (f32[128,512]{1,0:T(8,128)S(1)}, bf16[128,512]{1,0:T(8,128)(2,1)S(1)}, bf16[128,512]{1,0:T(8,128)(2,1)S(1)}) custom-call(s32[4,512]{1,0:T(4,128)S(1)} %copy-done.4, f32[4,512]{1,0:T(4,128)S(1)} %copy-done.5, bf16[512,4096]{1,0:T(8,128)(2,1)S(1)} %copy-done, bf16[2048,128]{1,0:T(8,128)(2,1)S(1)} %collective-permute-done.pseudo_ref, ...), custom_call_target="tpu_custom_call" | custom-call | flops 402653184 | bytes 5521408 | tf_op jit(solution)/shard_map/own/pallas_call | solution.py:171
  39.2 1.8 %collective-permute-done.1.far_ref = bf16[64,128]{1,0:T(8,128)(2,1)S(1)} collective-permute-done((bf16[64,128]{1,0:T(8,128)(2,1)S(1)}, bf16[64,128]{1,0:T(8,128)(2,1)S(1)}, u32[]{:S(2)}, u32[]{:S(2)}) %collective-permute-start.1) | collective-permute-done | bytes 16416 | tf_op jit(solution)/shard_map/ppermute | solution.py:287
  41.0 0.0 collective-permute-done.2.near_ref
  41.0 0.9 %power.1 = f32[2,512]{1,0:T(2,128)} custom-call(f32[128,512]{1,0:T(8,128)S(1)} %get-tuple-element.18.stress_ref, bf16[64,128]{1,0:T(8,128)(2,1)S(1)} %collective-permute-done.1.far_ref, bf16[64,128]{1,0:T(8,128)(2,1)S(1)} %collective-permute-done.2.near_ref, bf16[128,512]{1,0:T(8,128)(2,1)S(1)} %get-tuple-element.23.high_ref, ...), custom_call_target="tpu_custom_call" | custom-call | flops 33554432 | bytes 561152 | tf_op jit(solution)/shard_map/power/pallas_call | solution.py:171
  (1 shorter events, 0.0 us)
Async XLA Ops:
  0.0 0.7 %copy-start.7 = (f32[2]{0:T(128)S(1)}, f32[2]{0:T(128)}, u32[]{:S(2)}) copy-start(f32[2]{0:T(128)} %param.14) | copy-start | bytes 28
  0.0 0.7 %copy-start.3 = (f32[4096]{0:T(1024)S(1)}, f32[4096]{0:T(1024)}, u32[]{:S(2)}) copy-start(f32[4096]{0:T(1024)} %param.13) | copy-start | bytes 49156
  0.0 0.7 %copy-start.2 = (f32[4096]{0:T(1024)S(1)}, f32[4096]{0:T(1024)}, u32[]{:S(2)}) copy-start(f32[4096]{0:T(1024)} %param.12) | copy-start | bytes 49156
  0.0 0.7 %copy-start.6 = (bf16[16,128]{1,0:T(8,128)(2,1)S(1)}, bf16[16,128]{1,0:T(8,128)(2,1)}, u32[]{:S(2)}) copy-start(bf16[16,128]{1,0:T(8,128)(2,1)} %factor_ref.1) | copy-start | bytes 12292
  0.0 1.0 %copy-start.1 = (bf16[16,4096]{1,0:T(8,128)(2,1)S(1)}, bf16[16,4096]{1,0:T(8,128)(2,1)}, u32[]{:S(2)}) copy-start(bf16[16,4096]{1,0:T(8,128)(2,1)} %rows_ref.1) | copy-start | bytes 393220
  19.3 12.3 %copy-start = (bf16[512,4096]{1,0:T(8,128)(2,1)S(1)}, bf16[512,4096]{1,0:T(8,128)(2,1)}, u32[]{:S(2)}) copy-start(bf16[512,4096]{1,0:T(8,128)(2,1)} %modes_ref.3) | copy-start | bytes 12582916
  19.3 12.3 %copy-start.8 = (s32[128]{0:T(128)S(1)}, s32[128]{0:T(128)}, u32[]{:S(2)}) copy-start(s32[128]{0:T(128)} %param.15) | copy-start | bytes 1540
  19.7 18.0 %copy-start.4 = (s32[4,512]{1,0:T(4,128)S(1)}, s32[4,512]{1,0:T(4,128)}, u32[]{:S(2)}) copy-start(s32[4,512]{1,0:T(4,128)} %connect_ref.1) | copy-start | bytes 24580
  19.7 18.0 %copy-start.5 = (f32[4,512]{1,0:T(4,128)S(1)}, f32[4,512]{1,0:T(4,128)}, u32[]{:S(2)}) copy-start(f32[4,512]{1,0:T(4,128)} %coef_ref.1) | copy-start | bytes 24580
  31.7 2.2 %collective-permute-start = (bf16[2048,128]{1,0:T(8,128)(2,1)S(1)}, bf16[2048,128]{1,0:T(8,128)(2,1)S(1)}, u32[]{:S(2)}, u32[]{:S(2)}) collective-permute-start(bf16[2048,128]{1,0:T(8,128)(2,1)S(1)} %bitcast.5), channel_id=1, source_target_pairs={{0,1},{1,0},{2,3},{3,2},{4,5},{5,4},{6,7},{7,6},{8,9},{9,8},{10,11... | collective-permute-start | bytes 1572872 | tf_op jit(solution)/shard_map/ppermute | solution.py:259
  34.1 6.9 %collective-permute-start.1 = (bf16[64,128]{1,0:T(8,128)(2,1)S(1)}, bf16[64,128]{1,0:T(8,128)(2,1)S(1)}, u32[]{:S(2)}, u32[]{:S(2)}) collective-permute-start(bf16[64,128]{1,0:T(8,128)(2,1)S(1)} %get-tuple-element.21), channel_id=1, source_target_pairs={{1,2},{3,4},{5,6},{7,8},{9,10},{11,12},{13,14},{15,16},{17,18},{19... | collective-permute-start | bytes 49160 | tf_op jit(solution)/shard_map/ppermute | solution.py:287
  37.6 3.4 %collective-permute-start.2 = (bf16[64,128]{1,0:T(8,128)(2,1)S(1)}, bf16[64,128]{1,0:T(8,128)(2,1)S(1)}, u32[]{:S(2)}, u32[]{:S(2)}) collective-permute-start(bf16[64,128]{1,0:T(8,128)(2,1)S(1)} %get-tuple-element.22), channel_id=1, source_target_pairs={{0,1},{1,0},{2,3},{3,2},{4,5},{5,4},{6,7},{7,6},{8,9},{9,8},{10,11... | collective-permute-start | bytes 49160 | tf_op jit(solution)/shard_map/ppermute | solution.py:286
where the time goes:
time: 42.4 us; the launch traced here: 41.9 us
  blocking collectives  30.2 us (71%)
  Pallas kernels  5.23 us (12%)
  starting transfers between devices  3.56 us (8%)
  waiting for transfers between devices  1.8 us (4%)
  local copies, waits for them, and re-layouts  0.96 us (2%)
    all_to_all x1, blocking collectives, own_pseudo(): got = lax.all_to_all(sent, AXES, 0, 0)  18.3 us
    all_to_all x1, blocking collectives, local(): lax.all_to_all(own_pseudo(*inputs, copies=8), AXES, 0, 0, axis_index_grou...  11.9 us
    pallas_call x7, Pallas kernels, call(): pl.pallas_call(kernel, out_shape=shapes, in_specs=[whole()] * len(operand...  5.23 us
    ppermute x1, starting transfers between devices, local(): far = lax.ppermute(far, AXES, outer)  3.49 us
    ppermute x1, waiting for transfers between devices, local(): far = lax.ppermute(far, AXES, outer)  1.79 us
    unnamed x18, local copies, waits for them, and re-layouts  0.96 us
  transfers between devices with their start and end apart: 3, of which 1 were waited for; matrix products, arithmetic and copies ran while one was open for 0% of the time, Pallas kernels for 9%

commit v1 on v0

--- a/solution.py
+++ b/solution.py
@@ -32,6 +32,11 @@
     return device % 2 * 8 + device // 2 % 8
 
 
+def exchange_order(devices):
+    planes = devices // 4
+    return [z * planes + plane for plane in range(planes) for z in (0, 2, 1, 3)]
+
+
 def ones_kernel(ones_ref):
     ones_ref[...] = jnp.ones_like(ones_ref)
 
@@ -42,11 +47,11 @@
     parts = sent_ref.shape[1] // rows - 1
     lines = line_ref.shape[1]
     factor = factor_ref[...]
-    for device in range(devices):
+    for place, device in enumerate(exchange_order(devices)):
         for part in range(parts):
             here = (slab_of(device) * parts + part) * width
-            sent_ref[device, part * rows : (part + 1) * rows, :] = rows_ref[:, here : here + width]
-        sent_ref[device, parts * rows :, :] = factor
+            sent_ref[place, part * rows : (part + 1) * rows, :] = rows_ref[:, here : here + width]
+        sent_ref[place, parts * rows :, :] = factor
     slab = slab_of(lax.axis_index(AXES))
     one = ones_ref[0:1, :]
     for part in range(parts):
@@ -92,13 +97,23 @@
     other = pl.ds(pl.multiple_of((1 - odd) * depth, depth), depth)
     total = jnp.dot(modes_ref[:, mine], pseudo_ref[...], preferred_element_type=F32)
     total_ref[...] = total
-    pick = lax.broadcasted_iota(jnp.int32, (rows, boundary_ref.shape[1]), 0) == boundary_ref[...]
-    pick = pick.astype(F32).T
-    part_ref[...] = jnp.dot(
-        pick, total, precision=lax.Precision.HIGHEST, preferred_element_type=F32
-    )
+    exports = boundary_ref.shape[1]
+    chosen = jnp.broadcast_to(boundary_ref[...], (exports, exports)).astype(F32).T
+    column = lax.broadcasted_iota(jnp.int32, (exports, exports), 1).astype(F32)
+    pick = jnp.concatenate(
+        [(column + start == chosen).astype(F32) for start in range(0, rows, exports)], axis=1
+    ).astype(BF16)
+    high = total.astype(BF16)
+    rest = total - high.astype(F32)
+    middle = rest.astype(BF16)
+    low = (rest - middle.astype(F32)).astype(BF16)
+    parts = jnp.dot(
+        pick, jnp.concatenate([high, middle, low], axis=1), preferred_element_type=F32
+    )
+    width = total.shape[1]
+    part_ref[...] = parts[:, :width] + parts[:, width : 2 * width] + parts[:, 2 * width :]
     picked_ref[...] = jnp.dot(
-        pick.astype(BF16), modes_ref[:, other], preferred_element_type=F32
+        pick, modes_ref[:, other], preferred_element_type=F32
     ).astype(BF16)
 
 
@@ -221,7 +236,7 @@
         input_factor,
         flops=0,
     )
-    got = lax.all_to_all(sent, AXES, 0, 0)
+    got = lax.all_to_all(sent, AXES, 0, 0, axis_index_groups=[exchange_order(devices)])
     return call(
         functools.partial(pseudo_kernel, rows=rows, lines=lines),
         "pseudo",

time: 42.4 us -> 42.2 us (level)
    all_to_all x1, blocking collectives: 11.9 us -> 13.3 us  [local(): lax.all_to_all(own_pseudo(*inputs, copies=8), AXES, 0, 0, axis_index_grou...]
    all_to_all x1, blocking collectives: 18.3 us -> 17.1 us  [own_pseudo(): lax.all_to_all(sent, AXES, 0, 0, axis_index_groups=[exchange_order(device...]
  transfers between devices with their start and end apart: 3 -> 3, of which waited for: 1 -> 2; matrix products, arithmetic and copies ran while one was open for 0% -> 0% of each run, Pallas kernels for 9% -> 8%
where the time goes in v1:
time: 42.2 us; the launch traced here: 41.7 us
  blocking collectives  30.3 us (72%)
  Pallas kernels  4.86 us (12%)
  starting transfers between devices  3.47 us (8%)
  waiting for transfers between devices  1.99 us (5%)
  local copies, waits for them, and re-layouts  0.96 us (2%)
    all_to_all x1, blocking collectives, own_pseudo(): lax.all_to_all(sent, AXES, 0, 0, axis_index_groups=[exchange_order(device...  17.1 us
    all_to_all x1, blocking collectives, local(): lax.all_to_all(own_pseudo(*inputs, copies=8), AXES, 0, 0, axis_index_grou...  13.3 us
    pallas_call x7, Pallas kernels, call(): pl.pallas_call(kernel, out_shape=shapes, in_specs=[whole()] * len(operand...  4.86 us
    ppermute x1, starting transfers between devices, local(): far = lax.ppermute(far, AXES, outer)  3.39 us
    ppermute x1, waiting for transfers between devices, local(): far = lax.ppermute(far, AXES, outer)  1.89 us
    unnamed x18, local copies, waits for them, and re-layouts  0.96 us
  transfers between devices with their start and end apart: 3, of which 2 were waited for; matrix products, arithmetic and copies ran while one was open for 0% of the time, Pallas kernels for 8%

profile of v1, /device:TPU:8, one launch (start us, length us, event | category | flops | bytes accessed | tf_op | source)
XLA Modules:
  0.0 41.7 jit_solution(4208702012171335509)
XLA Ops:
  0.0 0.0 copy-start.7
  0.0 0.0 copy-start.3
  0.0 0.0 copy-start.2
  0.0 0.0 copy-start.6
  0.0 0.0 copy-start.1
  0.0 0.6 %copy-done.7 = f32[2]{0:T(128)S(1)} copy-done((f32[2]{0:T(128)S(1)}, f32[2]{0:T(128)}, u32[]{:S(2)}) %copy-start.7) | copy-done | bytes 32
  0.7 0.1 copy-done.3
  0.7 0.0 copy-done.2
  0.8 0.0 copy-done.6
  0.8 0.2 copy-done.1
  1.0 0.1 pack.1
  1.1 17.1 %all_to_all.10.got_ref = bf16[32,48,128]{2,1,0:T(8,128)(2,1)S(1)} all-to-all(bf16[32,48,128]{2,1,0:T(8,128)(2,1)S(1)} %get-tuple-element.16), channel_id=1, replica_groups={{0,16,8,24,1,17,9,25,2,18,10,26,3,19,11,27,4,20,12,28,5,21,13,29,6,22,1..., dimensions={0} | all-to-all | bytes 786432 | tf_op jit(solution)/shard_map/all_to_all | solution.py:239
  18.1 0.0 copy-start
  18.1 0.0 copy-start.8
  18.1 0.4 pseudo.1
  18.5 0.0 copy-start.4
  18.5 0.0 copy-start.5
  18.5 13.3 %all_to_all.11 = bf16[8,256,128]{2,1,0:T(8,128)(2,1)S(1)} all-to-all(bf16[8,256,128]{2,1,0:T(8,128)(2,1)S(1)} %pseudo.1), channel_id=1, replica_groups={{0,2,4,6,8,10,12,14},{1,3,5,7,9,11,13,15},{16,18,20,22,24,26,28,30},{17..., dimensions={0} | all-to-all | bytes 1048576 | tf_op jit(solution)/shard_map/all_to_all | solution.py:272
  31.8 0.0 collective-permute-start
  31.8 0.0 copy-done
  31.8 0.0 copy-done.8
  31.8 1.8 %first.1 = (f32[512,128]{1,0:T(8,128)S(1)}, f32[128,128]{1,0:T(8,128)S(1)}, bf16[128,2048]{1,0:T(8,128)(2,1)S(1)}) custom-call(s32[1,128]{1,0:T(1,128)S(1)} %bitcast.10, bf16[512,4096]{1,0:T(8,128)(2,1)S(1)} %copy-done, bf16[2048,128]{1,0:T(8,128)(2,1)S(1)} %bitcast.6), custom_call_target="tpu_custom_call" | custom-call | flops 536870912 | bytes 5571072 | tf_op jit(solution)/shard_map/first/pallas_call | solution.py:186
  33.6 0.1 collective-permute-done.pseudo_ref
  33.7 0.3 export.1
  34.0 3.4 %collective-permute-start.1 = (bf16[64,128]{1,0:T(8,128)(2,1)S(1)}, bf16[64,128]{1,0:T(8,128)(2,1)S(1)}, u32[]{:S(2)}, u32[]{:S(2)}) collective-permute-start(bf16[64,128]{1,0:T(8,128)(2,1)S(1)} %get-tuple-element.21), channel_id=1, source_target_pairs={{1,2},{3,4},{5,6},{7,8},{9,10},{11,12},{13,14},{15,16},{17,18},{19... | collective-permute-start | bytes 49160 | tf_op jit(solution)/shard_map/ppermute | solution.py:302
  37.4 0.1 collective-permute-start.2
  37.5 0.0 copy-done.4
  37.5 0.0 copy-done.5
  37.5 1.5 %own.1 = (f32[128,512]{1,0:T(8,128)S(1)}, bf16[128,512]{1,0:T(8,128)(2,1)S(1)}, bf16[128,512]{1,0:T(8,128)(2,1)S(1)}) custom-call(s32[4,512]{1,0:T(4,128)S(1)} %copy-done.4, f32[4,512]{1,0:T(4,128)S(1)} %copy-done.5, bf16[512,4096]{1,0:T(8,128)(2,1)S(1)} %copy-done, bf16[2048,128]{1,0:T(8,128)(2,1)S(1)} %collective-permute-done.pseudo_ref, ...), custom_call_target="tpu_custom_call" | custom-call | flops 402653184 | bytes 5521408 | tf_op jit(solution)/shard_map/own/pallas_call | solution.py:186
  39.0 1.9 %collective-permute-done.1.far_ref = bf16[64,128]{1,0:T(8,128)(2,1)S(1)} collective-permute-done((bf16[64,128]{1,0:T(8,128)(2,1)S(1)}, bf16[64,128]{1,0:T(8,128)(2,1)S(1)}, u32[]{:S(2)}, u32[]{:S(2)}) %collective-permute-start.1) | collective-permute-done | bytes 16416 | tf_op jit(solution)/shard_map/ppermute | solution.py:302
  40.9 0.0 collective-permute-done.2.near_ref
  40.9 0.9 %power.1 = f32[2,512]{1,0:T(2,128)} custom-call(f32[128,512]{1,0:T(8,128)S(1)} %get-tuple-element.18.stress_ref, bf16[64,128]{1,0:T(8,128)(2,1)S(1)} %collective-permute-done.1.far_ref, bf16[64,128]{1,0:T(8,128)(2,1)S(1)} %collective-permute-done.2.near_ref, bf16[128,512]{1,0:T(8,128)(2,1)S(1)} %get-tuple-element.23.high_ref, ...), custom_call_target="tpu_custom_call" | custom-call | flops 33554432 | bytes 561152 | tf_op jit(solution)/shard_map/power/pallas_call | solution.py:186
  (1 shorter events, 0.0 us)
Async XLA Ops:
  0.0 0.7 %copy-start.7 = (f32[2]{0:T(128)S(1)}, f32[2]{0:T(128)}, u32[]{:S(2)}) copy-start(f32[2]{0:T(128)} %param.14) | copy-start | bytes 28
  0.0 0.7 %copy-start.3 = (f32[4096]{0:T(1024)S(1)}, f32[4096]{0:T(1024)}, u32[]{:S(2)}) copy-start(f32[4096]{0:T(1024)} %param.13) | copy-start | bytes 49156
  0.0 0.7 %copy-start.2 = (f32[4096]{0:T(1024)S(1)}, f32[4096]{0:T(1024)}, u32[]{:S(2)}) copy-start(f32[4096]{0:T(1024)} %param.12) | copy-start | bytes 49156
  0.0 0.7 %copy-start.6 = (bf16[16,128]{1,0:T(8,128)(2,1)S(1)}, bf16[16,128]{1,0:T(8,128)(2,1)}, u32[]{:S(2)}) copy-start(bf16[16,128]{1,0:T(8,128)(2,1)} %factor_ref.1) | copy-start | bytes 12292
  0.0 1.0 %copy-start.1 = (bf16[16,4096]{1,0:T(8,128)(2,1)S(1)}, bf16[16,4096]{1,0:T(8,128)(2,1)}, u32[]{:S(2)}) copy-start(bf16[16,4096]{1,0:T(8,128)(2,1)} %rows_ref.1) | copy-start | bytes 393220
  18.1 13.7 %copy-start = (bf16[512,4096]{1,0:T(8,128)(2,1)S(1)}, bf16[512,4096]{1,0:T(8,128)(2,1)}, u32[]{:S(2)}) copy-start(bf16[512,4096]{1,0:T(8,128)(2,1)} %modes_ref.3) | copy-start | bytes 12582916
  18.1 13.7 %copy-start.8 = (s32[128]{0:T(128)S(1)}, s32[128]{0:T(128)}, u32[]{:S(2)}) copy-start(s32[128]{0:T(128)} %param.15) | copy-start | bytes 1540
  18.5 19.0 %copy-start.4 = (s32[4,512]{1,0:T(4,128)S(1)}, s32[4,512]{1,0:T(4,128)}, u32[]{:S(2)}) copy-start(s32[4,512]{1,0:T(4,128)} %connect_ref.1) | copy-start | bytes 24580
  18.5 19.0 %copy-start.5 = (f32[4,512]{1,0:T(4,128)S(1)}, f32[4,512]{1,0:T(4,128)}, u32[]{:S(2)}) copy-start(f32[4,512]{1,0:T(4,128)} %coef_ref.1) | copy-start | bytes 24580
  31.8 1.9 %collective-permute-start = (bf16[2048,128]{1,0:T(8,128)(2,1)S(1)}, bf16[2048,128]{1,0:T(8,128)(2,1)S(1)}, u32[]{:S(2)}, u32[]{:S(2)}) collective-permute-start(bf16[2048,128]{1,0:T(8,128)(2,1)S(1)} %bitcast.5), channel_id=1, source_target_pairs={{0,1},{1,0},{2,3},{3,2},{4,5},{5,4},{6,7},{7,6},{8,9},{9,8},{10,11... | collective-permute-start | bytes 1572872 | tf_op jit(solution)/shard_map/ppermute | solution.py:274
  34.0 6.9 %collective-permute-start.1 = (bf16[64,128]{1,0:T(8,128)(2,1)S(1)}, bf16[64,128]{1,0:T(8,128)(2,1)S(1)}, u32[]{:S(2)}, u32[]{:S(2)}) collective-permute-start(bf16[64,128]{1,0:T(8,128)(2,1)S(1)} %get-tuple-element.21), channel_id=1, source_target_pairs={{1,2},{3,4},{5,6},{7,8},{9,10},{11,12},{13,14},{15,16},{17,18},{19... | collective-permute-start | bytes 49160 | tf_op jit(solution)/shard_map/ppermute | solution.py:302
  37.4 3.5 %collective-permute-start.2 = (bf16[64,128]{1,0:T(8,128)(2,1)S(1)}, bf16[64,128]{1,0:T(8,128)(2,1)S(1)}, u32[]{:S(2)}, u32[]{:S(2)}) collective-permute-start(bf16[64,128]{1,0:T(8,128)(2,1)S(1)} %get-tuple-element.22), channel_id=1, source_target_pairs={{0,1},{1,0},{2,3},{3,2},{4,5},{5,4},{6,7},{7,6},{8,9},{9,8},{10,11... | collective-permute-start | bytes 49160 | tf_op jit(solution)/shard_map/ppermute | solution.py:301

commit v2 on v1

--- a/solution.py
+++ b/solution.py
@@ -28,31 +28,26 @@
     return detune / magnitude, -damped / magnitude
 
 
-def slab_of(device):
-    return device % 2 * 8 + device // 2 % 8
-
-
-def exchange_order(devices):
-    planes = devices // 4
-    return [z * planes + plane for plane in range(planes) for z in (0, 2, 1, 3)]
-
-
 def ones_kernel(ones_ref):
     ones_ref[...] = jnp.ones_like(ones_ref)
 
 
 def pack_kernel(ones_ref, line_ref, freq_ref, damping_ref, rows_ref, factor_ref, sent_ref, gain_ref):
-    devices, _, width = sent_ref.shape
+    chips, tall, width = sent_ref.shape
     rows = rows_ref.shape[0]
-    parts = sent_ref.shape[1] // rows - 1
+    parts = (tall // rows - 1) // 2
+    slabs = rows_ref.shape[1] // (2 * parts * width)
     lines = line_ref.shape[1]
     factor = factor_ref[...]
-    for place, device in enumerate(exchange_order(devices)):
-        for part in range(parts):
-            here = (slab_of(device) * parts + part) * width
-            sent_ref[place, part * rows : (part + 1) * rows, :] = rows_ref[:, here : here + width]
-        sent_ref[place, parts * rows :, :] = factor
-    slab = slab_of(lax.axis_index(AXES))
+    for chip in range(chips):
+        for half in range(2):
+            for part in range(parts):
+                here = ((half * slabs + chip % slabs) * parts + part) * width
+                place = (half * parts + part) * rows
+                sent_ref[chip, place : place + rows, :] = rows_ref[:, here : here + width]
+        sent_ref[chip, 2 * parts * rows :, :] = factor
+    me = lax.axis_index(AXES)
+    slab = me % 2 * slabs + me // 2 % slabs
     one = ones_ref[0:1, :]
     for part in range(parts):
         here = pl.ds(slab * parts + part, 1)
@@ -64,17 +59,27 @@
             gain_ref[row + 1 : row + 2, :] = imag * one
 
 
-def pseudo_kernel(gain_ref, got_ref, pseudo_ref, *, rows, lines):
-    devices, tall, width = got_ref.shape
-    parts = tall // rows - 1
-    factor = got_ref[:, parts * rows :, :].reshape(devices * rows, width)
+def partial_kernel(got_ref, own_ref, other_ref):
+    chips, tall, width = got_ref.shape
+    parts = own_ref.shape[0]
+    rows = tall // (2 * parts + 1)
+    factor = got_ref[:, 2 * parts * rows :, :].reshape(chips * rows, width)
+    odd = lax.axis_index(AXES) % 2
+    for sums_ref, half in ((other_ref, 1 - odd), (own_ref, odd)):
+        for part in range(parts):
+            here = pl.ds(pl.multiple_of((half * parts + part) * rows, rows), rows)
+            shapes = got_ref[:, here, :].reshape(chips * rows, width)
+            sums_ref[part] = lax.dot_general(
+                factor, shapes, (((0,), (0,)), ((), ())), preferred_element_type=F32
+            )
+
+
+def pseudo_kernel(gain_ref, own_ref, other_ref, pseudo_ref, *, lines):
+    parts, width, _ = own_ref.shape
     columns = width // lines
     half = columns // 2
     for part in range(parts):
-        shapes = got_ref[:, part * rows : (part + 1) * rows, :].reshape(devices * rows, width)
-        forced = lax.dot_general(
-            factor, shapes, (((0,), (0,)), ((), ())), preferred_element_type=F32
-        )
+        forced = own_ref[part] + other_ref[part]
         pieces = []
         for line in range(lines):
             row = 2 * (part * lines + line)
@@ -129,12 +134,12 @@
 
 
 def own_kernel(
-    connect_ref, coef_ref, modes_ref, pseudo_ref, total_ref, stress_ref, high_ref, low_ref, own_ref
+    connect_ref, coef_ref, modes_ref, pseudo_ref, total_ref, stress_ref, rim_ref, own_ref
 ):
     depth = pseudo_ref.shape[0]
     rows = modes_ref.shape[0]
     elems = connect_ref.shape[1]
-    rim = high_ref.shape[0] // 2
+    rim = rim_ref.shape[0] // 4
     odd = lax.axis_index(AXES) % 2
 
     def matrix(start, tall):
@@ -148,8 +153,9 @@
 
     after = rim + rows
     for place, start in ((0, after * odd), (1, after * (1 - odd))):
-        here = slice(place * rim, (place + 1) * rim)
-        high_ref[here, :], low_ref[here, :] = matrix(start, rim)
+        high, low = matrix(start, rim)
+        rim_ref[place * rim : (place + 1) * rim, :] = high
+        rim_ref[(place + 2) * rim : (place + 3) * rim, :] = low
     for start in range(0, rows, rim):
         here = slice(start, start + rim)
         own_ref[0, here, :], own_ref[1, here, :] = matrix(start + rim, rim)
@@ -162,13 +168,14 @@
     stress_ref[...] = stress + jnp.dot(table, own_ref[1], preferred_element_type=F32)
 
 
-def power_kernel(stress_ref, far_ref, near_ref, high_ref, low_ref, power_ref):
-    rows = jnp.concatenate([far_ref[...], near_ref[...]], axis=0)
-    stress = stress_ref[...]
-    for part in (high_ref, low_ref):
-        stress = stress + lax.dot_general(
-            rows, part[...], (((0,), (0,)), ((), ())), preferred_element_type=F32
-        )
+def power_kernel(stress_ref, far_ref, near_ref, rim_ref, power_ref):
+    rows = [far_ref[...], near_ref[...]]
+    stress = stress_ref[...] + lax.dot_general(
+        jnp.concatenate(rows + rows, axis=0),
+        rim_ref[...],
+        (((0,), (0,)), ((), ())),
+        preferred_element_type=F32,
+    )
     squares = stress * stress
     lines = power_ref.shape[0]
     columns = squares.shape[0] // lines
@@ -219,15 +226,16 @@
 
 def own_pseudo(input_rows, input_factor, mode_freq, mode_damping, line_freq, copies):
     devices = math.prod(FAST_SHAPE)
+    chips = devices // 2
     rows, modes = input_rows.shape
     width = input_factor.shape[1]
     lines = line_freq.shape[0]
-    parts = modes // (devices // 2 * width)
+    parts = modes // (chips * width)
     ones = call(ones_kernel, "ones", [((8, width), F32)], flops=LONG)
     sent, gains = call(
         pack_kernel,
         "pack",
-        [((devices, (parts + 1) * rows, width), BF16), ((parts * 2 * lines, width), F32)],
+        [((chips, (2 * parts + 1) * rows, width), BF16), ((parts * 2 * lines, width), F32)],
         ones,
         line_freq.reshape(1, lines),
         mode_freq.reshape(-1, width),
@@ -236,13 +244,23 @@
         input_factor,
         flops=0,
     )
-    got = lax.all_to_all(sent, AXES, 0, 0, axis_index_groups=[exchange_order(devices)])
+    cores = [[2 * chip + core for chip in range(chips)] for core in range(2)]
+    got = lax.all_to_all(sent, AXES, 0, 0, axis_index_groups=cores)
+    own, other = call(
+        partial_kernel,
+        "partial",
+        [((parts, width, width), F32)] * 2,
+        got,
+        flops=LONG,
+    )
+    other = lax.ppermute(other, AXES, [(i, i ^ 1) for i in range(devices)])
     return call(
-        functools.partial(pseudo_kernel, rows=rows, lines=lines),
+        functools.partial(pseudo_kernel, lines=lines),
         "pseudo",
         [((copies, parts * width, width), BF16)],
         gains,
-        got,
+        own,
+        other,
         flops=LONG,
     )
 
@@ -300,10 +318,10 @@
     outer += [(j, i) for i, j in outer]
     near = lax.ppermute(near, AXES, inner)
     far = lax.ppermute(far, AXES, outer)
-    stress, high, low = call(
+    stress, matrix = call(
         own_kernel,
         "own",
-        [((width, elems), F32)] + [((exports, elems), BF16)] * 2,
+        [((width, elems), F32), ((2 * exports, elems), BF16)],
         connectivity,
         stress_coef,
         mode_rows,
@@ -319,8 +337,7 @@
         stress,
         far,
         near,
-        high,
-        low,
+        matrix,
         flops=4 * exports * elems * width,
     )
 

time: 42.2 us -> 43.3 us (1.026)
  waiting for transfers between devices: 1.99 us -> 3.32 us
    ppermute x0 -> x1, waiting for transfers between devices: none -> 1.33 us  [own_pseudo(): other = lax.ppermute(other, AXES, [(i, i ^ 1) for i in range(devices)])]
    all_to_all x1, blocking collectives: 13.3 us -> 12.6 us  [local(): lax.all_to_all(own_pseudo(*inputs, copies=8), AXES, 0, 0, axis_index_grou...]
    pallas_call x7 -> x8, Pallas kernels: 4.86 us -> 4.82 us  [call(): pl.pallas_call(kernel, out_shape=shapes, in_specs=[whole()] * len(operand...]
  transfers between devices with their start and end apart: 3 -> 4, of which waited for: 2 -> 3; matrix products, arithmetic and copies ran while one was open for 0% -> 0% of each run, Pallas kernels for 8% -> 8%
where the time goes in v2:
time: 43.3 us; the launch traced here: 42.8 us
  blocking collectives  30 us (69%)
  Pallas kernels  4.82 us (11%)
  starting transfers between devices  3.55 us (8%)
  waiting for transfers between devices  3.32 us (8%)
  local copies, waits for them, and re-layouts  0.96 us (2%)
    all_to_all x1, blocking collectives, own_pseudo(): got = lax.all_to_all(sent, AXES, 0, 0, axis_index_groups=cores)  17.4 us
    all_to_all x1, blocking collectives, local(): lax.all_to_all(own_pseudo(*inputs, copies=8), AXES, 0, 0, axis_index_grou...  12.6 us
    pallas_call x8, Pallas kernels, call(): pl.pallas_call(kernel, out_shape=shapes, in_specs=[whole()] * len(operand...  4.82 us
    ppermute x1, starting transfers between devices, local(): far = lax.ppermute(far, AXES, outer)  3.41 us
    ppermute x1, waiting for transfers between devices, local(): far = lax.ppermute(far, AXES, outer)  1.88 us
    ppermute x1, waiting for transfers between devices, own_pseudo(): other = lax.ppermute(other, AXES, [(i, i ^ 1) for i in range(devices)])  1.33 us
    unnamed x18, local copies, waits for them, and re-layouts  0.96 us
  transfers between devices with their start and end apart: 4, of which 3 were waited for; matrix products, arithmetic and copies ran while one was open for 0% of the time, Pallas kernels for 8%

profile of v2, /device:TPU:8, one launch (start us, length us, event | category | flops | bytes accessed | tf_op | source)
XLA Modules:
  0.0 42.8 jit_solution(15158853265259540915)
XLA Ops:
  0.0 0.0 copy-start.7
  0.0 0.0 copy-start.3
  0.0 0.0 copy-start.2
  0.0 0.0 copy-start.6
  0.0 0.0 copy-start.1
  0.0 0.6 %copy-done.7 = f32[2]{0:T(128)S(1)} copy-done((f32[2]{0:T(128)S(1)}, f32[2]{0:T(128)}, u32[]{:S(2)}) %copy-start.7) | copy-done | bytes 32
  0.7 0.1 copy-done.3
  0.7 0.0 copy-done.2
  0.8 0.0 copy-done.6
  0.8 0.2 copy-done.1
  1.0 0.1 pack.1
  1.1 17.4 %all_to_all.10.got_ref = bf16[16,80,128]{2,1,0:T(8,128)(2,1)S(1)} all-to-all(bf16[16,80,128]{2,1,0:T(8,128)(2,1)S(1)} %get-tuple-element.17), channel_id=1, replica_groups={{0,2,4,6,8,10,12,14,16,18,20,22,24,26,28,30},{1,3,5,7,9,11,13,15,17,19,..., dimensions={0} | all-to-all | bytes 655360 | tf_op jit(solution)/shard_map/all_to_all | solution.py:248
  18.5 0.2 partial.1
  18.7 0.1 collective-permute-start
  18.8 1.3 %collective-permute-done.other_ref = f32[2,128,128]{2,1,0:T(8,128)S(1)} collective-permute-done((f32[2,128,128]{2,1,0:T(8,128)S(1)}, f32[2,128,128]{2,1,0:T(8,128)S(1)}, u32[]{:S(2)}, u32[]{:S(2)}) %collective-permute-start) | collective-permute-done | bytes 131104 | tf_op jit(solution)/shard_map/ppermute | solution.py:256
  20.1 0.0 copy-start
  20.1 0.0 copy-start.8
  20.1 0.1 pseudo.1
  20.3 0.0 copy-start.4
  20.3 0.0 copy-start.5
  20.3 12.6 %all_to_all.11 = bf16[8,256,128]{2,1,0:T(8,128)(2,1)S(1)} all-to-all(bf16[8,256,128]{2,1,0:T(8,128)(2,1)S(1)} %pseudo.1), channel_id=1, replica_groups={{0,2,4,6,8,10,12,14},{1,3,5,7,9,11,13,15},{16,18,20,22,24,26,28,30},{17..., dimensions={0} | all-to-all | bytes 1048576 | tf_op jit(solution)/shard_map/all_to_all | solution.py:290
  32.9 0.0 collective-permute-start.1
  32.9 0.0 copy-done
  32.9 0.0 copy-done.8
  32.9 1.8 %first.1 = (f32[512,128]{1,0:T(8,128)S(1)}, f32[128,128]{1,0:T(8,128)S(1)}, bf16[128,2048]{1,0:T(8,128)(2,1)S(1)}) custom-call(s32[1,128]{1,0:T(1,128)S(1)} %bitcast.10, bf16[512,4096]{1,0:T(8,128)(2,1)S(1)} %copy-done, bf16[2048,128]{1,0:T(8,128)(2,1)S(1)} %bitcast.6), custom_call_target="tpu_custom_call" | custom-call | flops 536870912 | bytes 5571072 | tf_op jit(solution)/shard_map/first/pallas_call | solution.py:193
  34.7 0.1 collective-permute-done.1.pseudo_ref
  34.8 0.3 export.1
  35.1 3.4 %collective-permute-start.2 = (bf16[64,128]{1,0:T(8,128)(2,1)S(1)}, bf16[64,128]{1,0:T(8,128)(2,1)S(1)}, u32[]{:S(2)}, u32[]{:S(2)}) collective-permute-start(bf16[64,128]{1,0:T(8,128)(2,1)S(1)} %get-tuple-element.24), channel_id=1, source_target_pairs={{1,2},{3,4},{5,6},{7,8},{9,10},{11,12},{13,14},{15,16},{17,18},{19... | collective-permute-start | bytes 49160 | tf_op jit(solution)/shard_map/ppermute | solution.py:320
  38.5 0.1 collective-permute-start.3
  38.6 0.0 copy-done.4
  38.6 0.0 copy-done.5
  38.6 1.5 %own.1 = (f32[128,512]{1,0:T(8,128)S(1)}, bf16[256,512]{1,0:T(8,128)(2,1)S(1)}) custom-call(s32[4,512]{1,0:T(4,128)S(1)} %copy-done.4, f32[4,512]{1,0:T(4,128)S(1)} %copy-done.5, bf16[512,4096]{1,0:T(8,128)(2,1)S(1)} %copy-done, bf16[2048,128]{1,0:T(8,128)(2,1)S(1)} %collective-permute-done.1.pseudo_ref, f32[512,128]{1,0:T(8,128)S(1)} %get-tuple-element.20.total_ref), custom_call_target="tpu_custom_call" | custom-call | flops 402653184 | bytes 5521408 | tf_op jit(solution)/shard_map/own/pallas_call | solution.py:193
  40.1 1.9 %collective-permute-done.2.far_ref = bf16[64,128]{1,0:T(8,128)(2,1)S(1)} collective-permute-done((bf16[64,128]{1,0:T(8,128)(2,1)S(1)}, bf16[64,128]{1,0:T(8,128)(2,1)S(1)}, u32[]{:S(2)}, u32[]{:S(2)}) %collective-permute-start.2) | collective-permute-done | bytes 16416 | tf_op jit(solution)/shard_map/ppermute | solution.py:320
  42.0 0.0 collective-permute-done.3.near_ref
  42.0 0.8 %power.1 = f32[2,512]{1,0:T(2,128)} custom-call(f32[128,512]{1,0:T(8,128)S(1)} %get-tuple-element.21.stress_ref, bf16[64,128]{1,0:T(8,128)(2,1)S(1)} %collective-permute-done.2.far_ref, bf16[64,128]{1,0:T(8,128)(2,1)S(1)} %collective-permute-done.3.near_ref, bf16[256,512]{1,0:T(8,128)(2,1)S(1)} %get-tuple-element.26.rim_ref), custom_call_target="tpu_custom_call" | custom-call | flops 33554432 | bytes 561152 | tf_op jit(solution)/shard_map/power/pallas_call | solution.py:193
  (1 shorter events, 0.0 us)
Async XLA Ops:
  0.0 0.7 %copy-start.7 = (f32[2]{0:T(128)S(1)}, f32[2]{0:T(128)}, u32[]{:S(2)}) copy-start(f32[2]{0:T(128)} %param.14) | copy-start | bytes 28
  0.0 0.7 %copy-start.3 = (f32[4096]{0:T(1024)S(1)}, f32[4096]{0:T(1024)}, u32[]{:S(2)}) copy-start(f32[4096]{0:T(1024)} %param.13) | copy-start | bytes 49156
  0.0 0.7 %copy-start.2 = (f32[4096]{0:T(1024)S(1)}, f32[4096]{0:T(1024)}, u32[]{:S(2)}) copy-start(f32[4096]{0:T(1024)} %param.12) | copy-start | bytes 49156
  0.0 0.7 %copy-start.6 = (bf16[16,128]{1,0:T(8,128)(2,1)S(1)}, bf16[16,128]{1,0:T(8,128)(2,1)}, u32[]{:S(2)}) copy-start(bf16[16,128]{1,0:T(8,128)(2,1)} %factor_ref.1) | copy-start | bytes 12292
  0.0 1.0 %copy-start.1 = (bf16[16,4096]{1,0:T(8,128)(2,1)S(1)}, bf16[16,4096]{1,0:T(8,128)(2,1)}, u32[]{:S(2)}) copy-start(bf16[16,4096]{1,0:T(8,128)(2,1)} %rows_ref.1) | copy-start | bytes 393220
  18.7 1.4 %collective-permute-start = (f32[2,128,128]{2,1,0:T(8,128)S(1)}, f32[2,128,128]{2,1,0:T(8,128)S(1)}, u32[]{:S(2)}, u32[]{:S(2)}) collective-permute-start(f32[2,128,128]{2,1,0:T(8,128)S(1)} %get-tuple-element.19), channel_id=1, source_target_pairs={{0,1},{1,0},{2,3},{3,2},{4,5},{5,4},{6,7},{7,6},{8,9},{9,8},{10,11... | collective-permute-start | bytes 393224 | tf_op jit(solution)/shard_map/ppermute | solution.py:256
  20.1 12.8 %copy-start = (bf16[512,4096]{1,0:T(8,128)(2,1)S(1)}, bf16[512,4096]{1,0:T(8,128)(2,1)}, u32[]{:S(2)}) copy-start(bf16[512,4096]{1,0:T(8,128)(2,1)} %modes_ref.3) | copy-start | bytes 12582916
  20.1 12.8 %copy-start.8 = (s32[128]{0:T(128)S(1)}, s32[128]{0:T(128)}, u32[]{:S(2)}) copy-start(s32[128]{0:T(128)} %param.15) | copy-start | bytes 1540
  20.3 18.3 %copy-start.4 = (s32[4,512]{1,0:T(4,128)S(1)}, s32[4,512]{1,0:T(4,128)}, u32[]{:S(2)}) copy-start(s32[4,512]{1,0:T(4,128)} %connect_ref.1) | copy-start | bytes 24580
  20.3 18.3 %copy-start.5 = (f32[4,512]{1,0:T(4,128)S(1)}, f32[4,512]{1,0:T(4,128)}, u32[]{:S(2)}) copy-start(f32[4,512]{1,0:T(4,128)} %coef_ref.1) | copy-start | bytes 24580
  32.9 1.9 %collective-permute-start.1 = (bf16[2048,128]{1,0:T(8,128)(2,1)S(1)}, bf16[2048,128]{1,0:T(8,128)(2,1)S(1)}, u32[]{:S(2)}, u32[]{:S(2)}) collective-permute-start(bf16[2048,128]{1,0:T(8,128)(2,1)S(1)} %bitcast.5), channel_id=1, source_target_pairs={{0,1},{1,0},{2,3},{3,2},{4,5},{5,4},{6,7},{7,6},{8,9},{9,8},{10,11... | collective-permute-start | bytes 1572872 | tf_op jit(solution)/shard_map/ppermute | solution.py:292
  35.1 6.9 %collective-permute-start.2 = (bf16[64,128]{1,0:T(8,128)(2,1)S(1)}, bf16[64,128]{1,0:T(8,128)(2,1)S(1)}, u32[]{:S(2)}, u32[]{:S(2)}) collective-permute-start(bf16[64,128]{1,0:T(8,128)(2,1)S(1)} %get-tuple-element.24), channel_id=1, source_target_pairs={{1,2},{3,4},{5,6},{7,8},{9,10},{11,12},{13,14},{15,16},{17,18},{19... | collective-permute-start | bytes 49160 | tf_op jit(solution)/shard_map/ppermute | solution.py:320
  38.5 3.4 %collective-permute-start.3 = (bf16[64,128]{1,0:T(8,128)(2,1)S(1)}, bf16[64,128]{1,0:T(8,128)(2,1)S(1)}, u32[]{:S(2)}, u32[]{:S(2)}) collective-permute-start(bf16[64,128]{1,0:T(8,128)(2,1)S(1)} %get-tuple-element.25), channel_id=1, source_target_pairs={{0,1},{1,0},{2,3},{3,2},{4,5},{5,4},{6,7},{7,6},{8,9},{9,8},{10,11... | collective-permute-start | bytes 49160 | tf_op jit(solution)/shard_map/ppermute | solution.py:319

commit v3 on v1

--- a/solution.py
+++ b/solution.py
@@ -32,56 +32,50 @@
     return device % 2 * 8 + device // 2 % 8
 
 
-def exchange_order(devices):
-    planes = devices // 4
-    return [z * planes + plane for plane in range(planes) for z in (0, 2, 1, 3)]
-
-
 def ones_kernel(ones_ref):
     ones_ref[...] = jnp.ones_like(ones_ref)
 
 
-def pack_kernel(ones_ref, line_ref, freq_ref, damping_ref, rows_ref, factor_ref, sent_ref, gain_ref):
+def pack_kernel(ones_ref, rows_ref, factor_ref, sent_ref):
     devices, _, width = sent_ref.shape
     rows = rows_ref.shape[0]
     parts = sent_ref.shape[1] // rows - 1
-    lines = line_ref.shape[1]
-    factor = factor_ref[...]
-    for place, device in enumerate(exchange_order(devices)):
+    factor = factor_ref[...] * ones_ref[0:1, :].astype(BF16)
+    for device in range(devices):
         for part in range(parts):
             here = (slab_of(device) * parts + part) * width
-            sent_ref[place, part * rows : (part + 1) * rows, :] = rows_ref[:, here : here + width]
-        sent_ref[place, parts * rows :, :] = factor
+            sent_ref[device, part * rows : (part + 1) * rows, :] = rows_ref[:, here : here + width]
+        sent_ref[device, parts * rows :, :] = factor
+
+
+def pseudo_kernel(line_ref, freq_ref, damping_ref, got_ref, pseudo_ref, *, rows):
+    devices, tall, width = got_ref.shape
+    parts = tall // rows - 1
+    lines = line_ref.shape[1]
+    columns = width // lines
+    half = columns // 2
     slab = slab_of(lax.axis_index(AXES))
-    one = ones_ref[0:1, :]
+    factor = got_ref[:, parts * rows :, :].reshape(devices * rows, width)
+    shapes = [
+        got_ref[:, part * rows : (part + 1) * rows, :].reshape(devices * rows, width)
+        for part in range(parts)
+    ]
+    forced = lax.dot_general(
+        factor,
+        jnp.concatenate(shapes, axis=1),
+        (((0,), (0,)), ((), ())),
+        preferred_element_type=F32,
+    )
     for part in range(parts):
         here = pl.ds(slab * parts + part, 1)
-        for line in range(lines):
-            omega = line_ref[:, line : line + 1]
-            real, imag = modal_gain(freq_ref[here, :], damping_ref[here, :], omega)
-            row = 2 * (part * lines + line)
-            gain_ref[row : row + 1, :] = real * one
-            gain_ref[row + 1 : row + 2, :] = imag * one
-
-
-def pseudo_kernel(gain_ref, got_ref, pseudo_ref, *, rows, lines):
-    devices, tall, width = got_ref.shape
-    parts = tall // rows - 1
-    factor = got_ref[:, parts * rows :, :].reshape(devices * rows, width)
-    columns = width // lines
-    half = columns // 2
-    for part in range(parts):
-        shapes = got_ref[:, part * rows : (part + 1) * rows, :].reshape(devices * rows, width)
-        forced = lax.dot_general(
-            factor, shapes, (((0,), (0,)), ((), ())), preferred_element_type=F32
-        )
+        summed = forced[:, part * width : (part + 1) * width]
         pieces = []
         for line in range(lines):
-            row = 2 * (part * lines + line)
-            gain_real = gain_ref[row : row + 1, :]
-            gain_imag = gain_ref[row + 1 : row + 2, :]
-            real = forced[line * columns : line * columns + half]
-            imag = forced[line * columns + half : (line + 1) * columns]
+            gain_real, gain_imag = modal_gain(
+                freq_ref[here, :], damping_ref[here, :], line_ref[:, line : line + 1]
+            )
+            real = summed[line * columns : line * columns + half]
+            imag = summed[line * columns + half : (line + 1) * columns]
             pieces.append(gain_real * real - gain_imag * imag)
             pieces.append(gain_real * imag + gain_imag * real)
         pseudo = jnp.concatenate(pieces, axis=0).T.astype(BF16)
@@ -129,12 +123,12 @@
 
 
 def own_kernel(
-    connect_ref, coef_ref, modes_ref, pseudo_ref, total_ref, stress_ref, high_ref, low_ref, own_ref
+    connect_ref, coef_ref, modes_ref, pseudo_ref, total_ref, stress_ref, rim_ref, own_ref
 ):
     depth = pseudo_ref.shape[0]
     rows = modes_ref.shape[0]
     elems = connect_ref.shape[1]
-    rim = high_ref.shape[0] // 2
+    rim = rim_ref.shape[0] // 4
     odd = lax.axis_index(AXES) % 2
 
     def matrix(start, tall):
@@ -148,8 +142,9 @@
 
     after = rim + rows
     for place, start in ((0, after * odd), (1, after * (1 - odd))):
-        here = slice(place * rim, (place + 1) * rim)
-        high_ref[here, :], low_ref[here, :] = matrix(start, rim)
+        high, low = matrix(start, rim)
+        rim_ref[place * rim : (place + 1) * rim, :] = high
+        rim_ref[(place + 2) * rim : (place + 3) * rim, :] = low
     for start in range(0, rows, rim):
         here = slice(start, start + rim)
         own_ref[0, here, :], own_ref[1, here, :] = matrix(start + rim, rim)
@@ -162,13 +157,14 @@
     stress_ref[...] = stress + jnp.dot(table, own_ref[1], preferred_element_type=F32)
 
 
-def power_kernel(stress_ref, far_ref, near_ref, high_ref, low_ref, power_ref):
-    rows = jnp.concatenate([far_ref[...], near_ref[...]], axis=0)
-    stress = stress_ref[...]
-    for part in (high_ref, low_ref):
-        stress = stress + lax.dot_general(
-            rows, part[...], (((0,), (0,)), ((), ())), preferred_element_type=F32
-        )
+def power_kernel(stress_ref, far_ref, near_ref, rim_ref, power_ref):
+    rows = [far_ref[...], near_ref[...]]
+    stress = stress_ref[...] + lax.dot_general(
+        jnp.concatenate(rows + rows, axis=0),
+        rim_ref[...],
+        (((0,), (0,)), ((), ())),
+        preferred_element_type=F32,
+    )
     squares = stress * stress
     lines = power_ref.shape[0]
     columns = squares.shape[0] // lines
@@ -224,24 +220,23 @@
     lines = line_freq.shape[0]
     parts = modes // (devices // 2 * width)
     ones = call(ones_kernel, "ones", [((8, width), F32)], flops=LONG)
-    sent, gains = call(
+    sent = call(
         pack_kernel,
         "pack",
-        [((devices, (parts + 1) * rows, width), BF16), ((parts * 2 * lines, width), F32)],
+        [((devices, (parts + 1) * rows, width), BF16)],
         ones,
+        input_rows,
+        input_factor,
+        flops=LONG,
+    )
+    got = lax.all_to_all(sent, AXES, 0, 0)
+    return call(
+        functools.partial(pseudo_kernel, rows=rows),
+        "pseudo",
+        [((copies, parts * width, width), BF16)],
         line_freq.reshape(1, lines),
         mode_freq.reshape(-1, width),
         mode_damping.reshape(-1, width),
-        input_rows,
-        input_factor,
-        flops=0,
-    )
-    got = lax.all_to_all(sent, AXES, 0, 0, axis_index_groups=[exchange_order(devices)])
-    return call(
-        functools.partial(pseudo_kernel, rows=rows, lines=lines),
-        "pseudo",
-        [((copies, parts * width, width), BF16)],
-        gains,
         got,
         flops=LONG,
     )
@@ -300,10 +295,10 @@
     outer += [(j, i) for i, j in outer]
     near = lax.ppermute(near, AXES, inner)
     far = lax.ppermute(far, AXES, outer)
-    stress, high, low = call(
+    stress, matrix = call(
         own_kernel,
         "own",
-        [((width, elems), F32)] + [((exports, elems), BF16)] * 2,
+        [((width, elems), F32), ((2 * exports, elems), BF16)],
         connectivity,
         stress_coef,
         mode_rows,
@@ -319,8 +314,7 @@
         stress,
         far,
         near,
-        high,
-        low,
+        matrix,
         flops=4 * exports * elems * width,
     )
 

time: 42.2 us -> 42 us (level)
    all_to_all x1, blocking collectives: 13.3 us -> 11.9 us  [local(): lax.all_to_all(own_pseudo(*inputs, copies=8), AXES, 0, 0, axis_index_grou...]
    all_to_all x1, blocking collectives: 17.1 us -> 18.3 us  [own_pseudo(): got = lax.all_to_all(sent, AXES, 0, 0)]
where the time goes in v3:
time: 42 us; the launch traced here: 41.4 us
  blocking collectives  30.2 us (72%)
  Pallas kernels  4.74 us (11%)
  starting transfers between devices  3.47 us (8%)
  waiting for transfers between devices  1.98 us (5%)
  local copies, waits for them, and re-layouts  0.95 us (2%)
    all_to_all x1, blocking collectives, own_pseudo(): got = lax.all_to_all(sent, AXES, 0, 0)  18.3 us
    all_to_all x1, blocking collectives, local(): lax.all_to_all(own_pseudo(*inputs, copies=8), AXES, 0, 0, axis_index_grou...  11.9 us
    pallas_call x7, Pallas kernels, call(): pl.pallas_call(kernel, out_shape=shapes, in_specs=[whole()] * len(operand...  4.74 us
    ppermute x1, starting transfers between devices, local(): far = lax.ppermute(far, AXES, outer)  3.4 us
    ppermute x1, waiting for transfers between devices, local(): far = lax.ppermute(far, AXES, outer)  1.88 us
    unnamed x18, local copies, waits for them, and re-layouts  0.95 us
  transfers between devices with their start and end apart: 3, of which 2 were waited for; matrix products, arithmetic and copies ran while one was open for 0% of the time, Pallas kernels for 8%

profile of v3, /device:TPU:8, one launch (start us, length us, event | category | flops | bytes accessed | tf_op | source)
XLA Modules:
  0.0 41.4 jit_solution(7714980958060372597)
XLA Ops:
  0.0 0.0 copy-start.7
  0.0 0.0 copy-start.4
  0.0 0.7 %copy-done.7 = bf16[16,128]{1,0:T(8,128)(2,1)S(1)} copy-done((bf16[16,128]{1,0:T(8,128)(2,1)S(1)}, bf16[16,128]{1,0:T(8,128)(2,1)}, u32[]{:S(2)}) %copy-start.7) | copy-done | bytes 4120
  0.7 0.2 copy-done.4
  0.9 0.0 copy-start.5
  0.9 0.0 copy-start.6
  0.9 0.0 copy-start.8
  1.0 18.3 %all_to_all.10.got_ref = bf16[32,48,128]{2,1,0:T(8,128)(2,1)S(1)} all-to-all(bf16[32,48,128]{2,1,0:T(8,128)(2,1)S(1)} %pack.1), channel_id=1, replica_groups=mesh['region'=8,'sub'=4] {'region','sub'}, dimensions={0} | all-to-all | bytes 786432 | tf_op jit(solution)/shard_map/all_to_all | solution.py:232
  19.2 0.0 copy-done.5
  19.2 0.0 copy-done.6
  19.3 0.0 copy-done.8
  19.3 0.0 copy-start
  19.3 0.0 copy-start.3
  19.3 0.3 pseudo.1
  19.6 0.0 copy-start.1
  19.6 0.0 copy-start.2
  19.6 11.9 %all_to_all.11 = bf16[8,256,128]{2,1,0:T(8,128)(2,1)S(1)} all-to-all(bf16[8,256,128]{2,1,0:T(8,128)(2,1)S(1)} %pseudo.1), channel_id=1, replica_groups={{0,2,4,6,8,10,12,14},{1,3,5,7,9,11,13,15},{16,18,20,22,24,26,28,30},{17..., dimensions={0} | all-to-all | bytes 1048576 | tf_op jit(solution)/shard_map/all_to_all | solution.py:267
  31.6 0.0 collective-permute-start
  31.6 0.0 copy-done
  31.6 0.0 copy-done.3
  31.6 1.8 %first.1 = (f32[512,128]{1,0:T(8,128)S(1)}, f32[128,128]{1,0:T(8,128)S(1)}, bf16[128,2048]{1,0:T(8,128)(2,1)S(1)}) custom-call(s32[1,128]{1,0:T(1,128)S(1)} %bitcast.7, bf16[512,4096]{1,0:T(8,128)(2,1)S(1)} %copy-done, bf16[2048,128]{1,0:T(8,128)(2,1)S(1)} %bitcast.6), custom_call_target="tpu_custom_call" | custom-call | flops 536870912 | bytes 5571072 | tf_op jit(solution)/shard_map/first/pallas_call | solution.py:182
  33.4 0.1 collective-permute-done.pseudo_ref
  33.5 0.3 export.1
  33.8 3.4 %collective-permute-start.1 = (bf16[64,128]{1,0:T(8,128)(2,1)S(1)}, bf16[64,128]{1,0:T(8,128)(2,1)S(1)}, u32[]{:S(2)}, u32[]{:S(2)}) collective-permute-start(bf16[64,128]{1,0:T(8,128)(2,1)S(1)} %get-tuple-element.16), channel_id=1, source_target_pairs={{1,2},{3,4},{5,6},{7,8},{9,10},{11,12},{13,14},{15,16},{17,18},{19... | collective-permute-start | bytes 49160 | tf_op jit(solution)/shard_map/ppermute | solution.py:297
  37.2 0.1 collective-permute-start.2
  37.3 0.0 copy-done.1
  37.3 0.0 copy-done.2
  37.3 1.5 %own.1 = (f32[128,512]{1,0:T(8,128)S(1)}, bf16[256,512]{1,0:T(8,128)(2,1)S(1)}) custom-call(s32[4,512]{1,0:T(4,128)S(1)} %copy-done.1, f32[4,512]{1,0:T(4,128)S(1)} %copy-done.2, bf16[512,4096]{1,0:T(8,128)(2,1)S(1)} %copy-done, bf16[2048,128]{1,0:T(8,128)(2,1)S(1)} %collective-permute-done.pseudo_ref, f32[512,128]{1,0:T(8,128)S(1)} %get-tuple-element.12.total_ref), custom_call_target="tpu_custom_call" | custom-call | flops 402653184 | bytes 5521408 | tf_op jit(solution)/shard_map/own/pallas_call | solution.py:182
  38.7 1.9 %collective-permute-done.1.far_ref = bf16[64,128]{1,0:T(8,128)(2,1)S(1)} collective-permute-done((bf16[64,128]{1,0:T(8,128)(2,1)S(1)}, bf16[64,128]{1,0:T(8,128)(2,1)S(1)}, u32[]{:S(2)}, u32[]{:S(2)}) %collective-permute-start.1) | collective-permute-done | bytes 16416 | tf_op jit(solution)/shard_map/ppermute | solution.py:297
  40.6 0.0 collective-permute-done.2.near_ref
  40.6 0.8 %power.1 = f32[2,512]{1,0:T(2,128)} custom-call(f32[128,512]{1,0:T(8,128)S(1)} %get-tuple-element.13.stress_ref, bf16[64,128]{1,0:T(8,128)(2,1)S(1)} %collective-permute-done.1.far_ref, bf16[64,128]{1,0:T(8,128)(2,1)S(1)} %collective-permute-done.2.near_ref, bf16[256,512]{1,0:T(8,128)(2,1)S(1)} %get-tuple-element.18.rim_ref), custom_call_target="tpu_custom_call" | custom-call | flops 33554432 | bytes 561152 | tf_op jit(solution)/shard_map/power/pallas_call | solution.py:182
  (2 shorter events, 0.0 us)
Async XLA Ops:
  0.0 0.7 %copy-start.7 = (bf16[16,128]{1,0:T(8,128)(2,1)S(1)}, bf16[16,128]{1,0:T(8,128)(2,1)}, u32[]{:S(2)}) copy-start(bf16[16,128]{1,0:T(8,128)(2,1)} %factor_ref.1) | copy-start | bytes 12292
  0.0 0.9 %copy-start.4 = (bf16[16,4096]{1,0:T(8,128)(2,1)S(1)}, bf16[16,4096]{1,0:T(8,128)(2,1)}, u32[]{:S(2)}) copy-start(bf16[16,4096]{1,0:T(8,128)(2,1)} %rows_ref.1) | copy-start | bytes 393220
  0.9 18.3 %copy-start.5 = (f32[4096]{0:T(1024)S(1)}, f32[4096]{0:T(1024)}, u32[]{:S(2)}) copy-start(f32[4096]{0:T(1024)} %param.12) | copy-start | bytes 49156
  0.9 18.3 %copy-start.6 = (f32[4096]{0:T(1024)S(1)}, f32[4096]{0:T(1024)}, u32[]{:S(2)}) copy-start(f32[4096]{0:T(1024)} %param.13) | copy-start | bytes 49156
  0.9 18.3 %copy-start.8 = (f32[2]{0:T(128)S(1)}, f32[2]{0:T(128)}, u32[]{:S(2)}) copy-start(f32[2]{0:T(128)} %param.14) | copy-start | bytes 28
  19.3 12.3 %copy-start = (bf16[512,4096]{1,0:T(8,128)(2,1)S(1)}, bf16[512,4096]{1,0:T(8,128)(2,1)}, u32[]{:S(2)}) copy-start(bf16[512,4096]{1,0:T(8,128)(2,1)} %modes_ref.3) | copy-start | bytes 12582916
  19.3 12.3 %copy-start.3 = (s32[128]{0:T(128)S(1)}, s32[128]{0:T(128)}, u32[]{:S(2)}) copy-start(s32[128]{0:T(128)} %param.15) | copy-start | bytes 1540
  19.6 17.6 %copy-start.1 = (s32[4,512]{1,0:T(4,128)S(1)}, s32[4,512]{1,0:T(4,128)}, u32[]{:S(2)}) copy-start(s32[4,512]{1,0:T(4,128)} %connect_ref.1) | copy-start | bytes 24580
  19.6 17.6 %copy-start.2 = (f32[4,512]{1,0:T(4,128)S(1)}, f32[4,512]{1,0:T(4,128)}, u32[]{:S(2)}) copy-start(f32[4,512]{1,0:T(4,128)} %coef_ref.1) | copy-start | bytes 24580
  31.6 1.9 %collective-permute-start = (bf16[2048,128]{1,0:T(8,128)(2,1)S(1)}, bf16[2048,128]{1,0:T(8,128)(2,1)S(1)}, u32[]{:S(2)}, u32[]{:S(2)}) collective-permute-start(bf16[2048,128]{1,0:T(8,128)(2,1)S(1)} %bitcast.5), channel_id=1, source_target_pairs={{0,1},{1,0},{2,3},{3,2},{4,5},{5,4},{6,7},{7,6},{8,9},{9,8},{10,11... | collective-permute-start | bytes 1572872 | tf_op jit(solution)/shard_map/ppermute | solution.py:269
  33.8 6.9 %collective-permute-start.1 = (bf16[64,128]{1,0:T(8,128)(2,1)S(1)}, bf16[64,128]{1,0:T(8,128)(2,1)S(1)}, u32[]{:S(2)}, u32[]{:S(2)}) collective-permute-start(bf16[64,128]{1,0:T(8,128)(2,1)S(1)} %get-tuple-element.16), channel_id=1, source_target_pairs={{1,2},{3,4},{5,6},{7,8},{9,10},{11,12},{13,14},{15,16},{17,18},{19... | collective-permute-start | bytes 49160 | tf_op jit(solution)/shard_map/ppermute | solution.py:297
  37.2 3.5 %collective-permute-start.2 = (bf16[64,128]{1,0:T(8,128)(2,1)S(1)}, bf16[64,128]{1,0:T(8,128)(2,1)S(1)}, u32[]{:S(2)}, u32[]{:S(2)}) collective-permute-start(bf16[64,128]{1,0:T(8,128)(2,1)S(1)} %get-tuple-element.17), channel_id=1, source_target_pairs={{0,1},{1,0},{2,3},{3,2},{4,5},{5,4},{6,7},{7,6},{8,9},{9,8},{10,11... | collective-permute-start | bytes 49160 | tf_op jit(solution)/shard_map/ppermute | solution.py:296

commit v4 on v3

--- a/solution.py
+++ b/solution.py
@@ -83,32 +83,43 @@
             pseudo_ref[copy, part * width : (part + 1) * width, :] = pseudo
 
 
-def first_kernel(boundary_ref, modes_ref, pseudo_ref, total_ref, part_ref, picked_ref):
+def for_core(depth, work):
+    odd = lax.axis_index(AXES) % 2
+    low, high = slice(0, depth), slice(depth, 2 * depth)
+    pl.when(odd == 0)(lambda: work(low, high))
+    pl.when(odd == 1)(lambda: work(high, low))
+
+
+def first_kernel(boundary_ref, modes_ref, pseudo_ref, total_ref, part_ref, picked_ref, pick_ref):
     rows = modes_ref.shape[0]
-    depth = pseudo_ref.shape[0]
-    odd = lax.axis_index(AXES) % 2
-    mine = pl.ds(pl.multiple_of(odd * depth, depth), depth)
-    other = pl.ds(pl.multiple_of((1 - odd) * depth, depth), depth)
-    total = jnp.dot(modes_ref[:, mine], pseudo_ref[...], preferred_element_type=F32)
-    total_ref[...] = total
     exports = boundary_ref.shape[1]
     chosen = jnp.broadcast_to(boundary_ref[...], (exports, exports)).astype(F32).T
     column = lax.broadcasted_iota(jnp.int32, (exports, exports), 1).astype(F32)
-    pick = jnp.concatenate(
+    pick_ref[...] = jnp.concatenate(
         [(column + start == chosen).astype(F32) for start in range(0, rows, exports)], axis=1
     ).astype(BF16)
-    high = total.astype(BF16)
-    rest = total - high.astype(F32)
-    middle = rest.astype(BF16)
-    low = (rest - middle.astype(F32)).astype(BF16)
-    parts = jnp.dot(
-        pick, jnp.concatenate([high, middle, low], axis=1), preferred_element_type=F32
-    )
-    width = total.shape[1]
-    part_ref[...] = parts[:, :width] + parts[:, width : 2 * width] + parts[:, 2 * width :]
-    picked_ref[...] = jnp.dot(
-        pick, modes_ref[:, other], preferred_element_type=F32
-    ).astype(BF16)
+
+    def product(mine, _):
+        total_ref[...] = jnp.dot(modes_ref[:, mine], pseudo_ref[...], preferred_element_type=F32)
+
+    def exported(_, other):
+        pick = pick_ref[...]
+        total = total_ref[...]
+        high = total.astype(BF16)
+        rest = total - high.astype(F32)
+        middle = rest.astype(BF16)
+        low = (rest - middle.astype(F32)).astype(BF16)
+        parts = jnp.dot(
+            pick, jnp.concatenate([high, middle, low], axis=1), preferred_element_type=F32
+        )
+        width = total.shape[1]
+        part_ref[...] = parts[:, :width] + parts[:, width : 2 * width] + parts[:, 2 * width :]
+        picked_ref[...] = jnp.dot(
+            pick, modes_ref[:, other], preferred_element_type=F32
+        ).astype(BF16)
+
+    for_core(pseudo_ref.shape[0], product)
+    for_core(pseudo_ref.shape[0], exported)
 
 
 def export_kernel(part_ref, picked_ref, pseudo_ref, far_ref, near_ref):
@@ -123,13 +134,20 @@
 
 
 def own_kernel(
-    connect_ref, coef_ref, modes_ref, pseudo_ref, total_ref, stress_ref, rim_ref, own_ref
+    connect_ref, coef_ref, modes_ref, pseudo_ref, total_ref, stress_ref, rim_ref, own_ref, table_ref
 ):
-    depth = pseudo_ref.shape[0]
     rows = modes_ref.shape[0]
     elems = connect_ref.shape[1]
     rim = rim_ref.shape[0] // 4
     odd = lax.axis_index(AXES) % 2
+
+    def responses(_, other):
+        total = total_ref[...] + jnp.dot(
+            modes_ref[:, other], pseudo_ref[...], preferred_element_type=F32
+        )
+        table_ref[...] = total.T.astype(BF16)
+
+    for_core(pseudo_ref.shape[0], responses)
 
     def matrix(start, tall):
         node = lax.broadcasted_iota(jnp.int32, (tall, elems), 0) + start
@@ -148,11 +166,7 @@
     for start in range(0, rows, rim):
         here = slice(start, start + rim)
         own_ref[0, here, :], own_ref[1, here, :] = matrix(start + rim, rim)
-    other = pl.ds(pl.multiple_of((1 - odd) * depth, depth), depth)
-    total = total_ref[...] + jnp.dot(
-        modes_ref[:, other], pseudo_ref[...], preferred_element_type=F32
-    )
-    table = total.T.astype(BF16)
+    table = table_ref[...]
     stress = jnp.dot(table, own_ref[0], preferred_element_type=F32)
     stress_ref[...] = stress + jnp.dot(table, own_ref[1], preferred_element_type=F32)
 
@@ -280,6 +294,7 @@
         mode_rows,
         mine,
         flops=rows * modes * (width + exports),
+        scratch=[pltpu.VMEM((exports, rows), BF16)],
     )
     far, near = call(
         export_kernel,
@@ -305,7 +320,7 @@
         theirs,
         total,
         flops=rows * modes * width + 4 * rows * elems * width,
-        scratch=[pltpu.VMEM((2, rows, elems), BF16)],
+        scratch=[pltpu.VMEM((2, rows, elems), BF16), pltpu.VMEM((width, rows), BF16)],
     )
     return call(
         power_kernel,

time: 42 us -> 41.7 us (level)
  waiting for transfers between devices: 1.98 us -> 2.47 us
    ppermute x1, waiting for transfers between devices: 0.1 us -> 0.54 us  [local(): theirs = lax.ppermute(mine, AXES, [(i, i ^ 1) for i in range(devices)])]
  transfers between devices with their start and end apart: 3 -> 3, of which waited for: 2 -> 2; matrix products, arithmetic and copies ran while one was open for 0% -> 0% of each run, Pallas kernels for 8% -> 7%
where the time goes in v4:
time: 41.7 us; the launch traced here: 41.4 us
  blocking collectives  30.2 us (72%)
  Pallas kernels  4.53 us (11%)
  starting transfers between devices  3.19 us (8%)
  waiting for transfers between devices  2.47 us (6%)
  local copies, waits for them, and re-layouts  0.95 us (2%)
    all_to_all x1, blocking collectives, own_pseudo(): got = lax.all_to_all(sent, AXES, 0, 0)  18.3 us
    all_to_all x1, blocking collectives, local(): lax.all_to_all(own_pseudo(*inputs, copies=8), AXES, 0, 0, axis_index_grou...  11.9 us
    pallas_call x7, Pallas kernels, call(): pl.pallas_call(kernel, out_shape=shapes, in_specs=[whole()] * len(operand...  4.53 us
    ppermute x1, starting transfers between devices, local(): far = lax.ppermute(far, AXES, outer)  3.12 us
    ppermute x1, waiting for transfers between devices, local(): far = lax.ppermute(far, AXES, outer)  1.93 us
    unnamed x18, local copies, waits for them, and re-layouts  0.95 us
  transfers between devices with their start and end apart: 3, of which 2 were waited for; matrix products, arithmetic and copies ran while one was open for 0% of the time, Pallas kernels for 7%

profile of v4, /device:TPU:8, one launch (start us, length us, event | category | flops | bytes accessed | tf_op | source)
XLA Modules:
  0.0 41.4 jit_solution(10470687446237807053)
XLA Ops:
  0.0 0.0 copy-start.7
  0.0 0.0 copy-start.4
  0.0 0.7 %copy-done.7 = bf16[16,128]{1,0:T(8,128)(2,1)S(1)} copy-done((bf16[16,128]{1,0:T(8,128)(2,1)S(1)}, bf16[16,128]{1,0:T(8,128)(2,1)}, u32[]{:S(2)}) %copy-start.7) | copy-done | bytes 4120
  0.7 0.2 copy-done.4
  0.9 0.0 copy-start.5
  0.9 0.0 copy-start.6
  0.9 0.0 copy-start.8
  1.0 18.3 %all_to_all.10.got_ref = bf16[32,48,128]{2,1,0:T(8,128)(2,1)S(1)} all-to-all(bf16[32,48,128]{2,1,0:T(8,128)(2,1)S(1)} %pack.1), channel_id=1, replica_groups=mesh['region'=8,'sub'=4] {'region','sub'}, dimensions={0} | all-to-all | bytes 786432 | tf_op jit(solution)/shard_map/all_to_all | solution.py:246
  19.2 0.0 copy-done.5
  19.2 0.0 copy-done.6
  19.3 0.0 copy-done.8
  19.3 0.0 copy-start
  19.3 0.0 copy-start.3
  19.3 0.3 pseudo.1
  19.6 0.0 copy-start.1
  19.6 0.0 copy-start.2
  19.6 11.9 %all_to_all.11 = bf16[8,256,128]{2,1,0:T(8,128)(2,1)S(1)} all-to-all(bf16[8,256,128]{2,1,0:T(8,128)(2,1)S(1)} %pseudo.1), channel_id=1, replica_groups={{0,2,4,6,8,10,12,14},{1,3,5,7,9,11,13,15},{16,18,20,22,24,26,28,30},{17..., dimensions={0} | all-to-all | bytes 1048576 | tf_op jit(solution)/shard_map/all_to_all | solution.py:281
  31.6 0.0 collective-permute-start
  31.6 0.0 copy-done
  31.6 0.0 copy-done.3
  31.6 1.4 %first.1 = (f32[512,128]{1,0:T(8,128)S(1)}, f32[128,128]{1,0:T(8,128)S(1)}, bf16[128,2048]{1,0:T(8,128)(2,1)S(1)}) custom-call(s32[1,128]{1,0:T(1,128)S(1)} %bitcast.7, bf16[512,4096]{1,0:T(8,128)(2,1)S(1)} %copy-done, bf16[2048,128]{1,0:T(8,128)(2,1)S(1)} %bitcast.6), custom_call_target="tpu_custom_call" | custom-call | flops 536870912 | bytes 5571072 | tf_op jit(solution)/shard_map/first/pallas_call | solution.py:196
  32.9 0.5 %collective-permute-done.pseudo_ref = bf16[2048,128]{1,0:T(8,128)(2,1)S(1)} collective-permute-done((bf16[2048,128]{1,0:T(8,128)(2,1)S(1)}, bf16[2048,128]{1,0:T(8,128)(2,1)S(1)}, u32[]{:S(2)}, u32[]{:S(2)}) %collective-permute-start) | collective-permute-done | bytes 524320 | tf_op jit(solution)/shard_map/ppermute | solution.py:283
  33.5 0.3 export.1
  33.8 3.1 %collective-permute-start.1 = (bf16[64,128]{1,0:T(8,128)(2,1)S(1)}, bf16[64,128]{1,0:T(8,128)(2,1)S(1)}, u32[]{:S(2)}, u32[]{:S(2)}) collective-permute-start(bf16[64,128]{1,0:T(8,128)(2,1)S(1)} %get-tuple-element.16), channel_id=1, source_target_pairs={{1,2},{3,4},{5,6},{7,8},{9,10},{11,12},{13,14},{15,16},{17,18},{19... | collective-permute-start | bytes 49160 | tf_op jit(solution)/shard_map/ppermute | solution.py:312
  36.9 0.1 collective-permute-start.2
  37.0 0.0 copy-done.1
  37.0 0.0 copy-done.2
  37.0 1.7 %own.1 = (f32[128,512]{1,0:T(8,128)S(1)}, bf16[256,512]{1,0:T(8,128)(2,1)S(1)}) custom-call(s32[4,512]{1,0:T(4,128)S(1)} %copy-done.1, f32[4,512]{1,0:T(4,128)S(1)} %copy-done.2, bf16[512,4096]{1,0:T(8,128)(2,1)S(1)} %copy-done, bf16[2048,128]{1,0:T(8,128)(2,1)S(1)} %collective-permute-done.pseudo_ref, f32[512,128]{1,0:T(8,128)S(1)} %get-tuple-element.12.total_ref), custom_call_target="tpu_custom_call" | custom-call | flops 402653184 | bytes 5521408 | tf_op jit(solution)/shard_map/own/pallas_call | solution.py:196
  38.7 1.9 %collective-permute-done.1.far_ref = bf16[64,128]{1,0:T(8,128)(2,1)S(1)} collective-permute-done((bf16[64,128]{1,0:T(8,128)(2,1)S(1)}, bf16[64,128]{1,0:T(8,128)(2,1)S(1)}, u32[]{:S(2)}, u32[]{:S(2)}) %collective-permute-start.1) | collective-permute-done | bytes 16416 | tf_op jit(solution)/shard_map/ppermute | solution.py:312
  40.6 0.0 collective-permute-done.2.near_ref
  40.6 0.8 %power.1 = f32[2,512]{1,0:T(2,128)} custom-call(f32[128,512]{1,0:T(8,128)S(1)} %get-tuple-element.13.stress_ref, bf16[64,128]{1,0:T(8,128)(2,1)S(1)} %collective-permute-done.1.far_ref, bf16[64,128]{1,0:T(8,128)(2,1)S(1)} %collective-permute-done.2.near_ref, bf16[256,512]{1,0:T(8,128)(2,1)S(1)} %get-tuple-element.18.rim_ref), custom_call_target="tpu_custom_call" | custom-call | flops 33554432 | bytes 561152 | tf_op jit(solution)/shard_map/power/pallas_call | solution.py:196
  (2 shorter events, 0.0 us)
Async XLA Ops:
  0.0 0.7 %copy-start.7 = (bf16[16,128]{1,0:T(8,128)(2,1)S(1)}, bf16[16,128]{1,0:T(8,128)(2,1)}, u32[]{:S(2)}) copy-start(bf16[16,128]{1,0:T(8,128)(2,1)} %factor_ref.1) | copy-start | bytes 12292
  0.0 0.9 %copy-start.4 = (bf16[16,4096]{1,0:T(8,128)(2,1)S(1)}, bf16[16,4096]{1,0:T(8,128)(2,1)}, u32[]{:S(2)}) copy-start(bf16[16,4096]{1,0:T(8,128)(2,1)} %rows_ref.1) | copy-start | bytes 393220
  0.9 18.3 %copy-start.5 = (f32[4096]{0:T(1024)S(1)}, f32[4096]{0:T(1024)}, u32[]{:S(2)}) copy-start(f32[4096]{0:T(1024)} %param.12) | copy-start | bytes 49156
  0.9 18.3 %copy-start.6 = (f32[4096]{0:T(1024)S(1)}, f32[4096]{0:T(1024)}, u32[]{:S(2)}) copy-start(f32[4096]{0:T(1024)} %param.13) | copy-start | bytes 49156
  0.9 18.3 %copy-start.8 = (f32[2]{0:T(128)S(1)}, f32[2]{0:T(128)}, u32[]{:S(2)}) copy-start(f32[2]{0:T(128)} %param.14) | copy-start | bytes 28
  19.3 12.3 %copy-start = (bf16[512,4096]{1,0:T(8,128)(2,1)S(1)}, bf16[512,4096]{1,0:T(8,128)(2,1)}, u32[]{:S(2)}) copy-start(bf16[512,4096]{1,0:T(8,128)(2,1)} %modes_ref.3) | copy-start | bytes 12582916
  19.3 12.3 %copy-start.3 = (s32[128]{0:T(128)S(1)}, s32[128]{0:T(128)}, u32[]{:S(2)}) copy-start(s32[128]{0:T(128)} %param.15) | copy-start | bytes 1540
  19.6 17.4 %copy-start.1 = (s32[4,512]{1,0:T(4,128)S(1)}, s32[4,512]{1,0:T(4,128)}, u32[]{:S(2)}) copy-start(s32[4,512]{1,0:T(4,128)} %connect_ref.1) | copy-start | bytes 24580
  19.6 17.4 %copy-start.2 = (f32[4,512]{1,0:T(4,128)S(1)}, f32[4,512]{1,0:T(4,128)}, u32[]{:S(2)}) copy-start(f32[4,512]{1,0:T(4,128)} %coef_ref.1) | copy-start | bytes 24580
  31.6 1.9 %collective-permute-start = (bf16[2048,128]{1,0:T(8,128)(2,1)S(1)}, bf16[2048,128]{1,0:T(8,128)(2,1)S(1)}, u32[]{:S(2)}, u32[]{:S(2)}) collective-permute-start(bf16[2048,128]{1,0:T(8,128)(2,1)S(1)} %bitcast.5), channel_id=1, source_target_pairs={{0,1},{1,0},{2,3},{3,2},{4,5},{5,4},{6,7},{7,6},{8,9},{9,8},{10,11... | collective-permute-start | bytes 1572872 | tf_op jit(solution)/shard_map/ppermute | solution.py:283
  33.8 6.9 %collective-permute-start.1 = (bf16[64,128]{1,0:T(8,128)(2,1)S(1)}, bf16[64,128]{1,0:T(8,128)(2,1)S(1)}, u32[]{:S(2)}, u32[]{:S(2)}) collective-permute-start(bf16[64,128]{1,0:T(8,128)(2,1)S(1)} %get-tuple-element.16), channel_id=1, source_target_pairs={{1,2},{3,4},{5,6},{7,8},{9,10},{11,12},{13,14},{15,16},{17,18},{19... | collective-permute-start | bytes 49160 | tf_op jit(solution)/shard_map/ppermute | solution.py:312
  36.9 3.7 %collective-permute-start.2 = (bf16[64,128]{1,0:T(8,128)(2,1)S(1)}, bf16[64,128]{1,0:T(8,128)(2,1)S(1)}, u32[]{:S(2)}, u32[]{:S(2)}) collective-permute-start(bf16[64,128]{1,0:T(8,128)(2,1)S(1)} %get-tuple-element.17), channel_id=1, source_target_pairs={{0,1},{1,0},{2,3},{3,2},{4,5},{5,4},{6,7},{7,6},{8,9},{9,8},{10,11... | collective-permute-start | bytes 49160 | tf_op jit(solution)/shard_map/ppermute | solution.py:311

commit v5 on v4

--- a/solution.py
+++ b/solution.py
@@ -29,7 +29,8 @@
 
 
 def slab_of(device):
-    return device % 2 * 8 + device // 2 % 8
+    chip = device // 2 % 8
+    return device % 2 * 8 + (chip ^ (chip // 2) ^ (chip // 4))
 
 
 def ones_kernel(ones_ref):
@@ -277,7 +278,8 @@
     elems = connectivity.shape[1]
     inputs = (input_rows, input_factor, mode_freq, mode_damping, line_freq)
     if shape == FAST_SHAPE and modes == devices * LANES and input_rows.shape[0] % 16 == 0:
-        groups = [[h * 16 + j * 2 + c for j in range(8)] for h in range(2) for c in range(2)]
+        cycle = [place ^ (place // 2) for place in range(8)]
+        groups = [[h * 16 + j * 2 + c for j in cycle] for h in range(2) for c in range(2)]
         got = lax.all_to_all(own_pseudo(*inputs, copies=8), AXES, 0, 0, axis_index_groups=groups)
         mine = got.reshape(modes // 2, width)
         theirs = lax.ppermute(mine, AXES, [(i, i ^ 1) for i in range(devices)])

time: 41.7 us -> 41.7 us (level)
  no operation moved by 1% of the time
where the time goes in v5:
time: 41.7 us; the launch traced here: 41.5 us
  blocking collectives  30.2 us (72%)
  Pallas kernels  4.52 us (11%)
  starting transfers between devices  3.2 us (8%)
  waiting for transfers between devices  2.47 us (6%)
  local copies, waits for them, and re-layouts  0.95 us (2%)
    all_to_all x1, blocking collectives, own_pseudo(): got = lax.all_to_all(sent, AXES, 0, 0)  18.3 us
    all_to_all x1, blocking collectives, local(): lax.all_to_all(own_pseudo(*inputs, copies=8), AXES, 0, 0, axis_index_grou...  11.9 us
    pallas_call x7, Pallas kernels, call(): pl.pallas_call(kernel, out_shape=shapes, in_specs=[whole()] * len(operand...  4.52 us
    ppermute x1, starting transfers between devices, local(): far = lax.ppermute(far, AXES, outer)  3.13 us
    ppermute x1, waiting for transfers between devices, local(): far = lax.ppermute(far, AXES, outer)  1.93 us
    unnamed x18, local copies, waits for them, and re-layouts  0.95 us
  transfers between devices with their start and end apart: 3, of which 2 were waited for; matrix products, arithmetic and copies ran while one was open for 0% of the time, Pallas kernels for 7%

profile of v5, /device:TPU:8, one launch (start us, length us, event | category | flops | bytes accessed | tf_op | source)
XLA Modules:
  0.0 41.5 jit_solution(12633065044818339401)
XLA Ops:
  0.0 0.0 copy-start.7
  0.0 0.0 copy-start.4
  0.0 0.7 %copy-done.7 = bf16[16,128]{1,0:T(8,128)(2,1)S(1)} copy-done((bf16[16,128]{1,0:T(8,128)(2,1)S(1)}, bf16[16,128]{1,0:T(8,128)(2,1)}, u32[]{:S(2)}) %copy-start.7) | copy-done | bytes 4120
  0.7 0.2 copy-done.4
  0.9 0.0 copy-start.5
  0.9 0.0 copy-start.6
  0.9 0.0 copy-start.8
  1.0 18.3 %all_to_all.10.got_ref = bf16[32,48,128]{2,1,0:T(8,128)(2,1)S(1)} all-to-all(bf16[32,48,128]{2,1,0:T(8,128)(2,1)S(1)} %pack.1), channel_id=1, replica_groups=mesh['region'=8,'sub'=4] {'region','sub'}, dimensions={0} | all-to-all | bytes 786432 | tf_op jit(solution)/shard_map/all_to_all | solution.py:247
  19.2 0.0 copy-done.5
  19.2 0.0 copy-done.6
  19.3 0.0 copy-done.8
  19.3 0.0 copy-start
  19.3 0.0 copy-start.3
  19.3 0.3 pseudo.1
  19.6 0.0 copy-start.1
  19.6 0.0 copy-start.2
  19.6 11.9 %all_to_all.11 = bf16[8,256,128]{2,1,0:T(8,128)(2,1)S(1)} all-to-all(bf16[8,256,128]{2,1,0:T(8,128)(2,1)S(1)} %pseudo.1), channel_id=1, replica_groups={{0,2,6,4,12,14,10,8},{1,3,7,5,13,15,11,9},{16,18,22,20,28,30,26,24},{17..., dimensions={0} | all-to-all | bytes 1048576 | tf_op jit(solution)/shard_map/all_to_all | solution.py:283
  31.6 0.0 collective-permute-start
  31.6 0.0 copy-done
  31.6 0.0 copy-done.3
  31.6 1.4 %first.1 = (f32[512,128]{1,0:T(8,128)S(1)}, f32[128,128]{1,0:T(8,128)S(1)}, bf16[128,2048]{1,0:T(8,128)(2,1)S(1)}) custom-call(s32[1,128]{1,0:T(1,128)S(1)} %bitcast.7, bf16[512,4096]{1,0:T(8,128)(2,1)S(1)} %copy-done, bf16[2048,128]{1,0:T(8,128)(2,1)S(1)} %bitcast.6), custom_call_target="tpu_custom_call" | custom-call | flops 536870912 | bytes 5571072 | tf_op jit(solution)/shard_map/first/pallas_call | solution.py:197
  33.0 0.5 %collective-permute-done.pseudo_ref = bf16[2048,128]{1,0:T(8,128)(2,1)S(1)} collective-permute-done((bf16[2048,128]{1,0:T(8,128)(2,1)S(1)}, bf16[2048,128]{1,0:T(8,128)(2,1)S(1)}, u32[]{:S(2)}, u32[]{:S(2)}) %collective-permute-start) | collective-permute-done | bytes 524320 | tf_op jit(solution)/shard_map/ppermute | solution.py:285
  33.5 0.3 export.1
  33.8 3.1 %collective-permute-start.1 = (bf16[64,128]{1,0:T(8,128)(2,1)S(1)}, bf16[64,128]{1,0:T(8,128)(2,1)S(1)}, u32[]{:S(2)}, u32[]{:S(2)}) collective-permute-start(bf16[64,128]{1,0:T(8,128)(2,1)S(1)} %get-tuple-element.16), channel_id=1, source_target_pairs={{1,2},{3,4},{5,6},{7,8},{9,10},{11,12},{13,14},{15,16},{17,18},{19... | collective-permute-start | bytes 49160 | tf_op jit(solution)/shard_map/ppermute | solution.py:314
  36.9 0.1 collective-permute-start.2
  37.0 0.0 copy-done.1
  37.0 0.0 copy-done.2
  37.0 1.7 %own.1 = (f32[128,512]{1,0:T(8,128)S(1)}, bf16[256,512]{1,0:T(8,128)(2,1)S(1)}) custom-call(s32[4,512]{1,0:T(4,128)S(1)} %copy-done.1, f32[4,512]{1,0:T(4,128)S(1)} %copy-done.2, bf16[512,4096]{1,0:T(8,128)(2,1)S(1)} %copy-done, bf16[2048,128]{1,0:T(8,128)(2,1)S(1)} %collective-permute-done.pseudo_ref, f32[512,128]{1,0:T(8,128)S(1)} %get-tuple-element.12.total_ref), custom_call_target="tpu_custom_call" | custom-call | flops 402653184 | bytes 5521408 | tf_op jit(solution)/shard_map/own/pallas_call | solution.py:197
  38.7 1.9 %collective-permute-done.1.far_ref = bf16[64,128]{1,0:T(8,128)(2,1)S(1)} collective-permute-done((bf16[64,128]{1,0:T(8,128)(2,1)S(1)}, bf16[64,128]{1,0:T(8,128)(2,1)S(1)}, u32[]{:S(2)}, u32[]{:S(2)}) %collective-permute-start.1) | collective-permute-done | bytes 16416 | tf_op jit(solution)/shard_map/ppermute | solution.py:314
  40.7 0.0 collective-permute-done.2.near_ref
  40.7 0.8 %power.1 = f32[2,512]{1,0:T(2,128)} custom-call(f32[128,512]{1,0:T(8,128)S(1)} %get-tuple-element.13.stress_ref, bf16[64,128]{1,0:T(8,128)(2,1)S(1)} %collective-permute-done.1.far_ref, bf16[64,128]{1,0:T(8,128)(2,1)S(1)} %collective-permute-done.2.near_ref, bf16[256,512]{1,0:T(8,128)(2,1)S(1)} %get-tuple-element.18.rim_ref), custom_call_target="tpu_custom_call" | custom-call | flops 33554432 | bytes 561152 | tf_op jit(solution)/shard_map/power/pallas_call | solution.py:197
  (2 shorter events, 0.0 us)
Async XLA Ops:
  0.0 0.7 %copy-start.7 = (bf16[16,128]{1,0:T(8,128)(2,1)S(1)}, bf16[16,128]{1,0:T(8,128)(2,1)}, u32[]{:S(2)}) copy-start(bf16[16,128]{1,0:T(8,128)(2,1)} %factor_ref.1) | copy-start | bytes 12292
  0.0 0.9 %copy-start.4 = (bf16[16,4096]{1,0:T(8,128)(2,1)S(1)}, bf16[16,4096]{1,0:T(8,128)(2,1)}, u32[]{:S(2)}) copy-start(bf16[16,4096]{1,0:T(8,128)(2,1)} %rows_ref.1) | copy-start | bytes 393220
  0.9 18.3 %copy-start.5 = (f32[4096]{0:T(1024)S(1)}, f32[4096]{0:T(1024)}, u32[]{:S(2)}) copy-start(f32[4096]{0:T(1024)} %param.12) | copy-start | bytes 49156
  0.9 18.3 %copy-start.6 = (f32[4096]{0:T(1024)S(1)}, f32[4096]{0:T(1024)}, u32[]{:S(2)}) copy-start(f32[4096]{0:T(1024)} %param.13) | copy-start | bytes 49156
  0.9 18.3 %copy-start.8 = (f32[2]{0:T(128)S(1)}, f32[2]{0:T(128)}, u32[]{:S(2)}) copy-start(f32[2]{0:T(128)} %param.14) | copy-start | bytes 28
  19.3 12.3 %copy-start = (bf16[512,4096]{1,0:T(8,128)(2,1)S(1)}, bf16[512,4096]{1,0:T(8,128)(2,1)}, u32[]{:S(2)}) copy-start(bf16[512,4096]{1,0:T(8,128)(2,1)} %modes_ref.3) | copy-start | bytes 12582916
  19.3 12.3 %copy-start.3 = (s32[128]{0:T(128)S(1)}, s32[128]{0:T(128)}, u32[]{:S(2)}) copy-start(s32[128]{0:T(128)} %param.15) | copy-start | bytes 1540
  19.6 17.4 %copy-start.1 = (s32[4,512]{1,0:T(4,128)S(1)}, s32[4,512]{1,0:T(4,128)}, u32[]{:S(2)}) copy-start(s32[4,512]{1,0:T(4,128)} %connect_ref.1) | copy-start | bytes 24580
  19.6 17.4 %copy-start.2 = (f32[4,512]{1,0:T(4,128)S(1)}, f32[4,512]{1,0:T(4,128)}, u32[]{:S(2)}) copy-start(f32[4,512]{1,0:T(4,128)} %coef_ref.1) | copy-start | bytes 24580
  31.6 1.9 %collective-permute-start = (bf16[2048,128]{1,0:T(8,128)(2,1)S(1)}, bf16[2048,128]{1,0:T(8,128)(2,1)S(1)}, u32[]{:S(2)}, u32[]{:S(2)}) collective-permute-start(bf16[2048,128]{1,0:T(8,128)(2,1)S(1)} %bitcast.5), channel_id=1, source_target_pairs={{0,1},{1,0},{2,3},{3,2},{4,5},{5,4},{6,7},{7,6},{8,9},{9,8},{10,11... | collective-permute-start | bytes 1572872 | tf_op jit(solution)/shard_map/ppermute | solution.py:285
  33.8 6.9 %collective-permute-start.1 = (bf16[64,128]{1,0:T(8,128)(2,1)S(1)}, bf16[64,128]{1,0:T(8,128)(2,1)S(1)}, u32[]{:S(2)}, u32[]{:S(2)}) collective-permute-start(bf16[64,128]{1,0:T(8,128)(2,1)S(1)} %get-tuple-element.16), channel_id=1, source_target_pairs={{1,2},{3,4},{5,6},{7,8},{9,10},{11,12},{13,14},{15,16},{17,18},{19... | collective-permute-start | bytes 49160 | tf_op jit(solution)/shard_map/ppermute | solution.py:314
  36.9 3.7 %collective-permute-start.2 = (bf16[64,128]{1,0:T(8,128)(2,1)S(1)}, bf16[64,128]{1,0:T(8,128)(2,1)S(1)}, u32[]{:S(2)}, u32[]{:S(2)}) collective-permute-start(bf16[64,128]{1,0:T(8,128)(2,1)S(1)} %get-tuple-element.17), channel_id=1, source_target_pairs={{0,1},{1,0},{2,3},{3,2},{4,5},{5,4},{6,7},{7,6},{8,9},{9,8},{10,11... | collective-permute-start | bytes 49160 | tf_op jit(solution)/shard_map/ppermute | solution.py:313

commit v6 on v5

--- a/solution.py
+++ b/solution.py
@@ -123,10 +123,12 @@
     for_core(pseudo_ref.shape[0], exported)
 
 
-def export_kernel(part_ref, picked_ref, pseudo_ref, far_ref, near_ref):
+def export_kernel(part_ref, picked_ref, low_ref, high_ref, far_ref, near_ref):
+    cut = low_ref.shape[0]
     export = part_ref[...] + jnp.dot(
-        picked_ref[...], pseudo_ref[...], preferred_element_type=F32
-    )
+        picked_ref[:, :cut], low_ref[...], preferred_element_type=F32
+    )
+    export = export + jnp.dot(picked_ref[:, cut:], high_ref[...], preferred_element_type=F32)
     export = export.astype(BF16)
     odd = lax.axis_index(AXES) % 2 == 1
     rim = far_ref.shape[0]
@@ -135,7 +137,8 @@
 
 
 def own_kernel(
-    connect_ref, coef_ref, modes_ref, pseudo_ref, total_ref, stress_ref, rim_ref, own_ref, table_ref
+    connect_ref, coef_ref, modes_ref, low_ref, high_ref, total_ref,
+    stress_ref, rim_ref, own_ref, table_ref,
 ):
     rows = modes_ref.shape[0]
     elems = connect_ref.shape[1]
@@ -143,12 +146,15 @@
     odd = lax.axis_index(AXES) % 2
 
     def responses(_, other):
-        total = total_ref[...] + jnp.dot(
-            modes_ref[:, other], pseudo_ref[...], preferred_element_type=F32
-        )
+        total = total_ref[...]
+        cut = low_ref.shape[0]
+        for part_ref, start in ((low_ref, other.start), (high_ref, other.start + cut)):
+            total = total + jnp.dot(
+                modes_ref[:, start : start + cut], part_ref[...], preferred_element_type=F32
+            )
         table_ref[...] = total.T.astype(BF16)
 
-    for_core(pseudo_ref.shape[0], responses)
+    for_core(2 * low_ref.shape[0], responses)
 
     def matrix(start, tall):
         node = lax.broadcasted_iota(jnp.int32, (tall, elems), 0) + start
@@ -282,12 +288,15 @@
         groups = [[h * 16 + j * 2 + c for j in cycle] for h in range(2) for c in range(2)]
         got = lax.all_to_all(own_pseudo(*inputs, copies=8), AXES, 0, 0, axis_index_groups=groups)
         mine = got.reshape(modes // 2, width)
-        theirs = lax.ppermute(mine, AXES, [(i, i ^ 1) for i in range(devices)])
+        cut = modes // 4
+        swap = [(i, i ^ 1) for i in range(devices)]
+        theirs = [lax.ppermute(part, AXES, swap) for part in (mine[:cut], mine[cut:])]
     else:
         pseudo = pseudo_by_sum(*inputs).reshape(2, modes // 2, width)
         core = lax.axis_index(AXES) % 2
         mine = lax.dynamic_index_in_dim(pseudo, core, 0, keepdims=False)
-        theirs = lax.dynamic_index_in_dim(pseudo, 1 - core, 0, keepdims=False)
+        other = lax.dynamic_index_in_dim(pseudo, 1 - core, 0, keepdims=False)
+        theirs = [other[: modes // 4], other[modes // 4 :]]
     total, part, picked = call(
         first_kernel,
         "first",
@@ -304,7 +313,7 @@
         [((rim, width), BF16)] * 2,
         part,
         picked,
-        theirs,
+        *theirs,
         flops=exports * modes * width,
     )
     inner = [(i, i ^ 1) for i in range(devices)]
@@ -319,7 +328,7 @@
         connectivity,
         stress_coef,
         mode_rows,
-        theirs,
+        *theirs,
         total,
         flops=rows * modes * width + 4 * rows * elems * width,
         scratch=[pltpu.VMEM((2, rows, elems), BF16), pltpu.VMEM((width, rows), BF16)],

time: 41.7 us -> 41.8 us (level)
  starting transfers between devices: 3.2 us -> 3.77 us
  waiting for transfers between devices: 2.47 us -> 1.96 us
    ppermute x1 -> x2, starting transfers between devices: 0.01 us -> 0.57 us  [local(): lax.ppermute(part, AXES, swap)]
    ppermute x1 -> x2, waiting for transfers between devices: 0.54 us -> 0.03 us  [local(): lax.ppermute(part, AXES, swap)]
  transfers between devices with their start and end apart: 3 -> 4, of which waited for: 2 -> 1; matrix products, arithmetic and copies ran while one was open for 0% -> 0% of each run, Pallas kernels for 7% -> 7%
where the time goes in v6:
time: 41.8 us; the launch traced here: 41.6 us
  blocking collectives  30.2 us (72%)
  Pallas kernels  4.52 us (11%)
  starting transfers between devices  3.77 us (9%)
  waiting for transfers between devices  1.96 us (5%)
  local copies, waits for them, and re-layouts  0.98 us (2%)
    all_to_all x1, blocking collectives, own_pseudo(): got = lax.all_to_all(sent, AXES, 0, 0)  18.3 us
    all_to_all x1, blocking collectives, local(): lax.all_to_all(own_pseudo(*inputs, copies=8), AXES, 0, 0, axis_index_grou...  11.9 us
    pallas_call x7, Pallas kernels, call(): pl.pallas_call(kernel, out_shape=shapes, in_specs=[whole()] * len(operand...  4.52 us
    ppermute x1, starting transfers between devices, local(): far = lax.ppermute(far, AXES, outer)  3.13 us
    ppermute x1, waiting for transfers between devices, local(): far = lax.ppermute(far, AXES, outer)  1.93 us
    unnamed x18, local copies, waits for them, and re-layouts  0.95 us
  transfers between devices with their start and end apart: 4, of which 1 were waited for; matrix products, arithmetic and copies ran while one was open for 0% of the time, Pallas kernels for 7%

profile of v6, /device:TPU:8, one launch (start us, length us, event | category | flops | bytes accessed | tf_op | source)
XLA Modules:
  0.0 41.6 jit_solution(17745837551594028611)
XLA Ops:
  0.0 0.0 copy-start.7
  0.0 0.0 copy-start.4
  0.0 0.7 %copy-done.7 = bf16[16,128]{1,0:T(8,128)(2,1)S(1)} copy-done((bf16[16,128]{1,0:T(8,128)(2,1)S(1)}, bf16[16,128]{1,0:T(8,128)(2,1)}, u32[]{:S(2)}) %copy-start.7) | copy-done | bytes 4120
  0.7 0.2 copy-done.4
  0.9 0.0 copy-start.5
  0.9 0.0 copy-start.6
  0.9 0.0 copy-start.8
  1.0 18.3 %all_to_all.10.got_ref = bf16[32,48,128]{2,1,0:T(8,128)(2,1)S(1)} all-to-all(bf16[32,48,128]{2,1,0:T(8,128)(2,1)S(1)} %pack.1), channel_id=1, replica_groups=mesh['region'=8,'sub'=4] {'region','sub'}, dimensions={0} | all-to-all | bytes 786432 | tf_op jit(solution)/shard_map/all_to_all | solution.py:253
  19.2 0.0 copy-done.5
  19.2 0.0 copy-done.6
  19.3 0.0 copy-done.8
  19.3 0.0 copy-start
  19.3 0.0 copy-start.3
  19.3 0.3 pseudo.1
  19.6 0.0 copy-start.1
  19.6 0.0 copy-start.2
  19.6 11.9 %all_to_all.11 = bf16[8,256,128]{2,1,0:T(8,128)(2,1)S(1)} all-to-all(bf16[8,256,128]{2,1,0:T(8,128)(2,1)S(1)} %pseudo.1), channel_id=1, replica_groups={{0,2,6,4,12,14,10,8},{1,3,7,5,13,15,11,9},{16,18,22,20,28,30,26,24},{17..., dimensions={0} | all-to-all | bytes 1048576 | tf_op jit(solution)/shard_map/all_to_all | solution.py:289
  31.6 0.1 collective-permute-start
  31.7 0.5 %collective-permute-start.1 = (bf16[1024,128]{1,0:T(8,128)(2,1)S(1)}, bf16[1024,128]{1,0:T(8,128)(2,1)S(1)}, u32[]{:S(2)}, u32[]{:S(2)}) collective-permute-start(bf16[1024,128]{1,0:T(8,128)(2,1)S(1)} %bitcast.12), channel_id=1, source_target_pairs={{0,1},{1,0},{2,3},{3,2},{4,5},{5,4},{6,7},{7,6},{8,9},{9,8},{10,11... | collective-permute-start | bytes 786440 | tf_op jit(solution)/shard_map/ppermute | solution.py:293
  32.2 0.0 copy-done
  32.2 0.0 copy-done.3
  32.2 1.4 %first.1 = (f32[512,128]{1,0:T(8,128)S(1)}, f32[128,128]{1,0:T(8,128)S(1)}, bf16[128,2048]{1,0:T(8,128)(2,1)S(1)}) custom-call(s32[1,128]{1,0:T(1,128)S(1)} %bitcast.8, bf16[512,4096]{1,0:T(8,128)(2,1)S(1)} %copy-done, bf16[2048,128]{1,0:T(8,128)(2,1)S(1)} %bitcast.7), custom_call_target="tpu_custom_call" | custom-call | flops 536870912 | bytes 5571072 | tf_op jit(solution)/shard_map/first/pallas_call | solution.py:203
  33.6 0.0 collective-permute-done.low_ref
  33.6 0.0 collective-permute-done.1.high_ref
  33.6 0.3 export.1
  33.9 3.1 %collective-permute-start.2 = (bf16[64,128]{1,0:T(8,128)(2,1)S(1)}, bf16[64,128]{1,0:T(8,128)(2,1)S(1)}, u32[]{:S(2)}, u32[]{:S(2)}) collective-permute-start(bf16[64,128]{1,0:T(8,128)(2,1)S(1)} %get-tuple-element.16), channel_id=1, source_target_pairs={{1,2},{3,4},{5,6},{7,8},{9,10},{11,12},{13,14},{15,16},{17,18},{19... | collective-permute-start | bytes 49160 | tf_op jit(solution)/shard_map/ppermute | solution.py:323
  37.0 0.1 collective-permute-start.3
  37.1 0.0 copy-done.1
  37.1 0.0 copy-done.2
  37.1 1.7 %own.1 = (f32[128,512]{1,0:T(8,128)S(1)}, bf16[256,512]{1,0:T(8,128)(2,1)S(1)}) custom-call(s32[4,512]{1,0:T(4,128)S(1)} %copy-done.1, f32[4,512]{1,0:T(4,128)S(1)} %copy-done.2, bf16[512,4096]{1,0:T(8,128)(2,1)S(1)} %copy-done, bf16[1024,128]{1,0:T(8,128)(2,1)S(1)} %collective-permute-done.low_ref, bf16[1024,128]{1,0:T(8,128)(2,1)S(1)} %collective-permute-done.1.high_ref, ...), custom_call_target="tpu_custom_call" | custom-call | flops 402653184 | bytes 5521408 | tf_op jit(solution)/shard_map/own/pallas_call | solution.py:203
  38.8 1.9 %collective-permute-done.2.far_ref = bf16[64,128]{1,0:T(8,128)(2,1)S(1)} collective-permute-done((bf16[64,128]{1,0:T(8,128)(2,1)S(1)}, bf16[64,128]{1,0:T(8,128)(2,1)S(1)}, u32[]{:S(2)}, u32[]{:S(2)}) %collective-permute-start.2) | collective-permute-done | bytes 16416 | tf_op jit(solution)/shard_map/ppermute | solution.py:323
  40.8 0.0 collective-permute-done.3.near_ref
  40.8 0.8 %power.1 = f32[2,512]{1,0:T(2,128)} custom-call(f32[128,512]{1,0:T(8,128)S(1)} %get-tuple-element.13.stress_ref, bf16[64,128]{1,0:T(8,128)(2,1)S(1)} %collective-permute-done.2.far_ref, bf16[64,128]{1,0:T(8,128)(2,1)S(1)} %collective-permute-done.3.near_ref, bf16[256,512]{1,0:T(8,128)(2,1)S(1)} %get-tuple-element.18.rim_ref), custom_call_target="tpu_custom_call" | custom-call | flops 33554432 | bytes 561152 | tf_op jit(solution)/shard_map/power/pallas_call | solution.py:203
  (3 shorter events, 0.1 us)
Async XLA Ops:
  0.0 0.7 %copy-start.7 = (bf16[16,128]{1,0:T(8,128)(2,1)S(1)}, bf16[16,128]{1,0:T(8,128)(2,1)}, u32[]{:S(2)}) copy-start(bf16[16,128]{1,0:T(8,128)(2,1)} %factor_ref.1) | copy-start | bytes 12292
  0.0 0.9 %copy-start.4 = (bf16[16,4096]{1,0:T(8,128)(2,1)S(1)}, bf16[16,4096]{1,0:T(8,128)(2,1)}, u32[]{:S(2)}) copy-start(bf16[16,4096]{1,0:T(8,128)(2,1)} %rows_ref.1) | copy-start | bytes 393220
  0.9 18.3 %copy-start.5 = (f32[4096]{0:T(1024)S(1)}, f32[4096]{0:T(1024)}, u32[]{:S(2)}) copy-start(f32[4096]{0:T(1024)} %param.12) | copy-start | bytes 49156
  0.9 18.3 %copy-start.6 = (f32[4096]{0:T(1024)S(1)}, f32[4096]{0:T(1024)}, u32[]{:S(2)}) copy-start(f32[4096]{0:T(1024)} %param.13) | copy-start | bytes 49156
  0.9 18.3 %copy-start.8 = (f32[2]{0:T(128)S(1)}, f32[2]{0:T(128)}, u32[]{:S(2)}) copy-start(f32[2]{0:T(128)} %param.14) | copy-start | bytes 28
  19.3 12.9 %copy-start = (bf16[512,4096]{1,0:T(8,128)(2,1)S(1)}, bf16[512,4096]{1,0:T(8,128)(2,1)}, u32[]{:S(2)}) copy-start(bf16[512,4096]{1,0:T(8,128)(2,1)} %modes_ref.3) | copy-start | bytes 12582916
  19.3 12.9 %copy-start.3 = (s32[128]{0:T(128)S(1)}, s32[128]{0:T(128)}, u32[]{:S(2)}) copy-start(s32[128]{0:T(128)} %param.15) | copy-start | bytes 1540
  19.6 17.5 %copy-start.1 = (s32[4,512]{1,0:T(4,128)S(1)}, s32[4,512]{1,0:T(4,128)}, u32[]{:S(2)}) copy-start(s32[4,512]{1,0:T(4,128)} %connect_ref.1) | copy-start | bytes 24580
  19.6 17.5 %copy-start.2 = (f32[4,512]{1,0:T(4,128)S(1)}, f32[4,512]{1,0:T(4,128)}, u32[]{:S(2)}) copy-start(f32[4,512]{1,0:T(4,128)} %coef_ref.1) | copy-start | bytes 24580
  31.6 1.9 %collective-permute-start = (bf16[1024,128]{1,0:T(8,128)(2,1)S(1)}, bf16[1024,128]{1,0:T(8,128)(2,1)S(1)}, u32[]{:S(2)}, u32[]{:S(2)}) collective-permute-start(bf16[1024,128]{1,0:T(8,128)(2,1)S(1)} %bitcast.13), channel_id=1, source_target_pairs={{0,1},{1,0},{2,3},{3,2},{4,5},{5,4},{6,7},{7,6},{8,9},{9,8},{10,11... | collective-permute-start | bytes 786440 | tf_op jit(solution)/shard_map/ppermute | solution.py:293
  31.7 1.9 %collective-permute-start.1 = (bf16[1024,128]{1,0:T(8,128)(2,1)S(1)}, bf16[1024,128]{1,0:T(8,128)(2,1)S(1)}, u32[]{:S(2)}, u32[]{:S(2)}) collective-permute-start(bf16[1024,128]{1,0:T(8,128)(2,1)S(1)} %bitcast.12), channel_id=1, source_target_pairs={{0,1},{1,0},{2,3},{3,2},{4,5},{5,4},{6,7},{7,6},{8,9},{9,8},{10,11... | collective-permute-start | bytes 786440 | tf_op jit(solution)/shard_map/ppermute | solution.py:293
  33.9 6.9 %collective-permute-start.2 = (bf16[64,128]{1,0:T(8,128)(2,1)S(1)}, bf16[64,128]{1,0:T(8,128)(2,1)S(1)}, u32[]{:S(2)}, u32[]{:S(2)}) collective-permute-start(bf16[64,128]{1,0:T(8,128)(2,1)S(1)} %get-tuple-element.16), channel_id=1, source_target_pairs={{1,2},{3,4},{5,6},{7,8},{9,10},{11,12},{13,14},{15,16},{17,18},{19... | collective-permute-start | bytes 49160 | tf_op jit(solution)/shard_map/ppermute | solution.py:323
  37.0 3.7 %collective-permute-start.3 = (bf16[64,128]{1,0:T(8,128)(2,1)S(1)}, bf16[64,128]{1,0:T(8,128)(2,1)S(1)}, u32[]{:S(2)}, u32[]{:S(2)}) collective-permute-start(bf16[64,128]{1,0:T(8,128)(2,1)S(1)} %get-tuple-element.17), channel_id=1, source_target_pairs={{0,1},{1,0},{2,3},{3,2},{4,5},{5,4},{6,7},{7,6},{8,9},{9,8},{10,11... | collective-permute-start | bytes 49160 | tf_op jit(solution)/shard_map/ppermute | solution.py:322

commit v7 on v6

--- a/solution.py
+++ b/solution.py
@@ -49,7 +49,9 @@
         sent_ref[device, parts * rows :, :] = factor
 
 
-def pseudo_kernel(line_ref, freq_ref, damping_ref, got_ref, pseudo_ref, *, rows):
+def pseudo_kernel(
+    boundary_ref, line_ref, freq_ref, damping_ref, got_ref, pseudo_ref, pick_ref, *, rows
+):
     devices, tall, width = got_ref.shape
     parts = tall // rows - 1
     lines = line_ref.shape[1]
@@ -82,6 +84,12 @@
         pseudo = jnp.concatenate(pieces, axis=0).T.astype(BF16)
         for copy in range(pseudo_ref.shape[0]):
             pseudo_ref[copy, part * width : (part + 1) * width, :] = pseudo
+    exports, owned = pick_ref.shape
+    chosen = jnp.broadcast_to(boundary_ref[...], (exports, exports)).astype(F32).T
+    column = lax.broadcasted_iota(jnp.int32, (exports, exports), 1).astype(F32)
+    for start in range(0, owned, exports):
+        pick = (column + start == chosen).astype(F32).astype(BF16)
+        pick_ref[:, start : start + exports] = pick
 
 
 def for_core(depth, work):
@@ -91,36 +99,28 @@
     pl.when(odd == 1)(lambda: work(high, low))
 
 
-def first_kernel(boundary_ref, modes_ref, pseudo_ref, total_ref, part_ref, picked_ref, pick_ref):
-    rows = modes_ref.shape[0]
-    exports = boundary_ref.shape[1]
-    chosen = jnp.broadcast_to(boundary_ref[...], (exports, exports)).astype(F32).T
-    column = lax.broadcasted_iota(jnp.int32, (exports, exports), 1).astype(F32)
-    pick_ref[...] = jnp.concatenate(
-        [(column + start == chosen).astype(F32) for start in range(0, rows, exports)], axis=1
-    ).astype(BF16)
-
-    def product(mine, _):
-        total_ref[...] = jnp.dot(modes_ref[:, mine], pseudo_ref[...], preferred_element_type=F32)
-
-    def exported(_, other):
-        pick = pick_ref[...]
-        total = total_ref[...]
-        high = total.astype(BF16)
-        rest = total - high.astype(F32)
-        middle = rest.astype(BF16)
-        low = (rest - middle.astype(F32)).astype(BF16)
-        parts = jnp.dot(
-            pick, jnp.concatenate([high, middle, low], axis=1), preferred_element_type=F32
-        )
-        width = total.shape[1]
-        part_ref[...] = parts[:, :width] + parts[:, width : 2 * width] + parts[:, 2 * width :]
+def first_kernel(pick_ref, modes_ref, pseudo_ref, total_ref, part_ref, picked_ref):
+    depth = pseudo_ref.shape[0]
+    odd = lax.axis_index(AXES) % 2
+    mine = pl.ds(pl.multiple_of(odd * depth, depth), depth)
+    total_ref[...] = jnp.dot(modes_ref[:, mine], pseudo_ref[...], preferred_element_type=F32)
+
+    def shapes(_, other):
         picked_ref[...] = jnp.dot(
-            pick, modes_ref[:, other], preferred_element_type=F32
+            pick_ref[...], modes_ref[:, other], preferred_element_type=F32
         ).astype(BF16)
 
-    for_core(pseudo_ref.shape[0], product)
-    for_core(pseudo_ref.shape[0], exported)
+    for_core(depth, shapes)
+    total = total_ref[...]
+    high = total.astype(BF16)
+    rest = total - high.astype(F32)
+    middle = rest.astype(BF16)
+    low = (rest - middle.astype(F32)).astype(BF16)
+    parts = jnp.dot(
+        pick_ref[...], jnp.concatenate([high, middle, low], axis=1), preferred_element_type=F32
+    )
+    width = total.shape[1]
+    part_ref[...] = parts[:, :width] + parts[:, width : 2 * width] + parts[:, 2 * width :]
 
 
 def export_kernel(part_ref, picked_ref, low_ref, high_ref, far_ref, near_ref):
@@ -234,7 +234,9 @@
     return jnp.concatenate(pieces, axis=1).astype(BF16)
 
 
-def own_pseudo(input_rows, input_factor, mode_freq, mode_damping, line_freq, copies):
+def own_pseudo(
+    input_rows, input_factor, mode_freq, mode_damping, line_freq, boundary_rows, owned, copies
+):
     devices = math.prod(FAST_SHAPE)
     rows, modes = input_rows.shape
     width = input_factor.shape[1]
@@ -254,7 +256,8 @@
     return call(
         functools.partial(pseudo_kernel, rows=rows),
         "pseudo",
-        [((copies, parts * width, width), BF16)],
+        [((copies, parts * width, width), BF16), ((boundary_rows.shape[0], owned), BF16)],
+        boundary_rows.reshape(1, -1),
         line_freq.reshape(1, lines),
         mode_freq.reshape(-1, width),
         mode_damping.reshape(-1, width),
@@ -286,13 +289,15 @@
     if shape == FAST_SHAPE and modes == devices * LANES and input_rows.shape[0] % 16 == 0:
         cycle = [place ^ (place // 2) for place in range(8)]
         groups = [[h * 16 + j * 2 + c for j in cycle] for h in range(2) for c in range(2)]
-        got = lax.all_to_all(own_pseudo(*inputs, copies=8), AXES, 0, 0, axis_index_groups=groups)
+        block, pick = own_pseudo(*inputs, boundary_rows, rows, copies=8)
+        got = lax.all_to_all(block, AXES, 0, 0, axis_index_groups=groups)
         mine = got.reshape(modes // 2, width)
         cut = modes // 4
         swap = [(i, i ^ 1) for i in range(devices)]
         theirs = [lax.ppermute(part, AXES, swap) for part in (mine[:cut], mine[cut:])]
     else:
         pseudo = pseudo_by_sum(*inputs).reshape(2, modes // 2, width)
+        pick = (boundary_rows[:, None] == jnp.arange(rows)[None, :]).astype(BF16)
         core = lax.axis_index(AXES) % 2
         mine = lax.dynamic_index_in_dim(pseudo, core, 0, keepdims=False)
         other = lax.dynamic_index_in_dim(pseudo, 1 - core, 0, keepdims=False)
@@ -301,11 +306,10 @@
         first_kernel,
         "first",
         [((rows, width), F32), ((exports, width), F32), ((exports, modes // 2), BF16)],
-        boundary_rows.reshape(1, exports),
+        pick,
         mode_rows,
         mine,
         flops=rows * modes * (width + exports),
-        scratch=[pltpu.VMEM((exports, rows), BF16)],
     )
     far, near = call(
         export_kernel,

time: 41.8 us -> 41.8 us (level)
  no operation moved by 1% of the time
where the time goes in v7:
time: 41.8 us; the launch traced here: 41.6 us
  blocking collectives  30.2 us (72%)
  Pallas kernels  4.55 us (11%)
  starting transfers between devices  3.75 us (9%)
  waiting for transfers between devices  1.95 us (5%)
  local copies, waits for them, and re-layouts  0.97 us (2%)
    all_to_all x1, blocking collectives, own_pseudo(): got = lax.all_to_all(sent, AXES, 0, 0)  18.3 us
    all_to_all x1, blocking collectives, local(): got = lax.all_to_all(block, AXES, 0, 0, axis_index_groups=groups)  11.9 us
    pallas_call x7, Pallas kernels, call(): pl.pallas_call(kernel, out_shape=shapes, in_specs=[whole()] * len(operand...  4.55 us
    ppermute x1, starting transfers between devices, local(): far = lax.ppermute(far, AXES, outer)  3.11 us
    ppermute x1, waiting for transfers between devices, local(): far = lax.ppermute(far, AXES, outer)  1.95 us
    unnamed x18, local copies, waits for them, and re-layouts  0.94 us
  transfers between devices with their start and end apart: 4, of which 1 were waited for; matrix products, arithmetic and copies ran while one was open for 0% of the time, Pallas kernels for 7%

profile of v7, /device:TPU:8, one launch (start us, length us, event | category | flops | bytes accessed | tf_op | source)
XLA Modules:
  0.0 41.6 jit_solution(7934606553174570335)
XLA Ops:
  0.0 0.0 copy-start.3
  0.0 0.0 copy-start.6
  0.0 0.9 %copy-done.3 = bf16[16,4096]{1,0:T(8,128)(2,1)S(1)} copy-done((bf16[16,4096]{1,0:T(8,128)(2,1)S(1)}, bf16[16,4096]{1,0:T(8,128)(2,1)}, u32[]{:S(2)}) %copy-start.3) | copy-done | bytes 131096
  0.9 0.0 copy-done.6
  0.9 0.0 copy-start.4
  0.9 0.0 copy-start.5
  0.9 0.0 copy-start.7
  0.9 0.0 copy-start.8
  1.0 18.3 %all_to_all.10.got_ref = bf16[32,48,128]{2,1,0:T(8,128)(2,1)S(1)} all-to-all(bf16[32,48,128]{2,1,0:T(8,128)(2,1)S(1)} %pack.1), channel_id=1, replica_groups=mesh['region'=8,'sub'=4] {'region','sub'}, dimensions={0} | all-to-all | bytes 786432 | tf_op jit(solution)/shard_map/all_to_all | solution.py:255
  19.3 0.0 copy-done.4
  19.3 0.0 copy-done.5
  19.3 0.0 copy-done.7
  19.3 0.0 copy-done.8
  19.3 0.0 copy-start
  19.3 0.3 pseudo.1
  19.6 0.0 copy-start.1
  19.6 0.0 copy-start.2
  19.6 11.9 %all_to_all.11 = bf16[8,256,128]{2,1,0:T(8,128)(2,1)S(1)} all-to-all(bf16[8,256,128]{2,1,0:T(8,128)(2,1)S(1)} %get-tuple-element.14), channel_id=1, replica_groups={{0,2,6,4,12,14,10,8},{1,3,7,5,13,15,11,9},{16,18,22,20,28,30,26,24},{17..., dimensions={0} | all-to-all | bytes 1048576 | tf_op jit(solution)/shard_map/all_to_all | solution.py:293
  31.6 0.1 collective-permute-start
  31.7 0.5 %collective-permute-start.1 = (bf16[1024,128]{1,0:T(8,128)(2,1)S(1)}, bf16[1024,128]{1,0:T(8,128)(2,1)S(1)}, u32[]{:S(2)}, u32[]{:S(2)}) collective-permute-start(bf16[1024,128]{1,0:T(8,128)(2,1)S(1)} %bitcast.12), channel_id=1, source_target_pairs={{0,1},{1,0},{2,3},{3,2},{4,5},{5,4},{6,7},{7,6},{8,9},{9,8},{10,11... | collective-permute-start | bytes 786440 | tf_op jit(solution)/shard_map/ppermute | solution.py:297
  32.2 0.0 copy-done
  32.2 1.4 %first.1 = (f32[512,128]{1,0:T(8,128)S(1)}, f32[128,128]{1,0:T(8,128)S(1)}, bf16[128,2048]{1,0:T(8,128)(2,1)S(1)}) custom-call(bf16[128,512]{1,0:T(8,128)(2,1)S(1)} %get-tuple-element.15.pick_ref, bf16[512,4096]{1,0:T(8,128)(2,1)S(1)} %copy-done, bf16[2048,128]{1,0:T(8,128)(2,1)S(1)} %bitcast.7), custom_call_target="tpu_custom_call" | custom-call | flops 536870912 | bytes 5701632 | tf_op jit(solution)/shard_map/first/pallas_call | solution.py:203
  33.6 0.0 collective-permute-done.low_ref
  33.6 0.0 collective-permute-done.1.high_ref
  33.6 0.3 export.1
  33.9 3.1 %collective-permute-start.2 = (bf16[64,128]{1,0:T(8,128)(2,1)S(1)}, bf16[64,128]{1,0:T(8,128)(2,1)S(1)}, u32[]{:S(2)}, u32[]{:S(2)}) collective-permute-start(bf16[64,128]{1,0:T(8,128)(2,1)S(1)} %get-tuple-element.20), channel_id=1, source_target_pairs={{1,2},{3,4},{5,6},{7,8},{9,10},{11,12},{13,14},{15,16},{17,18},{19... | collective-permute-start | bytes 49160 | tf_op jit(solution)/shard_map/ppermute | solution.py:327
  37.0 0.1 collective-permute-start.3
  37.1 0.0 copy-done.1
  37.1 0.0 copy-done.2
  37.1 1.7 %own.1 = (f32[128,512]{1,0:T(8,128)S(1)}, bf16[256,512]{1,0:T(8,128)(2,1)S(1)}) custom-call(s32[4,512]{1,0:T(4,128)S(1)} %copy-done.1, f32[4,512]{1,0:T(4,128)S(1)} %copy-done.2, bf16[512,4096]{1,0:T(8,128)(2,1)S(1)} %copy-done, bf16[1024,128]{1,0:T(8,128)(2,1)S(1)} %collective-permute-done.low_ref, bf16[1024,128]{1,0:T(8,128)(2,1)S(1)} %collective-permute-done.1.high_ref, ...), custom_call_target="tpu_custom_call" | custom-call | flops 402653184 | bytes 5521408 | tf_op jit(solution)/shard_map/own/pallas_call | solution.py:203
  38.8 1.9 %collective-permute-done.2.far_ref = bf16[64,128]{1,0:T(8,128)(2,1)S(1)} collective-permute-done((bf16[64,128]{1,0:T(8,128)(2,1)S(1)}, bf16[64,128]{1,0:T(8,128)(2,1)S(1)}, u32[]{:S(2)}, u32[]{:S(2)}) %collective-permute-start.2) | collective-permute-done | bytes 16416 | tf_op jit(solution)/shard_map/ppermute | solution.py:327
  40.8 0.0 collective-permute-done.3.near_ref
  40.8 0.8 %power.1 = f32[2,512]{1,0:T(2,128)} custom-call(f32[128,512]{1,0:T(8,128)S(1)} %get-tuple-element.17.stress_ref, bf16[64,128]{1,0:T(8,128)(2,1)S(1)} %collective-permute-done.2.far_ref, bf16[64,128]{1,0:T(8,128)(2,1)S(1)} %collective-permute-done.3.near_ref, bf16[256,512]{1,0:T(8,128)(2,1)S(1)} %get-tuple-element.22.rim_ref), custom_call_target="tpu_custom_call" | custom-call | flops 33554432 | bytes 561152 | tf_op jit(solution)/shard_map/power/pallas_call | solution.py:203
  (3 shorter events, 0.1 us)
Async XLA Ops:
  0.0 0.9 %copy-start.3 = (bf16[16,4096]{1,0:T(8,128)(2,1)S(1)}, bf16[16,4096]{1,0:T(8,128)(2,1)}, u32[]{:S(2)}) copy-start(bf16[16,4096]{1,0:T(8,128)(2,1)} %rows_ref.1) | copy-start | bytes 393220
  0.0 0.9 %copy-start.6 = (bf16[16,128]{1,0:T(8,128)(2,1)S(1)}, bf16[16,128]{1,0:T(8,128)(2,1)}, u32[]{:S(2)}) copy-start(bf16[16,128]{1,0:T(8,128)(2,1)} %factor_ref.1) | copy-start | bytes 12292
  0.9 18.3 %copy-start.4 = (f32[4096]{0:T(1024)S(1)}, f32[4096]{0:T(1024)}, u32[]{:S(2)}) copy-start(f32[4096]{0:T(1024)} %param.12) | copy-start | bytes 49156
  0.9 18.3 %copy-start.5 = (f32[4096]{0:T(1024)S(1)}, f32[4096]{0:T(1024)}, u32[]{:S(2)}) copy-start(f32[4096]{0:T(1024)} %param.13) | copy-start | bytes 49156
  0.9 18.3 %copy-start.7 = (s32[128]{0:T(128)S(1)}, s32[128]{0:T(128)}, u32[]{:S(2)}) copy-start(s32[128]{0:T(128)} %param.15) | copy-start | bytes 1540
  0.9 18.3 %copy-start.8 = (f32[2]{0:T(128)S(1)}, f32[2]{0:T(128)}, u32[]{:S(2)}) copy-start(f32[2]{0:T(128)} %param.14) | copy-start | bytes 28
  19.3 12.9 %copy-start = (bf16[512,4096]{1,0:T(8,128)(2,1)S(1)}, bf16[512,4096]{1,0:T(8,128)(2,1)}, u32[]{:S(2)}) copy-start(bf16[512,4096]{1,0:T(8,128)(2,1)} %modes_ref.3) | copy-start | bytes 12582916
  19.6 17.5 %copy-start.1 = (s32[4,512]{1,0:T(4,128)S(1)}, s32[4,512]{1,0:T(4,128)}, u32[]{:S(2)}) copy-start(s32[4,512]{1,0:T(4,128)} %connect_ref.1) | copy-start | bytes 24580
  19.6 17.5 %copy-start.2 = (f32[4,512]{1,0:T(4,128)S(1)}, f32[4,512]{1,0:T(4,128)}, u32[]{:S(2)}) copy-start(f32[4,512]{1,0:T(4,128)} %coef_ref.1) | copy-start | bytes 24580
  31.6 2.0 %collective-permute-start = (bf16[1024,128]{1,0:T(8,128)(2,1)S(1)}, bf16[1024,128]{1,0:T(8,128)(2,1)S(1)}, u32[]{:S(2)}, u32[]{:S(2)}) collective-permute-start(bf16[1024,128]{1,0:T(8,128)(2,1)S(1)} %bitcast.13), channel_id=1, source_target_pairs={{0,1},{1,0},{2,3},{3,2},{4,5},{5,4},{6,7},{7,6},{8,9},{9,8},{10,11... | collective-permute-start | bytes 786440 | tf_op jit(solution)/shard_map/ppermute | solution.py:297
  31.7 1.9 %collective-permute-start.1 = (bf16[1024,128]{1,0:T(8,128)(2,1)S(1)}, bf16[1024,128]{1,0:T(8,128)(2,1)S(1)}, u32[]{:S(2)}, u32[]{:S(2)}) collective-permute-start(bf16[1024,128]{1,0:T(8,128)(2,1)S(1)} %bitcast.12), channel_id=1, source_target_pairs={{0,1},{1,0},{2,3},{3,2},{4,5},{5,4},{6,7},{7,6},{8,9},{9,8},{10,11... | collective-permute-start | bytes 786440 | tf_op jit(solution)/shard_map/ppermute | solution.py:297
  33.9 6.9 %collective-permute-start.2 = (bf16[64,128]{1,0:T(8,128)(2,1)S(1)}, bf16[64,128]{1,0:T(8,128)(2,1)S(1)}, u32[]{:S(2)}, u32[]{:S(2)}) collective-permute-start(bf16[64,128]{1,0:T(8,128)(2,1)S(1)} %get-tuple-element.20), channel_id=1, source_target_pairs={{1,2},{3,4},{5,6},{7,8},{9,10},{11,12},{13,14},{15,16},{17,18},{19... | collective-permute-start | bytes 49160 | tf_op jit(solution)/shard_map/ppermute | solution.py:327
  37.0 3.7 %collective-permute-start.3 = (bf16[64,128]{1,0:T(8,128)(2,1)S(1)}, bf16[64,128]{1,0:T(8,128)(2,1)S(1)}, u32[]{:S(2)}, u32[]{:S(2)}) collective-permute-start(bf16[64,128]{1,0:T(8,128)(2,1)S(1)} %get-tuple-element.21), channel_id=1, source_target_pairs={{0,1},{1,0},{2,3},{3,2},{4,5},{5,4},{6,7},{7,6},{8,9},{9,8},{10,11... | collective-permute-start | bytes 49160 | tf_op jit(solution)/shard_map/ppermute | solution.py:326

commit v8 on v5

--- a/solution.py
+++ b/solution.py
@@ -124,9 +124,15 @@
 
 
 def export_kernel(part_ref, picked_ref, pseudo_ref, far_ref, near_ref):
-    export = part_ref[...] + jnp.dot(
-        picked_ref[...], pseudo_ref[...], preferred_element_type=F32
-    )
+    exports = part_ref.shape[0]
+    cut = pseudo_ref.shape[0] // 2
+    width = pseudo_ref.shape[1]
+    both = jnp.dot(
+        jnp.concatenate([picked_ref[:, :cut], picked_ref[:, cut:]], axis=0),
+        jnp.concatenate([pseudo_ref[:cut], pseudo_ref[cut:]], axis=1),
+        preferred_element_type=F32,
+    )
+    export = part_ref[...] + both[:exports, :width] + both[exports:, width:]
     export = export.astype(BF16)
     odd = lax.axis_index(AXES) % 2 == 1
     rim = far_ref.shape[0]
@@ -142,13 +148,12 @@
     rim = rim_ref.shape[0] // 4
     odd = lax.axis_index(AXES) % 2
 
-    def responses(_, other):
-        total = total_ref[...] + jnp.dot(
-            modes_ref[:, other], pseudo_ref[...], preferred_element_type=F32
-        )
-        table_ref[...] = total.T.astype(BF16)
-
-    for_core(pseudo_ref.shape[0], responses)
+    depth = pseudo_ref.shape[0]
+    other = pl.ds(pl.multiple_of((1 - odd) * depth, depth), depth)
+    total = total_ref[...] + jnp.dot(
+        modes_ref[:, other], pseudo_ref[...], preferred_element_type=F32
+    )
+    table_ref[...] = total.T.astype(BF16)
 
     def matrix(start, tall):
         node = lax.broadcasted_iota(jnp.int32, (tall, elems), 0) + start

time: 41.7 us -> 41.7 us (level)
  no operation moved by 1% of the time
where the time goes in v8:
time: 41.7 us; the launch traced here: 41.5 us
  blocking collectives  30.2 us (72%)
  Pallas kernels  4.32 us (10%)
  starting transfers between devices  3.2 us (8%)
  waiting for transfers between devices  2.7 us (6%)
  local copies, waits for them, and re-layouts  0.95 us (2%)
    all_to_all x1, blocking collectives, own_pseudo(): got = lax.all_to_all(sent, AXES, 0, 0)  18.3 us
    all_to_all x1, blocking collectives, local(): lax.all_to_all(own_pseudo(*inputs, copies=8), AXES, 0, 0, axis_index_grou...  11.9 us
    pallas_call x7, Pallas kernels, call(): pl.pallas_call(kernel, out_shape=shapes, in_specs=[whole()] * len(operand...  4.32 us
    ppermute x1, starting transfers between devices, local(): far = lax.ppermute(far, AXES, outer)  3.13 us
    ppermute x1, waiting for transfers between devices, local(): far = lax.ppermute(far, AXES, outer)  2.15 us
    unnamed x18, local copies, waits for them, and re-layouts  0.95 us
  transfers between devices with their start and end apart: 3, of which 2 were waited for; matrix products, arithmetic and copies ran while one was open for 0% of the time, Pallas kernels for 7%

profile of v8, /device:TPU:8, one launch (start us, length us, event | category | flops | bytes accessed | tf_op | source)
XLA Modules:
  0.0 41.5 jit_solution(5486876910957342704)
XLA Ops:
  0.0 0.0 copy-start.7
  0.0 0.0 copy-start.4
  0.0 0.7 %copy-done.7 = bf16[16,128]{1,0:T(8,128)(2,1)S(1)} copy-done((bf16[16,128]{1,0:T(8,128)(2,1)S(1)}, bf16[16,128]{1,0:T(8,128)(2,1)}, u32[]{:S(2)}) %copy-start.7) | copy-done | bytes 4120
  0.7 0.2 copy-done.4
  0.9 0.0 copy-start.5
  0.9 0.0 copy-start.6
  0.9 0.0 copy-start.8
  1.0 18.3 %all_to_all.10.got_ref = bf16[32,48,128]{2,1,0:T(8,128)(2,1)S(1)} all-to-all(bf16[32,48,128]{2,1,0:T(8,128)(2,1)S(1)} %pack.1), channel_id=1, replica_groups=mesh['region'=8,'sub'=4] {'region','sub'}, dimensions={0} | all-to-all | bytes 786432 | tf_op jit(solution)/shard_map/all_to_all | solution.py:252
  19.2 0.0 copy-done.5
  19.2 0.0 copy-done.6
  19.3 0.0 copy-done.8
  19.3 0.0 copy-start
  19.3 0.0 copy-start.3
  19.3 0.3 pseudo.1
  19.6 0.0 copy-start.1
  19.6 0.0 copy-start.2
  19.6 11.9 %all_to_all.11 = bf16[8,256,128]{2,1,0:T(8,128)(2,1)S(1)} all-to-all(bf16[8,256,128]{2,1,0:T(8,128)(2,1)S(1)} %pseudo.1), channel_id=1, replica_groups={{0,2,6,4,12,14,10,8},{1,3,7,5,13,15,11,9},{16,18,22,20,28,30,26,24},{17..., dimensions={0} | all-to-all | bytes 1048576 | tf_op jit(solution)/shard_map/all_to_all | solution.py:288
  31.6 0.0 collective-permute-start
  31.6 0.0 copy-done
  31.6 0.0 copy-done.3
  31.6 1.4 %first.1 = (f32[512,128]{1,0:T(8,128)S(1)}, f32[128,128]{1,0:T(8,128)S(1)}, bf16[128,2048]{1,0:T(8,128)(2,1)S(1)}) custom-call(s32[1,128]{1,0:T(1,128)S(1)} %bitcast.7, bf16[512,4096]{1,0:T(8,128)(2,1)S(1)} %copy-done, bf16[2048,128]{1,0:T(8,128)(2,1)S(1)} %bitcast.6), custom_call_target="tpu_custom_call" | custom-call | flops 536870912 | bytes 5571072 | tf_op jit(solution)/shard_map/first/pallas_call | solution.py:202
  33.0 0.5 %collective-permute-done.pseudo_ref = bf16[2048,128]{1,0:T(8,128)(2,1)S(1)} collective-permute-done((bf16[2048,128]{1,0:T(8,128)(2,1)S(1)}, bf16[2048,128]{1,0:T(8,128)(2,1)S(1)}, u32[]{:S(2)}, u32[]{:S(2)}) %collective-permute-start) | collective-permute-done | bytes 524320 | tf_op jit(solution)/shard_map/ppermute | solution.py:290
  33.5 0.3 export.1
  33.8 3.1 %collective-permute-start.1 = (bf16[64,128]{1,0:T(8,128)(2,1)S(1)}, bf16[64,128]{1,0:T(8,128)(2,1)S(1)}, u32[]{:S(2)}, u32[]{:S(2)}) collective-permute-start(bf16[64,128]{1,0:T(8,128)(2,1)S(1)} %get-tuple-element.16), channel_id=1, source_target_pairs={{1,2},{3,4},{5,6},{7,8},{9,10},{11,12},{13,14},{15,16},{17,18},{19... | collective-permute-start | bytes 49160 | tf_op jit(solution)/shard_map/ppermute | solution.py:319
  37.0 0.1 collective-permute-start.2
  37.0 0.0 copy-done.1
  37.0 0.0 copy-done.2
  37.1 1.5 %own.1 = (f32[128,512]{1,0:T(8,128)S(1)}, bf16[256,512]{1,0:T(8,128)(2,1)S(1)}) custom-call(s32[4,512]{1,0:T(4,128)S(1)} %copy-done.1, f32[4,512]{1,0:T(4,128)S(1)} %copy-done.2, bf16[512,4096]{1,0:T(8,128)(2,1)S(1)} %copy-done, bf16[2048,128]{1,0:T(8,128)(2,1)S(1)} %collective-permute-done.pseudo_ref, f32[512,128]{1,0:T(8,128)S(1)} %get-tuple-element.12.total_ref), custom_call_target="tpu_custom_call" | custom-call | flops 402653184 | bytes 5521408 | tf_op jit(solution)/shard_map/own/pallas_call | solution.py:202
  38.5 2.2 %collective-permute-done.1.far_ref = bf16[64,128]{1,0:T(8,128)(2,1)S(1)} collective-permute-done((bf16[64,128]{1,0:T(8,128)(2,1)S(1)}, bf16[64,128]{1,0:T(8,128)(2,1)S(1)}, u32[]{:S(2)}, u32[]{:S(2)}) %collective-permute-start.1) | collective-permute-done | bytes 16416 | tf_op jit(solution)/shard_map/ppermute | solution.py:319
  40.7 0.0 collective-permute-done.2.near_ref
  40.7 0.8 %power.1 = f32[2,512]{1,0:T(2,128)} custom-call(f32[128,512]{1,0:T(8,128)S(1)} %get-tuple-element.13.stress_ref, bf16[64,128]{1,0:T(8,128)(2,1)S(1)} %collective-permute-done.1.far_ref, bf16[64,128]{1,0:T(8,128)(2,1)S(1)} %collective-permute-done.2.near_ref, bf16[256,512]{1,0:T(8,128)(2,1)S(1)} %get-tuple-element.18.rim_ref), custom_call_target="tpu_custom_call" | custom-call | flops 33554432 | bytes 561152 | tf_op jit(solution)/shard_map/power/pallas_call | solution.py:202
  (2 shorter events, 0.0 us)
Async XLA Ops:
  0.0 0.7 %copy-start.7 = (bf16[16,128]{1,0:T(8,128)(2,1)S(1)}, bf16[16,128]{1,0:T(8,128)(2,1)}, u32[]{:S(2)}) copy-start(bf16[16,128]{1,0:T(8,128)(2,1)} %factor_ref.1) | copy-start | bytes 12292
  0.0 0.9 %copy-start.4 = (bf16[16,4096]{1,0:T(8,128)(2,1)S(1)}, bf16[16,4096]{1,0:T(8,128)(2,1)}, u32[]{:S(2)}) copy-start(bf16[16,4096]{1,0:T(8,128)(2,1)} %rows_ref.1) | copy-start | bytes 393220
  0.9 18.3 %copy-start.5 = (f32[4096]{0:T(1024)S(1)}, f32[4096]{0:T(1024)}, u32[]{:S(2)}) copy-start(f32[4096]{0:T(1024)} %param.12) | copy-start | bytes 49156
  0.9 18.3 %copy-start.6 = (f32[4096]{0:T(1024)S(1)}, f32[4096]{0:T(1024)}, u32[]{:S(2)}) copy-start(f32[4096]{0:T(1024)} %param.13) | copy-start | bytes 49156
  0.9 18.3 %copy-start.8 = (f32[2]{0:T(128)S(1)}, f32[2]{0:T(128)}, u32[]{:S(2)}) copy-start(f32[2]{0:T(128)} %param.14) | copy-start | bytes 28
  19.3 12.3 %copy-start = (bf16[512,4096]{1,0:T(8,128)(2,1)S(1)}, bf16[512,4096]{1,0:T(8,128)(2,1)}, u32[]{:S(2)}) copy-start(bf16[512,4096]{1,0:T(8,128)(2,1)} %modes_ref.3) | copy-start | bytes 12582916
  19.3 12.3 %copy-start.3 = (s32[128]{0:T(128)S(1)}, s32[128]{0:T(128)}, u32[]{:S(2)}) copy-start(s32[128]{0:T(128)} %param.15) | copy-start | bytes 1540
  19.6 17.4 %copy-start.1 = (s32[4,512]{1,0:T(4,128)S(1)}, s32[4,512]{1,0:T(4,128)}, u32[]{:S(2)}) copy-start(s32[4,512]{1,0:T(4,128)} %connect_ref.1) | copy-start | bytes 24580
  19.6 17.4 %copy-start.2 = (f32[4,512]{1,0:T(4,128)S(1)}, f32[4,512]{1,0:T(4,128)}, u32[]{:S(2)}) copy-start(f32[4,512]{1,0:T(4,128)} %coef_ref.1) | copy-start | bytes 24580
  31.6 1.9 %collective-permute-start = (bf16[2048,128]{1,0:T(8,128)(2,1)S(1)}, bf16[2048,128]{1,0:T(8,128)(2,1)S(1)}, u32[]{:S(2)}, u32[]{:S(2)}) collective-permute-start(bf16[2048,128]{1,0:T(8,128)(2,1)S(1)} %bitcast.5), channel_id=1, source_target_pairs={{0,1},{1,0},{2,3},{3,2},{4,5},{5,4},{6,7},{7,6},{8,9},{9,8},{10,11... | collective-permute-start | bytes 1572872 | tf_op jit(solution)/shard_map/ppermute | solution.py:290
  33.8 6.9 %collective-permute-start.1 = (bf16[64,128]{1,0:T(8,128)(2,1)S(1)}, bf16[64,128]{1,0:T(8,128)(2,1)S(1)}, u32[]{:S(2)}, u32[]{:S(2)}) collective-permute-start(bf16[64,128]{1,0:T(8,128)(2,1)S(1)} %get-tuple-element.16), channel_id=1, source_target_pairs={{1,2},{3,4},{5,6},{7,8},{9,10},{11,12},{13,14},{15,16},{17,18},{19... | collective-permute-start | bytes 49160 | tf_op jit(solution)/shard_map/ppermute | solution.py:319
  37.0 3.7 %collective-permute-start.2 = (bf16[64,128]{1,0:T(8,128)(2,1)S(1)}, bf16[64,128]{1,0:T(8,128)(2,1)S(1)}, u32[]{:S(2)}, u32[]{:S(2)}) collective-permute-start(bf16[64,128]{1,0:T(8,128)(2,1)S(1)} %get-tuple-element.17), channel_id=1, source_target_pairs={{0,1},{1,0},{2,3},{3,2},{4,5},{5,4},{6,7},{7,6},{8,9},{9,8},{10,11... | collective-permute-start | bytes 49160 | tf_op jit(solution)/shard_map/ppermute | solution.py:318

commit v9 on v8

--- a/solution.py
+++ b/solution.py
@@ -30,7 +30,7 @@
 
 def slab_of(device):
     chip = device // 2 % 8
-    return device % 2 * 8 + (chip ^ (chip // 2) ^ (chip // 4))
+    return 2 * (chip ^ (chip // 2) ^ (chip // 4)) + device % 2
 
 
 def ones_kernel(ones_ref):
@@ -41,10 +41,11 @@
     devices, _, width = sent_ref.shape
     rows = rows_ref.shape[0]
     parts = sent_ref.shape[1] // rows - 1
+    slabs = rows_ref.shape[1] // (parts * width)
     factor = factor_ref[...] * ones_ref[0:1, :].astype(BF16)
     for device in range(devices):
         for part in range(parts):
-            here = (slab_of(device) * parts + part) * width
+            here = (part * slabs + slab_of(device)) * width
             sent_ref[device, part * rows : (part + 1) * rows, :] = rows_ref[:, here : here + width]
         sent_ref[device, parts * rows :, :] = factor
 
@@ -56,6 +57,7 @@
     columns = width // lines
     half = columns // 2
     slab = slab_of(lax.axis_index(AXES))
+    slabs = freq_ref.shape[0] // parts
     factor = got_ref[:, parts * rows :, :].reshape(devices * rows, width)
     shapes = [
         got_ref[:, part * rows : (part + 1) * rows, :].reshape(devices * rows, width)
@@ -68,7 +70,7 @@
         preferred_element_type=F32,
     )
     for part in range(parts):
-        here = pl.ds(slab * parts + part, 1)
+        here = pl.ds(part * slabs + slab, 1)
         summed = forced[:, part * width : (part + 1) * width]
         pieces = []
         for line in range(lines):
@@ -80,8 +82,8 @@
             pieces.append(gain_real * real - gain_imag * imag)
             pieces.append(gain_real * imag + gain_imag * real)
         pseudo = jnp.concatenate(pieces, axis=0).T.astype(BF16)
-        for copy in range(pseudo_ref.shape[0]):
-            pseudo_ref[copy, part * width : (part + 1) * width, :] = pseudo
+        for member in range(part, pseudo_ref.shape[0], parts):
+            pseudo_ref[member] = pseudo
 
 
 def for_core(depth, work):
@@ -233,7 +235,7 @@
     return jnp.concatenate(pieces, axis=1).astype(BF16)
 
 
-def own_pseudo(input_rows, input_factor, mode_freq, mode_damping, line_freq, copies):
+def own_pseudo(input_rows, input_factor, mode_freq, mode_damping, line_freq, members):
     devices = math.prod(FAST_SHAPE)
     rows, modes = input_rows.shape
     width = input_factor.shape[1]
@@ -253,7 +255,7 @@
     return call(
         functools.partial(pseudo_kernel, rows=rows),
         "pseudo",
-        [((copies, parts * width, width), BF16)],
+        [((members, width, width), BF16)],
         line_freq.reshape(1, lines),
         mode_freq.reshape(-1, width),
         mode_damping.reshape(-1, width),
@@ -284,8 +286,9 @@
     inputs = (input_rows, input_factor, mode_freq, mode_damping, line_freq)
     if shape == FAST_SHAPE and modes == devices * LANES and input_rows.shape[0] % 16 == 0:
         cycle = [place ^ (place // 2) for place in range(8)]
-        groups = [[h * 16 + j * 2 + c for j in cycle] for h in range(2) for c in range(2)]
-        got = lax.all_to_all(own_pseudo(*inputs, copies=8), AXES, 0, 0, axis_index_groups=groups)
+        groups = [[h * 16 + j * 2 + c for j in cycle for c in range(2)] for h in range(2)]
+        block = own_pseudo(*inputs, members=16)
+        got = lax.all_to_all(block, AXES, 0, 0, axis_index_groups=groups)
         mine = got.reshape(modes // 2, width)
         theirs = lax.ppermute(mine, AXES, [(i, i ^ 1) for i in range(devices)])
     else:

time: 41.7 us -> 42.3 us (1.014)
  blocking collectives: 30.2 us -> 30.7 us
    all_to_all x1, blocking collectives: 11.9 us -> 12.5 us  [local(): got = lax.all_to_all(block, AXES, 0, 0, axis_index_groups=groups)]
where the time goes in v9:
time: 42.3 us; the launch traced here: 42 us
  blocking collectives  30.7 us (73%)
  Pallas kernels  4.32 us (10%)
  starting transfers between devices  3.44 us (8%)
  waiting for transfers between devices  2.49 us (6%)
  local copies, waits for them, and re-layouts  0.95 us (2%)
    all_to_all x1, blocking collectives, own_pseudo(): got = lax.all_to_all(sent, AXES, 0, 0)  18.3 us
    all_to_all x1, blocking collectives, local(): got = lax.all_to_all(block, AXES, 0, 0, axis_index_groups=groups)  12.5 us
    pallas_call x7, Pallas kernels, call(): pl.pallas_call(kernel, out_shape=shapes, in_specs=[whole()] * len(operand...  4.32 us
    ppermute x1, starting transfers between devices, local(): far = lax.ppermute(far, AXES, outer)  2.94 us
    ppermute x1, waiting for transfers between devices, local(): far = lax.ppermute(far, AXES, outer)  2.23 us
    unnamed x18, local copies, waits for them, and re-layouts  0.95 us
  transfers between devices with their start and end apart: 3, of which 2 were waited for; matrix products, arithmetic and copies ran while one was open for 0% of the time, Pallas kernels for 7%

profile of v9, /device:TPU:8, one launch (start us, length us, event | category | flops | bytes accessed | tf_op | source)
XLA Modules:
  0.0 42.0 jit_solution(6252272885568687223)
XLA Ops:
  0.0 0.0 copy-start.7
  0.0 0.0 copy-start.4
  0.0 0.7 %copy-done.7 = bf16[16,128]{1,0:T(8,128)(2,1)S(1)} copy-done((bf16[16,128]{1,0:T(8,128)(2,1)S(1)}, bf16[16,128]{1,0:T(8,128)(2,1)}, u32[]{:S(2)}) %copy-start.7) | copy-done | bytes 4120
  0.7 0.2 copy-done.4
  0.9 0.0 copy-start.5
  0.9 0.0 copy-start.6
  0.9 0.0 copy-start.8
  1.0 18.3 %all_to_all.10.got_ref = bf16[32,48,128]{2,1,0:T(8,128)(2,1)S(1)} all-to-all(bf16[32,48,128]{2,1,0:T(8,128)(2,1)S(1)} %pack.1), channel_id=1, replica_groups=mesh['region'=8,'sub'=4] {'region','sub'}, dimensions={0} | all-to-all | bytes 786432 | tf_op jit(solution)/shard_map/all_to_all | solution.py:254
  19.2 0.0 copy-done.5
  19.2 0.0 copy-done.6
  19.3 0.0 copy-done.8
  19.3 0.0 copy-start
  19.3 0.0 copy-start.3
  19.3 0.3 pseudo.1
  19.6 0.0 copy-start.1
  19.6 0.0 copy-start.2
  19.6 12.5 %all_to_all.11 = bf16[16,128,128]{2,1,0:T(8,128)(2,1)S(1)} all-to-all(bf16[16,128,128]{2,1,0:T(8,128)(2,1)S(1)} %pseudo.1), channel_id=1, replica_groups={{0,1,2,3,6,7,4,5,12,13,14,15,10,11,8,9},{16,17,18,19,22,23,20,21,28,29,..., dimensions={0} | all-to-all | bytes 1048576 | tf_op jit(solution)/shard_map/all_to_all | solution.py:291
  32.1 0.3 collective-permute-start
  32.4 0.0 copy-done
  32.4 0.0 copy-done.3
  32.4 1.4 %first.1 = (f32[512,128]{1,0:T(8,128)S(1)}, f32[128,128]{1,0:T(8,128)S(1)}, bf16[128,2048]{1,0:T(8,128)(2,1)S(1)}) custom-call(s32[1,128]{1,0:T(1,128)S(1)} %bitcast.7, bf16[512,4096]{1,0:T(8,128)(2,1)S(1)} %copy-done, bf16[2048,128]{1,0:T(8,128)(2,1)S(1)} %bitcast.6), custom_call_target="tpu_custom_call" | custom-call | flops 536870912 | bytes 5571072 | tf_op jit(solution)/shard_map/first/pallas_call | solution.py:204
  33.8 0.2 collective-permute-done.pseudo_ref
  34.0 0.3 export.1
  34.3 2.9 %collective-permute-start.1 = (bf16[64,128]{1,0:T(8,128)(2,1)S(1)}, bf16[64,128]{1,0:T(8,128)(2,1)S(1)}, u32[]{:S(2)}, u32[]{:S(2)}) collective-permute-start(bf16[64,128]{1,0:T(8,128)(2,1)S(1)} %get-tuple-element.16), channel_id=1, source_target_pairs={{1,2},{3,4},{5,6},{7,8},{9,10},{11,12},{13,14},{15,16},{17,18},{19... | collective-permute-start | bytes 49160 | tf_op jit(solution)/shard_map/ppermute | solution.py:322
  37.3 0.2 collective-permute-start.2
  37.5 0.0 copy-done.1
  37.5 0.0 copy-done.2
  37.5 1.5 %own.1 = (f32[128,512]{1,0:T(8,128)S(1)}, bf16[256,512]{1,0:T(8,128)(2,1)S(1)}) custom-call(s32[4,512]{1,0:T(4,128)S(1)} %copy-done.1, f32[4,512]{1,0:T(4,128)S(1)} %copy-done.2, bf16[512,4096]{1,0:T(8,128)(2,1)S(1)} %copy-done, bf16[2048,128]{1,0:T(8,128)(2,1)S(1)} %collective-permute-done.pseudo_ref, f32[512,128]{1,0:T(8,128)S(1)} %get-tuple-element.12.total_ref), custom_call_target="tpu_custom_call" | custom-call | flops 402653184 | bytes 5521408 | tf_op jit(solution)/shard_map/own/pallas_call | solution.py:204
  39.0 2.2 %collective-permute-done.1.far_ref = bf16[64,128]{1,0:T(8,128)(2,1)S(1)} collective-permute-done((bf16[64,128]{1,0:T(8,128)(2,1)S(1)}, bf16[64,128]{1,0:T(8,128)(2,1)S(1)}, u32[]{:S(2)}, u32[]{:S(2)}) %collective-permute-start.1) | collective-permute-done | bytes 16416 | tf_op jit(solution)/shard_map/ppermute | solution.py:322
  41.2 0.0 collective-permute-done.2.near_ref
  41.2 0.8 %power.1 = f32[2,512]{1,0:T(2,128)} custom-call(f32[128,512]{1,0:T(8,128)S(1)} %get-tuple-element.13.stress_ref, bf16[64,128]{1,0:T(8,128)(2,1)S(1)} %collective-permute-done.1.far_ref, bf16[64,128]{1,0:T(8,128)(2,1)S(1)} %collective-permute-done.2.near_ref, bf16[256,512]{1,0:T(8,128)(2,1)S(1)} %get-tuple-element.18.rim_ref), custom_call_target="tpu_custom_call" | custom-call | flops 33554432 | bytes 561152 | tf_op jit(solution)/shard_map/power/pallas_call | solution.py:204
  (2 shorter events, 0.0 us)
Async XLA Ops:
  0.0 0.7 %copy-start.7 = (bf16[16,128]{1,0:T(8,128)(2,1)S(1)}, bf16[16,128]{1,0:T(8,128)(2,1)}, u32[]{:S(2)}) copy-start(bf16[16,128]{1,0:T(8,128)(2,1)} %factor_ref.1) | copy-start | bytes 12292
  0.0 0.9 %copy-start.4 = (bf16[16,4096]{1,0:T(8,128)(2,1)S(1)}, bf16[16,4096]{1,0:T(8,128)(2,1)}, u32[]{:S(2)}) copy-start(bf16[16,4096]{1,0:T(8,128)(2,1)} %rows_ref.1) | copy-start | bytes 393220
  0.9 18.3 %copy-start.5 = (f32[4096]{0:T(1024)S(1)}, f32[4096]{0:T(1024)}, u32[]{:S(2)}) copy-start(f32[4096]{0:T(1024)} %param.12) | copy-start | bytes 49156
  0.9 18.3 %copy-start.6 = (f32[4096]{0:T(1024)S(1)}, f32[4096]{0:T(1024)}, u32[]{:S(2)}) copy-start(f32[4096]{0:T(1024)} %param.13) | copy-start | bytes 49156
  0.9 18.3 %copy-start.8 = (f32[2]{0:T(128)S(1)}, f32[2]{0:T(128)}, u32[]{:S(2)}) copy-start(f32[2]{0:T(128)} %param.14) | copy-start | bytes 28
  19.3 13.2 %copy-start = (bf16[512,4096]{1,0:T(8,128)(2,1)S(1)}, bf16[512,4096]{1,0:T(8,128)(2,1)}, u32[]{:S(2)}) copy-start(bf16[512,4096]{1,0:T(8,128)(2,1)} %modes_ref.3) | copy-start | bytes 12582916
  19.3 13.1 %copy-start.3 = (s32[128]{0:T(128)S(1)}, s32[128]{0:T(128)}, u32[]{:S(2)}) copy-start(s32[128]{0:T(128)} %param.15) | copy-start | bytes 1540
  19.6 17.9 %copy-start.1 = (s32[4,512]{1,0:T(4,128)S(1)}, s32[4,512]{1,0:T(4,128)}, u32[]{:S(2)}) copy-start(s32[4,512]{1,0:T(4,128)} %connect_ref.1) | copy-start | bytes 24580
  19.6 17.9 %copy-start.2 = (f32[4,512]{1,0:T(4,128)S(1)}, f32[4,512]{1,0:T(4,128)}, u32[]{:S(2)}) copy-start(f32[4,512]{1,0:T(4,128)} %coef_ref.1) | copy-start | bytes 24580
  32.1 1.9 %collective-permute-start = (bf16[2048,128]{1,0:T(8,128)(2,1)S(1)}, bf16[2048,128]{1,0:T(8,128)(2,1)S(1)}, u32[]{:S(2)}, u32[]{:S(2)}) collective-permute-start(bf16[2048,128]{1,0:T(8,128)(2,1)S(1)} %bitcast.5), channel_id=1, source_target_pairs={{0,1},{1,0},{2,3},{3,2},{4,5},{5,4},{6,7},{7,6},{8,9},{9,8},{10,11... | collective-permute-start | bytes 1572872 | tf_op jit(solution)/shard_map/ppermute | solution.py:293
  34.3 6.9 %collective-permute-start.1 = (bf16[64,128]{1,0:T(8,128)(2,1)S(1)}, bf16[64,128]{1,0:T(8,128)(2,1)S(1)}, u32[]{:S(2)}, u32[]{:S(2)}) collective-permute-start(bf16[64,128]{1,0:T(8,128)(2,1)S(1)} %get-tuple-element.16), channel_id=1, source_target_pairs={{1,2},{3,4},{5,6},{7,8},{9,10},{11,12},{13,14},{15,16},{17,18},{19... | collective-permute-start | bytes 49160 | tf_op jit(solution)/shard_map/ppermute | solution.py:322
  37.3 3.9 %collective-permute-start.2 = (bf16[64,128]{1,0:T(8,128)(2,1)S(1)}, bf16[64,128]{1,0:T(8,128)(2,1)S(1)}, u32[]{:S(2)}, u32[]{:S(2)}) collective-permute-start(bf16[64,128]{1,0:T(8,128)(2,1)S(1)} %get-tuple-element.17), channel_id=1, source_target_pairs={{0,1},{1,0},{2,3},{3,2},{4,5},{5,4},{6,7},{7,6},{8,9},{9,8},{10,11... | collective-permute-start | bytes 49160 | tf_op jit(solution)/shard_map/ppermute | solution.py:321

commit v10 on v6

--- a/solution.py
+++ b/solution.py
@@ -100,12 +100,13 @@
         [(column + start == chosen).astype(F32) for start in range(0, rows, exports)], axis=1
     ).astype(BF16)
 
-    def product(mine, _):
-        total_ref[...] = jnp.dot(modes_ref[:, mine], pseudo_ref[...], preferred_element_type=F32)
-
-    def exported(_, other):
+    def work(mine, other):
         pick = pick_ref[...]
-        total = total_ref[...]
+        picked_ref[...] = jnp.dot(
+            pick, modes_ref[:, other], preferred_element_type=F32
+        ).astype(BF16)
+        total = jnp.dot(modes_ref[:, mine], pseudo_ref[...], preferred_element_type=F32)
+        total_ref[...] = total
         high = total.astype(BF16)
         rest = total - high.astype(F32)
         middle = rest.astype(BF16)
@@ -115,12 +116,8 @@
         )
         width = total.shape[1]
         part_ref[...] = parts[:, :width] + parts[:, width : 2 * width] + parts[:, 2 * width :]
-        picked_ref[...] = jnp.dot(
-            pick, modes_ref[:, other], preferred_element_type=F32
-        ).astype(BF16)
-
-    for_core(pseudo_ref.shape[0], product)
-    for_core(pseudo_ref.shape[0], exported)
+
+    for_core(pseudo_ref.shape[0], work)
 
 
 def export_kernel(part_ref, picked_ref, low_ref, high_ref, far_ref, near_ref):
@@ -145,16 +142,12 @@
     rim = rim_ref.shape[0] // 4
     odd = lax.axis_index(AXES) % 2
 
-    def responses(_, other):
-        total = total_ref[...]
-        cut = low_ref.shape[0]
-        for part_ref, start in ((low_ref, other.start), (high_ref, other.start + cut)):
-            total = total + jnp.dot(
-                modes_ref[:, start : start + cut], part_ref[...], preferred_element_type=F32
-            )
-        table_ref[...] = total.T.astype(BF16)
-
-    for_core(2 * low_ref.shape[0], responses)
+    cut = low_ref.shape[0]
+    total = total_ref[...]
+    for part, part_ref in enumerate((low_ref, high_ref)):
+        here = pl.ds(pl.multiple_of((2 * (1 - odd) + part) * cut, cut), cut)
+        total = total + jnp.dot(modes_ref[:, here], part_ref[...], preferred_element_type=F32)
+    table_ref[...] = total.T.astype(BF16)
 
     def matrix(start, tall):
         node = lax.broadcasted_iota(jnp.int32, (tall, elems), 0) + start

time: 41.8 us -> 41.9 us (level)
  no operation moved by 1% of the time
where the time goes in v10:
time: 41.9 us; the launch traced here: 41.6 us
  blocking collectives  30.2 us (72%)
  Pallas kernels  4.52 us (11%)
  starting transfers between devices  3.71 us (9%)
  waiting for transfers between devices  2.07 us (5%)
  local copies, waits for them, and re-layouts  0.98 us (2%)
    all_to_all x1, blocking collectives, own_pseudo(): got = lax.all_to_all(sent, AXES, 0, 0)  18.3 us
    all_to_all x1, blocking collectives, local(): lax.all_to_all(own_pseudo(*inputs, copies=8), AXES, 0, 0, axis_index_grou...  11.9 us
    pallas_call x7, Pallas kernels, call(): pl.pallas_call(kernel, out_shape=shapes, in_specs=[whole()] * len(operand...  4.52 us
    ppermute x1, starting transfers between devices, local(): far = lax.ppermute(far, AXES, outer)  3.07 us
    ppermute x1, waiting for transfers between devices, local(): far = lax.ppermute(far, AXES, outer)  2.06 us
    unnamed x18, local copies, waits for them, and re-layouts  0.95 us
  transfers between devices with their start and end apart: 4, of which 1 were waited for; matrix products, arithmetic and copies ran while one was open for 0% of the time, Pallas kernels for 7%

profile of v10, /device:TPU:8, one launch (start us, length us, event | category | flops | bytes accessed | tf_op | source)
XLA Modules:
  0.0 41.6 jit_solution(17357281210033166715)
XLA Ops:
  0.0 0.0 copy-start.7
  0.0 0.0 copy-start.4
  0.0 0.7 %copy-done.7 = bf16[16,128]{1,0:T(8,128)(2,1)S(1)} copy-done((bf16[16,128]{1,0:T(8,128)(2,1)S(1)}, bf16[16,128]{1,0:T(8,128)(2,1)}, u32[]{:S(2)}) %copy-start.7) | copy-done | bytes 4120
  0.7 0.2 copy-done.4
  0.9 0.0 copy-start.5
  0.9 0.0 copy-start.6
  0.9 0.0 copy-start.8
  1.0 18.3 %all_to_all.10.got_ref = bf16[32,48,128]{2,1,0:T(8,128)(2,1)S(1)} all-to-all(bf16[32,48,128]{2,1,0:T(8,128)(2,1)S(1)} %pack.1), channel_id=1, replica_groups=mesh['region'=8,'sub'=4] {'region','sub'}, dimensions={0} | all-to-all | bytes 786432 | tf_op jit(solution)/shard_map/all_to_all | solution.py:246
  19.2 0.0 copy-done.5
  19.2 0.0 copy-done.6
  19.3 0.0 copy-done.8
  19.3 0.0 copy-start
  19.3 0.0 copy-start.3
  19.3 0.3 pseudo.1
  19.6 0.0 copy-start.1
  19.6 0.0 copy-start.2
  19.6 11.9 %all_to_all.11 = bf16[8,256,128]{2,1,0:T(8,128)(2,1)S(1)} all-to-all(bf16[8,256,128]{2,1,0:T(8,128)(2,1)S(1)} %pseudo.1), channel_id=1, replica_groups={{0,2,6,4,12,14,10,8},{1,3,7,5,13,15,11,9},{16,18,22,20,28,30,26,24},{17..., dimensions={0} | all-to-all | bytes 1048576 | tf_op jit(solution)/shard_map/all_to_all | solution.py:282
  31.6 0.1 collective-permute-start
  31.7 0.5 %collective-permute-start.1 = (bf16[1024,128]{1,0:T(8,128)(2,1)S(1)}, bf16[1024,128]{1,0:T(8,128)(2,1)S(1)}, u32[]{:S(2)}, u32[]{:S(2)}) collective-permute-start(bf16[1024,128]{1,0:T(8,128)(2,1)S(1)} %bitcast.12), channel_id=1, source_target_pairs={{0,1},{1,0},{2,3},{3,2},{4,5},{5,4},{6,7},{7,6},{8,9},{9,8},{10,11... | collective-permute-start | bytes 786440 | tf_op jit(solution)/shard_map/ppermute | solution.py:286
  32.2 0.0 copy-done
  32.2 0.0 copy-done.3
  32.2 1.4 %first.1 = (f32[512,128]{1,0:T(8,128)S(1)}, f32[128,128]{1,0:T(8,128)S(1)}, bf16[128,2048]{1,0:T(8,128)(2,1)S(1)}) custom-call(s32[1,128]{1,0:T(1,128)S(1)} %bitcast.8, bf16[512,4096]{1,0:T(8,128)(2,1)S(1)} %copy-done, bf16[2048,128]{1,0:T(8,128)(2,1)S(1)} %bitcast.7), custom_call_target="tpu_custom_call" | custom-call | flops 536870912 | bytes 5571072 | tf_op jit(solution)/shard_map/first/pallas_call | solution.py:196
  33.6 0.0 collective-permute-done.low_ref
  33.6 0.0 collective-permute-done.1.high_ref
  33.7 0.3 export.1
  34.0 3.1 %collective-permute-start.2 = (bf16[64,128]{1,0:T(8,128)(2,1)S(1)}, bf16[64,128]{1,0:T(8,128)(2,1)S(1)}, u32[]{:S(2)}, u32[]{:S(2)}) collective-permute-start(bf16[64,128]{1,0:T(8,128)(2,1)S(1)} %get-tuple-element.16), channel_id=1, source_target_pairs={{1,2},{3,4},{5,6},{7,8},{9,10},{11,12},{13,14},{15,16},{17,18},{19... | collective-permute-start | bytes 49160 | tf_op jit(solution)/shard_map/ppermute | solution.py:316
  37.0 0.1 collective-permute-start.3
  37.1 0.0 copy-done.1
  37.1 0.0 copy-done.2
  37.1 1.6 %own.1 = (f32[128,512]{1,0:T(8,128)S(1)}, bf16[256,512]{1,0:T(8,128)(2,1)S(1)}) custom-call(s32[4,512]{1,0:T(4,128)S(1)} %copy-done.1, f32[4,512]{1,0:T(4,128)S(1)} %copy-done.2, bf16[512,4096]{1,0:T(8,128)(2,1)S(1)} %copy-done, bf16[1024,128]{1,0:T(8,128)(2,1)S(1)} %collective-permute-done.low_ref, bf16[1024,128]{1,0:T(8,128)(2,1)S(1)} %collective-permute-done.1.high_ref, ...), custom_call_target="tpu_custom_call" | custom-call | flops 402653184 | bytes 5521408 | tf_op jit(solution)/shard_map/own/pallas_call | solution.py:196
  38.8 2.1 %collective-permute-done.2.far_ref = bf16[64,128]{1,0:T(8,128)(2,1)S(1)} collective-permute-done((bf16[64,128]{1,0:T(8,128)(2,1)S(1)}, bf16[64,128]{1,0:T(8,128)(2,1)S(1)}, u32[]{:S(2)}, u32[]{:S(2)}) %collective-permute-start.2) | collective-permute-done | bytes 16416 | tf_op jit(solution)/shard_map/ppermute | solution.py:316
  40.8 0.0 collective-permute-done.3.near_ref
  40.8 0.8 %power.1 = f32[2,512]{1,0:T(2,128)} custom-call(f32[128,512]{1,0:T(8,128)S(1)} %get-tuple-element.13.stress_ref, bf16[64,128]{1,0:T(8,128)(2,1)S(1)} %collective-permute-done.2.far_ref, bf16[64,128]{1,0:T(8,128)(2,1)S(1)} %collective-permute-done.3.near_ref, bf16[256,512]{1,0:T(8,128)(2,1)S(1)} %get-tuple-element.18.rim_ref), custom_call_target="tpu_custom_call" | custom-call | flops 33554432 | bytes 561152 | tf_op jit(solution)/shard_map/power/pallas_call | solution.py:196
  (3 shorter events, 0.1 us)
Async XLA Ops:
  0.0 0.7 %copy-start.7 = (bf16[16,128]{1,0:T(8,128)(2,1)S(1)}, bf16[16,128]{1,0:T(8,128)(2,1)}, u32[]{:S(2)}) copy-start(bf16[16,128]{1,0:T(8,128)(2,1)} %factor_ref.1) | copy-start | bytes 12292
  0.0 0.9 %copy-start.4 = (bf16[16,4096]{1,0:T(8,128)(2,1)S(1)}, bf16[16,4096]{1,0:T(8,128)(2,1)}, u32[]{:S(2)}) copy-start(bf16[16,4096]{1,0:T(8,128)(2,1)} %rows_ref.1) | copy-start | bytes 393220
  0.9 18.3 %copy-start.5 = (f32[4096]{0:T(1024)S(1)}, f32[4096]{0:T(1024)}, u32[]{:S(2)}) copy-start(f32[4096]{0:T(1024)} %param.12) | copy-start | bytes 49156
  0.9 18.3 %copy-start.6 = (f32[4096]{0:T(1024)S(1)}, f32[4096]{0:T(1024)}, u32[]{:S(2)}) copy-start(f32[4096]{0:T(1024)} %param.13) | copy-start | bytes 49156
  0.9 18.3 %copy-start.8 = (f32[2]{0:T(128)S(1)}, f32[2]{0:T(128)}, u32[]{:S(2)}) copy-start(f32[2]{0:T(128)} %param.14) | copy-start | bytes 28
  19.3 12.9 %copy-start = (bf16[512,4096]{1,0:T(8,128)(2,1)S(1)}, bf16[512,4096]{1,0:T(8,128)(2,1)}, u32[]{:S(2)}) copy-start(bf16[512,4096]{1,0:T(8,128)(2,1)} %modes_ref.3) | copy-start | bytes 12582916
  19.3 12.9 %copy-start.3 = (s32[128]{0:T(128)S(1)}, s32[128]{0:T(128)}, u32[]{:S(2)}) copy-start(s32[128]{0:T(128)} %param.15) | copy-start | bytes 1540
  19.6 17.5 %copy-start.1 = (s32[4,512]{1,0:T(4,128)S(1)}, s32[4,512]{1,0:T(4,128)}, u32[]{:S(2)}) copy-start(s32[4,512]{1,0:T(4,128)} %connect_ref.1) | copy-start | bytes 24580
  19.6 17.5 %copy-start.2 = (f32[4,512]{1,0:T(4,128)S(1)}, f32[4,512]{1,0:T(4,128)}, u32[]{:S(2)}) copy-start(f32[4,512]{1,0:T(4,128)} %coef_ref.1) | copy-start | bytes 24580
  31.6 2.0 %collective-permute-start = (bf16[1024,128]{1,0:T(8,128)(2,1)S(1)}, bf16[1024,128]{1,0:T(8,128)(2,1)S(1)}, u32[]{:S(2)}, u32[]{:S(2)}) collective-permute-start(bf16[1024,128]{1,0:T(8,128)(2,1)S(1)} %bitcast.13), channel_id=1, source_target_pairs={{0,1},{1,0},{2,3},{3,2},{4,5},{5,4},{6,7},{7,6},{8,9},{9,8},{10,11... | collective-permute-start | bytes 786440 | tf_op jit(solution)/shard_map/ppermute | solution.py:286
  31.7 1.9 %collective-permute-start.1 = (bf16[1024,128]{1,0:T(8,128)(2,1)S(1)}, bf16[1024,128]{1,0:T(8,128)(2,1)S(1)}, u32[]{:S(2)}, u32[]{:S(2)}) collective-permute-start(bf16[1024,128]{1,0:T(8,128)(2,1)S(1)} %bitcast.12), channel_id=1, source_target_pairs={{0,1},{1,0},{2,3},{3,2},{4,5},{5,4},{6,7},{7,6},{8,9},{9,8},{10,11... | collective-permute-start | bytes 786440 | tf_op jit(solution)/shard_map/ppermute | solution.py:286
  34.0 6.9 %collective-permute-start.2 = (bf16[64,128]{1,0:T(8,128)(2,1)S(1)}, bf16[64,128]{1,0:T(8,128)(2,1)S(1)}, u32[]{:S(2)}, u32[]{:S(2)}) collective-permute-start(bf16[64,128]{1,0:T(8,128)(2,1)S(1)} %get-tuple-element.16), channel_id=1, source_target_pairs={{1,2},{3,4},{5,6},{7,8},{9,10},{11,12},{13,14},{15,16},{17,18},{19... | collective-permute-start | bytes 49160 | tf_op jit(solution)/shard_map/ppermute | solution.py:316
  37.0 3.8 %collective-permute-start.3 = (bf16[64,128]{1,0:T(8,128)(2,1)S(1)}, bf16[64,128]{1,0:T(8,128)(2,1)S(1)}, u32[]{:S(2)}, u32[]{:S(2)}) collective-permute-start(bf16[64,128]{1,0:T(8,128)(2,1)S(1)} %get-tuple-element.17), channel_id=1, source_target_pairs={{0,1},{1,0},{2,3},{3,2},{4,5},{5,4},{6,7},{7,6},{8,9},{9,8},{10,11... | collective-permute-start | bytes 49160 | tf_op jit(solution)/shard_map/ppermute | solution.py:315

commit v11 on v8

--- a/solution.py
+++ b/solution.py
@@ -79,7 +79,7 @@
             imag = summed[line * columns + half : (line + 1) * columns]
             pieces.append(gain_real * real - gain_imag * imag)
             pieces.append(gain_real * imag + gain_imag * real)
-        pseudo = jnp.concatenate(pieces, axis=0).T.astype(BF16)
+        pseudo = jnp.concatenate(pieces, axis=0).astype(BF16).T
         for copy in range(pseudo_ref.shape[0]):
             pseudo_ref[copy, part * width : (part + 1) * width, :] = pseudo
 
@@ -153,7 +153,7 @@
     total = total_ref[...] + jnp.dot(
         modes_ref[:, other], pseudo_ref[...], preferred_element_type=F32
     )
-    table_ref[...] = total.T.astype(BF16)
+    table_ref[...] = total.astype(BF16).T
 
     def matrix(start, tall):
         node = lax.broadcasted_iota(jnp.int32, (tall, elems), 0) + start
@@ -178,12 +178,9 @@
 
 
 def power_kernel(stress_ref, far_ref, near_ref, rim_ref, power_ref):
-    rows = [far_ref[...], near_ref[...]]
-    stress = stress_ref[...] + lax.dot_general(
-        jnp.concatenate(rows + rows, axis=0),
-        rim_ref[...],
-        (((0,), (0,)), ((), ())),
-        preferred_element_type=F32,
+    rows = jnp.concatenate([far_ref[...], near_ref[...]], axis=0).T
+    stress = stress_ref[...] + jnp.dot(
+        jnp.concatenate([rows, rows], axis=1), rim_ref[...], preferred_element_type=F32
     )
     squares = stress * stress
     lines = power_ref.shape[0]

time: 41.7 us -> 41.7 us (level)
  no operation moved by 1% of the time
where the time goes in v11:
time: 41.7 us; the launch traced here: 41.5 us
  blocking collectives  30.2 us (72%)
  Pallas kernels  4.33 us (10%)
  starting transfers between devices  3.2 us (8%)
  waiting for transfers between devices  2.7 us (6%)
  local copies, waits for them, and re-layouts  0.95 us (2%)
    all_to_all x1, blocking collectives, own_pseudo(): got = lax.all_to_all(sent, AXES, 0, 0)  18.3 us
    all_to_all x1, blocking collectives, local(): lax.all_to_all(own_pseudo(*inputs, copies=8), AXES, 0, 0, axis_index_grou...  11.9 us
    pallas_call x7, Pallas kernels, call(): pl.pallas_call(kernel, out_shape=shapes, in_specs=[whole()] * len(operand...  4.33 us
    ppermute x1, starting transfers between devices, local(): far = lax.ppermute(far, AXES, outer)  3.13 us
    ppermute x1, waiting for transfers between devices, local(): far = lax.ppermute(far, AXES, outer)  2.16 us
    unnamed x18, local copies, waits for them, and re-layouts  0.95 us
  transfers between devices with their start and end apart: 3, of which 2 were waited for; matrix products, arithmetic and copies ran while one was open for 0% of the time, Pallas kernels for 7%

profile of v11, /device:TPU:8, one launch (start us, length us, event | category | flops | bytes accessed | tf_op | source)
XLA Modules:
  0.0 41.5 jit_solution(18242734043313311185)
XLA Ops:
  0.0 0.0 copy-start.7
  0.0 0.0 copy-start.4
  0.0 0.7 %copy-done.7 = bf16[16,128]{1,0:T(8,128)(2,1)S(1)} copy-done((bf16[16,128]{1,0:T(8,128)(2,1)S(1)}, bf16[16,128]{1,0:T(8,128)(2,1)}, u32[]{:S(2)}) %copy-start.7) | copy-done | bytes 4120
  0.7 0.2 copy-done.4
  0.9 0.0 copy-start.5
  0.9 0.0 copy-start.6
  0.9 0.0 copy-start.8
  1.0 18.3 %all_to_all.10.got_ref = bf16[32,48,128]{2,1,0:T(8,128)(2,1)S(1)} all-to-all(bf16[32,48,128]{2,1,0:T(8,128)(2,1)S(1)} %pack.1), channel_id=1, replica_groups=mesh['region'=8,'sub'=4] {'region','sub'}, dimensions={0} | all-to-all | bytes 786432 | tf_op jit(solution)/shard_map/all_to_all | solution.py:249
  19.2 0.0 copy-done.5
  19.2 0.0 copy-done.6
  19.3 0.0 copy-done.8
  19.3 0.0 copy-start
  19.3 0.0 copy-start.3
  19.3 0.3 pseudo.1
  19.6 0.0 copy-start.1
  19.6 0.0 copy-start.2
  19.7 11.9 %all_to_all.11 = bf16[8,256,128]{2,1,0:T(8,128)(2,1)S(1)} all-to-all(bf16[8,256,128]{2,1,0:T(8,128)(2,1)S(1)} %pseudo.1), channel_id=1, replica_groups={{0,2,6,4,12,14,10,8},{1,3,7,5,13,15,11,9},{16,18,22,20,28,30,26,24},{17..., dimensions={0} | all-to-all | bytes 1048576 | tf_op jit(solution)/shard_map/all_to_all | solution.py:285
  31.6 0.0 collective-permute-start
  31.6 0.0 copy-done
  31.6 0.0 copy-done.3
  31.6 1.4 %first.1 = (f32[512,128]{1,0:T(8,128)S(1)}, f32[128,128]{1,0:T(8,128)S(1)}, bf16[128,2048]{1,0:T(8,128)(2,1)S(1)}) custom-call(s32[1,128]{1,0:T(1,128)S(1)} %bitcast.7, bf16[512,4096]{1,0:T(8,128)(2,1)S(1)} %copy-done, bf16[2048,128]{1,0:T(8,128)(2,1)S(1)} %bitcast.6), custom_call_target="tpu_custom_call" | custom-call | flops 536870912 | bytes 5571072 | tf_op jit(solution)/shard_map/first/pallas_call | solution.py:199
  33.0 0.5 %collective-permute-done.pseudo_ref = bf16[2048,128]{1,0:T(8,128)(2,1)S(1)} collective-permute-done((bf16[2048,128]{1,0:T(8,128)(2,1)S(1)}, bf16[2048,128]{1,0:T(8,128)(2,1)S(1)}, u32[]{:S(2)}, u32[]{:S(2)}) %collective-permute-start) | collective-permute-done | bytes 524320 | tf_op jit(solution)/shard_map/ppermute | solution.py:287
  33.5 0.3 export.1
  33.8 3.1 %collective-permute-start.1 = (bf16[64,128]{1,0:T(8,128)(2,1)S(1)}, bf16[64,128]{1,0:T(8,128)(2,1)S(1)}, u32[]{:S(2)}, u32[]{:S(2)}) collective-permute-start(bf16[64,128]{1,0:T(8,128)(2,1)S(1)} %get-tuple-element.16), channel_id=1, source_target_pairs={{1,2},{3,4},{5,6},{7,8},{9,10},{11,12},{13,14},{15,16},{17,18},{19... | collective-permute-start | bytes 49160 | tf_op jit(solution)/shard_map/ppermute | solution.py:316
  37.0 0.1 collective-permute-start.2
  37.0 0.0 copy-done.1
  37.1 0.0 copy-done.2
  37.1 1.5 %own.1 = (f32[128,512]{1,0:T(8,128)S(1)}, bf16[256,512]{1,0:T(8,128)(2,1)S(1)}) custom-call(s32[4,512]{1,0:T(4,128)S(1)} %copy-done.1, f32[4,512]{1,0:T(4,128)S(1)} %copy-done.2, bf16[512,4096]{1,0:T(8,128)(2,1)S(1)} %copy-done, bf16[2048,128]{1,0:T(8,128)(2,1)S(1)} %collective-permute-done.pseudo_ref, f32[512,128]{1,0:T(8,128)S(1)} %get-tuple-element.12.total_ref), custom_call_target="tpu_custom_call" | custom-call | flops 402653184 | bytes 5521408 | tf_op jit(solution)/shard_map/own/pallas_call | solution.py:199
  38.5 2.2 %collective-permute-done.1.far_ref = bf16[64,128]{1,0:T(8,128)(2,1)S(1)} collective-permute-done((bf16[64,128]{1,0:T(8,128)(2,1)S(1)}, bf16[64,128]{1,0:T(8,128)(2,1)S(1)}, u32[]{:S(2)}, u32[]{:S(2)}) %collective-permute-start.1) | collective-permute-done | bytes 16416 | tf_op jit(solution)/shard_map/ppermute | solution.py:316
  40.7 0.0 collective-permute-done.2.near_ref
  40.7 0.8 %power.1 = f32[2,512]{1,0:T(2,128)} custom-call(f32[128,512]{1,0:T(8,128)S(1)} %get-tuple-element.13.stress_ref, bf16[64,128]{1,0:T(8,128)(2,1)S(1)} %collective-permute-done.1.far_ref, bf16[64,128]{1,0:T(8,128)(2,1)S(1)} %collective-permute-done.2.near_ref, bf16[256,512]{1,0:T(8,128)(2,1)S(1)} %get-tuple-element.18.rim_ref), custom_call_target="tpu_custom_call" | custom-call | flops 33554432 | bytes 561152 | tf_op jit(solution)/shard_map/power/pallas_call | solution.py:199
  (2 shorter events, 0.0 us)
Async XLA Ops:
  0.0 0.7 %copy-start.7 = (bf16[16,128]{1,0:T(8,128)(2,1)S(1)}, bf16[16,128]{1,0:T(8,128)(2,1)}, u32[]{:S(2)}) copy-start(bf16[16,128]{1,0:T(8,128)(2,1)} %factor_ref.1) | copy-start | bytes 12292
  0.0 0.9 %copy-start.4 = (bf16[16,4096]{1,0:T(8,128)(2,1)S(1)}, bf16[16,4096]{1,0:T(8,128)(2,1)}, u32[]{:S(2)}) copy-start(bf16[16,4096]{1,0:T(8,128)(2,1)} %rows_ref.1) | copy-start | bytes 393220
  0.9 18.3 %copy-start.5 = (f32[4096]{0:T(1024)S(1)}, f32[4096]{0:T(1024)}, u32[]{:S(2)}) copy-start(f32[4096]{0:T(1024)} %param.12) | copy-start | bytes 49156
  0.9 18.3 %copy-start.6 = (f32[4096]{0:T(1024)S(1)}, f32[4096]{0:T(1024)}, u32[]{:S(2)}) copy-start(f32[4096]{0:T(1024)} %param.13) | copy-start | bytes 49156
  0.9 18.3 %copy-start.8 = (f32[2]{0:T(128)S(1)}, f32[2]{0:T(128)}, u32[]{:S(2)}) copy-start(f32[2]{0:T(128)} %param.14) | copy-start | bytes 28
  19.3 12.3 %copy-start = (bf16[512,4096]{1,0:T(8,128)(2,1)S(1)}, bf16[512,4096]{1,0:T(8,128)(2,1)}, u32[]{:S(2)}) copy-start(bf16[512,4096]{1,0:T(8,128)(2,1)} %modes_ref.3) | copy-start | bytes 12582916
  19.3 12.3 %copy-start.3 = (s32[128]{0:T(128)S(1)}, s32[128]{0:T(128)}, u32[]{:S(2)}) copy-start(s32[128]{0:T(128)} %param.15) | copy-start | bytes 1540
  19.6 17.4 %copy-start.1 = (s32[4,512]{1,0:T(4,128)S(1)}, s32[4,512]{1,0:T(4,128)}, u32[]{:S(2)}) copy-start(s32[4,512]{1,0:T(4,128)} %connect_ref.1) | copy-start | bytes 24580
  19.6 17.4 %copy-start.2 = (f32[4,512]{1,0:T(4,128)S(1)}, f32[4,512]{1,0:T(4,128)}, u32[]{:S(2)}) copy-start(f32[4,512]{1,0:T(4,128)} %coef_ref.1) | copy-start | bytes 24580
  31.6 1.9 %collective-permute-start = (bf16[2048,128]{1,0:T(8,128)(2,1)S(1)}, bf16[2048,128]{1,0:T(8,128)(2,1)S(1)}, u32[]{:S(2)}, u32[]{:S(2)}) collective-permute-start(bf16[2048,128]{1,0:T(8,128)(2,1)S(1)} %bitcast.5), channel_id=1, source_target_pairs={{0,1},{1,0},{2,3},{3,2},{4,5},{5,4},{6,7},{7,6},{8,9},{9,8},{10,11... | collective-permute-start | bytes 1572872 | tf_op jit(solution)/shard_map/ppermute | solution.py:287
  33.8 6.9 %collective-permute-start.1 = (bf16[64,128]{1,0:T(8,128)(2,1)S(1)}, bf16[64,128]{1,0:T(8,128)(2,1)S(1)}, u32[]{:S(2)}, u32[]{:S(2)}) collective-permute-start(bf16[64,128]{1,0:T(8,128)(2,1)S(1)} %get-tuple-element.16), channel_id=1, source_target_pairs={{1,2},{3,4},{5,6},{7,8},{9,10},{11,12},{13,14},{15,16},{17,18},{19... | collective-permute-start | bytes 49160 | tf_op jit(solution)/shard_map/ppermute | solution.py:316
  37.0 3.7 %collective-permute-start.2 = (bf16[64,128]{1,0:T(8,128)(2,1)S(1)}, bf16[64,128]{1,0:T(8,128)(2,1)S(1)}, u32[]{:S(2)}, u32[]{:S(2)}) collective-permute-start(bf16[64,128]{1,0:T(8,128)(2,1)S(1)} %get-tuple-element.17), channel_id=1, source_target_pairs={{0,1},{1,0},{2,3},{3,2},{4,5},{5,4},{6,7},{7,6},{8,9},{9,8},{10,11... | collective-permute-start | bytes 49160 | tf_op jit(solution)/shard_map/ppermute | solution.py:315

commit v12 on v8

--- a/solution.py
+++ b/solution.py
@@ -30,7 +30,8 @@
 
 def slab_of(device):
     chip = device // 2 % 8
-    return device % 2 * 8 + (chip ^ (chip // 2) ^ (chip // 4))
+    step = chip % 2 + chip // 4 * 2 + chip // 2 % 2 * 4
+    return device % 2 * 8 + (step ^ (step // 2) ^ (step // 4))
 
 
 def ones_kernel(ones_ref):
@@ -283,7 +284,7 @@
     elems = connectivity.shape[1]
     inputs = (input_rows, input_factor, mode_freq, mode_damping, line_freq)
     if shape == FAST_SHAPE and modes == devices * LANES and input_rows.shape[0] % 16 == 0:
-        cycle = [place ^ (place // 2) for place in range(8)]
+        cycle = [0, 1, 5, 4, 6, 7, 3, 2]
         groups = [[h * 16 + j * 2 + c for j in cycle] for h in range(2) for c in range(2)]
         got = lax.all_to_all(own_pseudo(*inputs, copies=8), AXES, 0, 0, axis_index_groups=groups)
         mine = got.reshape(modes // 2, width)

time: 41.7 us -> 41.7 us (level)
  no operation moved by 1% of the time
where the time goes in v12:
time: 41.7 us; the launch traced here: 41.5 us
  blocking collectives  30.2 us (72%)
  Pallas kernels  4.32 us (10%)
  starting transfers between devices  3.2 us (8%)
  waiting for transfers between devices  2.7 us (6%)
  local copies, waits for them, and re-layouts  0.95 us (2%)
    all_to_all x1, blocking collectives, own_pseudo(): got = lax.all_to_all(sent, AXES, 0, 0)  18.3 us
    all_to_all x1, blocking collectives, local(): lax.all_to_all(own_pseudo(*inputs, copies=8), AXES, 0, 0, axis_index_grou...  11.9 us
    pallas_call x7, Pallas kernels, call(): pl.pallas_call(kernel, out_shape=shapes, in_specs=[whole()] * len(operand...  4.32 us
    ppermute x1, starting transfers between devices, local(): far = lax.ppermute(far, AXES, outer)  3.13 us
    ppermute x1, waiting for transfers between devices, local(): far = lax.ppermute(far, AXES, outer)  2.15 us
    unnamed x18, local copies, waits for them, and re-layouts  0.95 us
  transfers between devices with their start and end apart: 3, of which 2 were waited for; matrix products, arithmetic and copies ran while one was open for 0% of the time, Pallas kernels for 7%

profile of v12, /device:TPU:8, one launch (start us, length us, event | category | flops | bytes accessed | tf_op | source)
XLA Modules:
  0.0 41.5 jit_solution(1009244025507048490)
XLA Ops:
  0.0 0.0 copy-start.7
  0.0 0.0 copy-start.4
  0.0 0.7 %copy-done.7 = bf16[16,128]{1,0:T(8,128)(2,1)S(1)} copy-done((bf16[16,128]{1,0:T(8,128)(2,1)S(1)}, bf16[16,128]{1,0:T(8,128)(2,1)}, u32[]{:S(2)}) %copy-start.7) | copy-done | bytes 4120
  0.7 0.2 copy-done.4
  0.9 0.0 copy-start.5
  0.9 0.0 copy-start.6
  0.9 0.0 copy-start.8
  1.0 18.3 %all_to_all.10.got_ref = bf16[32,48,128]{2,1,0:T(8,128)(2,1)S(1)} all-to-all(bf16[32,48,128]{2,1,0:T(8,128)(2,1)S(1)} %pack.1), channel_id=1, replica_groups=mesh['region'=8,'sub'=4] {'region','sub'}, dimensions={0} | all-to-all | bytes 786432 | tf_op jit(solution)/shard_map/all_to_all | solution.py:253
  19.2 0.0 copy-done.5
  19.2 0.0 copy-done.6
  19.3 0.0 copy-done.8
  19.3 0.0 copy-start
  19.3 0.0 copy-start.3
  19.3 0.3 pseudo.1
  19.6 0.0 copy-start.1
  19.6 0.0 copy-start.2
  19.6 11.9 %all_to_all.11 = bf16[8,256,128]{2,1,0:T(8,128)(2,1)S(1)} all-to-all(bf16[8,256,128]{2,1,0:T(8,128)(2,1)S(1)} %pseudo.1), channel_id=1, replica_groups={{0,2,10,8,12,14,6,4},{1,3,11,9,13,15,7,5},{16,18,26,24,28,30,22,20},{17..., dimensions={0} | all-to-all | bytes 1048576 | tf_op jit(solution)/shard_map/all_to_all | solution.py:289
  31.6 0.0 collective-permute-start
  31.6 0.0 copy-done
  31.6 0.0 copy-done.3
  31.6 1.3 %first.1 = (f32[512,128]{1,0:T(8,128)S(1)}, f32[128,128]{1,0:T(8,128)S(1)}, bf16[128,2048]{1,0:T(8,128)(2,1)S(1)}) custom-call(s32[1,128]{1,0:T(1,128)S(1)} %bitcast.7, bf16[512,4096]{1,0:T(8,128)(2,1)S(1)} %copy-done, bf16[2048,128]{1,0:T(8,128)(2,1)S(1)} %bitcast.6), custom_call_target="tpu_custom_call" | custom-call | flops 536870912 | bytes 5571072 | tf_op jit(solution)/shard_map/first/pallas_call | solution.py:203
  32.9 0.5 %collective-permute-done.pseudo_ref = bf16[2048,128]{1,0:T(8,128)(2,1)S(1)} collective-permute-done((bf16[2048,128]{1,0:T(8,128)(2,1)S(1)}, bf16[2048,128]{1,0:T(8,128)(2,1)S(1)}, u32[]{:S(2)}, u32[]{:S(2)}) %collective-permute-start) | collective-permute-done | bytes 524320 | tf_op jit(solution)/shard_map/ppermute | solution.py:291
  33.5 0.3 export.1
  33.8 3.1 %collective-permute-start.1 = (bf16[64,128]{1,0:T(8,128)(2,1)S(1)}, bf16[64,128]{1,0:T(8,128)(2,1)S(1)}, u32[]{:S(2)}, u32[]{:S(2)}) collective-permute-start(bf16[64,128]{1,0:T(8,128)(2,1)S(1)} %get-tuple-element.16), channel_id=1, source_target_pairs={{1,2},{3,4},{5,6},{7,8},{9,10},{11,12},{13,14},{15,16},{17,18},{19... | collective-permute-start | bytes 49160 | tf_op jit(solution)/shard_map/ppermute | solution.py:320
  36.9 0.1 collective-permute-start.2
  37.0 0.0 copy-done.1
  37.0 0.0 copy-done.2
  37.0 1.5 %own.1 = (f32[128,512]{1,0:T(8,128)S(1)}, bf16[256,512]{1,0:T(8,128)(2,1)S(1)}) custom-call(s32[4,512]{1,0:T(4,128)S(1)} %copy-done.1, f32[4,512]{1,0:T(4,128)S(1)} %copy-done.2, bf16[512,4096]{1,0:T(8,128)(2,1)S(1)} %copy-done, bf16[2048,128]{1,0:T(8,128)(2,1)S(1)} %collective-permute-done.pseudo_ref, f32[512,128]{1,0:T(8,128)S(1)} %get-tuple-element.12.total_ref), custom_call_target="tpu_custom_call" | custom-call | flops 402653184 | bytes 5521408 | tf_op jit(solution)/shard_map/own/pallas_call | solution.py:203
  38.5 2.2 %collective-permute-done.1.far_ref = bf16[64,128]{1,0:T(8,128)(2,1)S(1)} collective-permute-done((bf16[64,128]{1,0:T(8,128)(2,1)S(1)}, bf16[64,128]{1,0:T(8,128)(2,1)S(1)}, u32[]{:S(2)}, u32[]{:S(2)}) %collective-permute-start.1) | collective-permute-done | bytes 16416 | tf_op jit(solution)/shard_map/ppermute | solution.py:320
  40.7 0.0 collective-permute-done.2.near_ref
  40.7 0.8 %power.1 = f32[2,512]{1,0:T(2,128)} custom-call(f32[128,512]{1,0:T(8,128)S(1)} %get-tuple-element.13.stress_ref, bf16[64,128]{1,0:T(8,128)(2,1)S(1)} %collective-permute-done.1.far_ref, bf16[64,128]{1,0:T(8,128)(2,1)S(1)} %collective-permute-done.2.near_ref, bf16[256,512]{1,0:T(8,128)(2,1)S(1)} %get-tuple-element.18.rim_ref), custom_call_target="tpu_custom_call" | custom-call | flops 33554432 | bytes 561152 | tf_op jit(solution)/shard_map/power/pallas_call | solution.py:203
  (2 shorter events, 0.0 us)
Async XLA Ops:
  0.0 0.7 %copy-start.7 = (bf16[16,128]{1,0:T(8,128)(2,1)S(1)}, bf16[16,128]{1,0:T(8,128)(2,1)}, u32[]{:S(2)}) copy-start(bf16[16,128]{1,0:T(8,128)(2,1)} %factor_ref.1) | copy-start | bytes 12292
  0.0 0.9 %copy-start.4 = (bf16[16,4096]{1,0:T(8,128)(2,1)S(1)}, bf16[16,4096]{1,0:T(8,128)(2,1)}, u32[]{:S(2)}) copy-start(bf16[16,4096]{1,0:T(8,128)(2,1)} %rows_ref.1) | copy-start | bytes 393220
  0.9 18.3 %copy-start.5 = (f32[4096]{0:T(1024)S(1)}, f32[4096]{0:T(1024)}, u32[]{:S(2)}) copy-start(f32[4096]{0:T(1024)} %param.12) | copy-start | bytes 49156
  0.9 18.3 %copy-start.6 = (f32[4096]{0:T(1024)S(1)}, f32[4096]{0:T(1024)}, u32[]{:S(2)}) copy-start(f32[4096]{0:T(1024)} %param.13) | copy-start | bytes 49156
  0.9 18.3 %copy-start.8 = (f32[2]{0:T(128)S(1)}, f32[2]{0:T(128)}, u32[]{:S(2)}) copy-start(f32[2]{0:T(128)} %param.14) | copy-start | bytes 28
  19.3 12.3 %copy-start = (bf16[512,4096]{1,0:T(8,128)(2,1)S(1)}, bf16[512,4096]{1,0:T(8,128)(2,1)}, u32[]{:S(2)}) copy-start(bf16[512,4096]{1,0:T(8,128)(2,1)} %modes_ref.3) | copy-start | bytes 12582916
  19.3 12.3 %copy-start.3 = (s32[128]{0:T(128)S(1)}, s32[128]{0:T(128)}, u32[]{:S(2)}) copy-start(s32[128]{0:T(128)} %param.15) | copy-start | bytes 1540
  19.6 17.4 %copy-start.1 = (s32[4,512]{1,0:T(4,128)S(1)}, s32[4,512]{1,0:T(4,128)}, u32[]{:S(2)}) copy-start(s32[4,512]{1,0:T(4,128)} %connect_ref.1) | copy-start | bytes 24580
  19.6 17.4 %copy-start.2 = (f32[4,512]{1,0:T(4,128)S(1)}, f32[4,512]{1,0:T(4,128)}, u32[]{:S(2)}) copy-start(f32[4,512]{1,0:T(4,128)} %coef_ref.1) | copy-start | bytes 24580
  31.6 1.9 %collective-permute-start = (bf16[2048,128]{1,0:T(8,128)(2,1)S(1)}, bf16[2048,128]{1,0:T(8,128)(2,1)S(1)}, u32[]{:S(2)}, u32[]{:S(2)}) collective-permute-start(bf16[2048,128]{1,0:T(8,128)(2,1)S(1)} %bitcast.5), channel_id=1, source_target_pairs={{0,1},{1,0},{2,3},{3,2},{4,5},{5,4},{6,7},{7,6},{8,9},{9,8},{10,11... | collective-permute-start | bytes 1572872 | tf_op jit(solution)/shard_map/ppermute | solution.py:291
  33.8 6.9 %collective-permute-start.1 = (bf16[64,128]{1,0:T(8,128)(2,1)S(1)}, bf16[64,128]{1,0:T(8,128)(2,1)S(1)}, u32[]{:S(2)}, u32[]{:S(2)}) collective-permute-start(bf16[64,128]{1,0:T(8,128)(2,1)S(1)} %get-tuple-element.16), channel_id=1, source_target_pairs={{1,2},{3,4},{5,6},{7,8},{9,10},{11,12},{13,14},{15,16},{17,18},{19... | collective-permute-start | bytes 49160 | tf_op jit(solution)/shard_map/ppermute | solution.py:320
  36.9 3.7 %collective-permute-start.2 = (bf16[64,128]{1,0:T(8,128)(2,1)S(1)}, bf16[64,128]{1,0:T(8,128)(2,1)S(1)}, u32[]{:S(2)}, u32[]{:S(2)}) collective-permute-start(bf16[64,128]{1,0:T(8,128)(2,1)S(1)} %get-tuple-element.17), channel_id=1, source_target_pairs={{0,1},{1,0},{2,3},{3,2},{4,5},{5,4},{6,7},{7,6},{8,9},{9,8},{10,11... | collective-permute-start | bytes 49160 | tf_op jit(solution)/shard_map/ppermute | solution.py:319

commit v13 on v8

--- a/solution.py
+++ b/solution.py
@@ -94,7 +94,12 @@
 def first_kernel(boundary_ref, modes_ref, pseudo_ref, total_ref, part_ref, picked_ref, pick_ref):
     rows = modes_ref.shape[0]
     exports = boundary_ref.shape[1]
-    chosen = jnp.broadcast_to(boundary_ref[...], (exports, exports)).astype(F32).T
+    odd = lax.axis_index(AXES) % 2
+    rim = exports // 2
+    listed = boundary_ref[...]
+    turned = jnp.concatenate([listed[:, rim:], listed[:, :rim]], axis=1)
+    listed = jnp.where(odd == 1, turned, listed)
+    chosen = jnp.broadcast_to(listed, (exports, exports)).astype(F32).T
     column = lax.broadcasted_iota(jnp.int32, (exports, exports), 1).astype(F32)
     pick_ref[...] = jnp.concatenate(
         [(column + start == chosen).astype(F32) for start in range(0, rows, exports)], axis=1
@@ -123,21 +128,12 @@
     for_core(pseudo_ref.shape[0], exported)
 
 
-def export_kernel(part_ref, picked_ref, pseudo_ref, far_ref, near_ref):
-    exports = part_ref.shape[0]
-    cut = pseudo_ref.shape[0] // 2
-    width = pseudo_ref.shape[1]
-    both = jnp.dot(
-        jnp.concatenate([picked_ref[:, :cut], picked_ref[:, cut:]], axis=0),
-        jnp.concatenate([pseudo_ref[:cut], pseudo_ref[cut:]], axis=1),
-        preferred_element_type=F32,
-    )
-    export = part_ref[...] + both[:exports, :width] + both[exports:, width:]
-    export = export.astype(BF16)
-    odd = lax.axis_index(AXES) % 2 == 1
-    rim = far_ref.shape[0]
-    far_ref[...] = jnp.where(odd, export[rim:], export[:rim])
-    near_ref[...] = jnp.where(odd, export[:rim], export[rim:])
+def export_kernel(part_ref, picked_ref, pseudo_ref, export_ref, *, start):
+    here = slice(start, start + export_ref.shape[0])
+    export_ref[...] = (
+        part_ref[here, :]
+        + jnp.dot(picked_ref[here, :], pseudo_ref[...], preferred_element_type=F32)
+    ).astype(BF16)
 
 
 def own_kernel(
@@ -303,14 +299,17 @@
         flops=rows * modes * (width + exports),
         scratch=[pltpu.VMEM((exports, rows), BF16)],
     )
-    far, near = call(
-        export_kernel,
-        "export",
-        [((rim, width), BF16)] * 2,
-        part,
-        picked,
-        theirs,
-        flops=exports * modes * width,
+    far, near = (
+        call(
+            functools.partial(export_kernel, start=start),
+            name,
+            [((rim, width), BF16)],
+            part,
+            picked,
+            theirs,
+            flops=rim * modes * width,
+        )
+        for name, start in (("far", 0), ("near", rim))
     )
     inner = [(i, i ^ 1) for i in range(devices)]
     outer = [(i, i + 1) for i in range(1, devices - 1, 2)]

time: 41.7 us -> 41.6 us (level)
    pallas_call x7 -> x8, Pallas kernels: 4.32 us -> 4.5 us  [call(): pl.pallas_call(kernel, out_shape=shapes, in_specs=[whole()] * len(operand...]
where the time goes in v13:
time: 41.6 us; the launch traced here: 41.4 us
  blocking collectives  30.2 us (73%)
  Pallas kernels  4.5 us (11%)
  starting transfers between devices  3.2 us (8%)
  waiting for transfers between devices  2.41 us (6%)
  local copies, waits for them, and re-layouts  0.95 us (2%)
    all_to_all x1, blocking collectives, own_pseudo(): got = lax.all_to_all(sent, AXES, 0, 0)  18.3 us
    all_to_all x1, blocking collectives, local(): lax.all_to_all(own_pseudo(*inputs, copies=8), AXES, 0, 0, axis_index_grou...  11.9 us
    pallas_call x8, Pallas kernels, call(): pl.pallas_call(kernel, out_shape=shapes, in_specs=[whole()] * len(operand...  4.5 us
    ppermute x1, starting transfers between devices, local(): far = lax.ppermute(far, AXES, outer)  3.13 us
    ppermute x1, waiting for transfers between devices, local(): far = lax.ppermute(far, AXES, outer)  1.94 us
    unnamed x18, local copies, waits for them, and re-layouts  0.95 us
  transfers between devices with their start and end apart: 3, of which 2 were waited for; matrix products, arithmetic and copies ran while one was open for 0% of the time, Pallas kernels for 7%

profile of v13, /device:TPU:8, one launch (start us, length us, event | category | flops | bytes accessed | tf_op | source)
XLA Modules:
  0.0 41.4 jit_solution(15477550261566041736)
XLA Ops:
  0.0 0.0 copy-start.7
  0.0 0.0 copy-start.4
  0.0 0.7 %copy-done.7 = bf16[16,128]{1,0:T(8,128)(2,1)S(1)} copy-done((bf16[16,128]{1,0:T(8,128)(2,1)S(1)}, bf16[16,128]{1,0:T(8,128)(2,1)}, u32[]{:S(2)}) %copy-start.7) | copy-done | bytes 4120
  0.7 0.2 copy-done.4
  0.9 0.0 copy-start.5
  0.9 0.0 copy-start.6
  0.9 0.0 copy-start.8
  1.0 18.3 %all_to_all.10.got_ref = bf16[32,48,128]{2,1,0:T(8,128)(2,1)S(1)} all-to-all(bf16[32,48,128]{2,1,0:T(8,128)(2,1)S(1)} %pack.1), channel_id=1, replica_groups=mesh['region'=8,'sub'=4] {'region','sub'}, dimensions={0} | all-to-all | bytes 786432 | tf_op jit(solution)/shard_map/all_to_all | solution.py:248
  19.2 0.0 copy-done.5
  19.2 0.0 copy-done.6
  19.3 0.0 copy-done.8
  19.3 0.0 copy-start
  19.3 0.0 copy-start.3
  19.3 0.3 pseudo.1
  19.6 0.0 copy-start.1
  19.6 0.0 copy-start.2
  19.6 11.9 %all_to_all.11 = bf16[8,256,128]{2,1,0:T(8,128)(2,1)S(1)} all-to-all(bf16[8,256,128]{2,1,0:T(8,128)(2,1)S(1)} %pseudo.1), channel_id=1, replica_groups={{0,2,6,4,12,14,10,8},{1,3,7,5,13,15,11,9},{16,18,22,20,28,30,26,24},{17..., dimensions={0} | all-to-all | bytes 1048576 | tf_op jit(solution)/shard_map/all_to_all | solution.py:284
  31.6 0.0 collective-permute-start
  31.6 0.0 copy-done
  31.6 0.0 copy-done.3
  31.6 1.4 %first.1 = (f32[512,128]{1,0:T(8,128)S(1)}, f32[128,128]{1,0:T(8,128)S(1)}, bf16[128,2048]{1,0:T(8,128)(2,1)S(1)}) custom-call(s32[1,128]{1,0:T(1,128)S(1)} %bitcast.7, bf16[512,4096]{1,0:T(8,128)(2,1)S(1)} %copy-done, bf16[2048,128]{1,0:T(8,128)(2,1)S(1)} %bitcast.6), custom_call_target="tpu_custom_call" | custom-call | flops 536870912 | bytes 5571072 | tf_op jit(solution)/shard_map/first/pallas_call | solution.py:198
  33.0 0.5 %collective-permute-done.pseudo_ref = bf16[2048,128]{1,0:T(8,128)(2,1)S(1)} collective-permute-done((bf16[2048,128]{1,0:T(8,128)(2,1)S(1)}, bf16[2048,128]{1,0:T(8,128)(2,1)S(1)}, u32[]{:S(2)}, u32[]{:S(2)}) %collective-permute-start) | collective-permute-done | bytes 524320 | tf_op jit(solution)/shard_map/ppermute | solution.py:286
  33.5 0.2 far.1
  33.7 3.1 %collective-permute-start.1 = (bf16[64,128]{1,0:T(8,128)(2,1)S(1)}, bf16[64,128]{1,0:T(8,128)(2,1)S(1)}, u32[]{:S(2)}, u32[]{:S(2)}) collective-permute-start(bf16[64,128]{1,0:T(8,128)(2,1)S(1)} %far.1), channel_id=1, source_target_pairs={{1,2},{3,4},{5,6},{7,8},{9,10},{11,12},{13,14},{15,16},{17,18},{19... | collective-permute-start | bytes 49160 | tf_op jit(solution)/shard_map/ppermute | solution.py:318
  36.9 0.2 near.1
  37.1 0.1 collective-permute-start.2
  37.2 0.0 copy-done.1
  37.2 0.0 copy-done.2
  37.2 1.5 %own.1 = (f32[128,512]{1,0:T(8,128)S(1)}, bf16[256,512]{1,0:T(8,128)(2,1)S(1)}) custom-call(s32[4,512]{1,0:T(4,128)S(1)} %copy-done.1, f32[4,512]{1,0:T(4,128)S(1)} %copy-done.2, bf16[512,4096]{1,0:T(8,128)(2,1)S(1)} %copy-done, bf16[2048,128]{1,0:T(8,128)(2,1)S(1)} %collective-permute-done.pseudo_ref, f32[512,128]{1,0:T(8,128)S(1)} %get-tuple-element.10.total_ref), custom_call_target="tpu_custom_call" | custom-call | flops 402653184 | bytes 5521408 | tf_op jit(solution)/shard_map/own/pallas_call | solution.py:198
  38.6 1.9 %collective-permute-done.1.far_ref = bf16[64,128]{1,0:T(8,128)(2,1)S(1)} collective-permute-done((bf16[64,128]{1,0:T(8,128)(2,1)S(1)}, bf16[64,128]{1,0:T(8,128)(2,1)S(1)}, u32[]{:S(2)}, u32[]{:S(2)}) %collective-permute-start.1) | collective-permute-done | bytes 16416 | tf_op jit(solution)/shard_map/ppermute | solution.py:318
  40.6 0.0 collective-permute-done.2.near_ref
  40.6 0.8 %power.1 = f32[2,512]{1,0:T(2,128)} custom-call(f32[128,512]{1,0:T(8,128)S(1)} %get-tuple-element.11.stress_ref, bf16[64,128]{1,0:T(8,128)(2,1)S(1)} %collective-permute-done.1.far_ref, bf16[64,128]{1,0:T(8,128)(2,1)S(1)} %collective-permute-done.2.near_ref, bf16[256,512]{1,0:T(8,128)(2,1)S(1)} %get-tuple-element.14.rim_ref), custom_call_target="tpu_custom_call" | custom-call | flops 33554432 | bytes 561152 | tf_op jit(solution)/shard_map/power/pallas_call | solution.py:198
  (2 shorter events, 0.0 us)
Async XLA Ops:
  0.0 0.7 %copy-start.7 = (bf16[16,128]{1,0:T(8,128)(2,1)S(1)}, bf16[16,128]{1,0:T(8,128)(2,1)}, u32[]{:S(2)}) copy-start(bf16[16,128]{1,0:T(8,128)(2,1)} %factor_ref.1) | copy-start | bytes 12292
  0.0 0.9 %copy-start.4 = (bf16[16,4096]{1,0:T(8,128)(2,1)S(1)}, bf16[16,4096]{1,0:T(8,128)(2,1)}, u32[]{:S(2)}) copy-start(bf16[16,4096]{1,0:T(8,128)(2,1)} %rows_ref.1) | copy-start | bytes 393220
  0.9 18.3 %copy-start.5 = (f32[4096]{0:T(1024)S(1)}, f32[4096]{0:T(1024)}, u32[]{:S(2)}) copy-start(f32[4096]{0:T(1024)} %param.12) | copy-start | bytes 49156
  0.9 18.3 %copy-start.6 = (f32[4096]{0:T(1024)S(1)}, f32[4096]{0:T(1024)}, u32[]{:S(2)}) copy-start(f32[4096]{0:T(1024)} %param.13) | copy-start | bytes 49156
  0.9 18.3 %copy-start.8 = (f32[2]{0:T(128)S(1)}, f32[2]{0:T(128)}, u32[]{:S(2)}) copy-start(f32[2]{0:T(128)} %param.14) | copy-start | bytes 28
  19.3 12.3 %copy-start = (bf16[512,4096]{1,0:T(8,128)(2,1)S(1)}, bf16[512,4096]{1,0:T(8,128)(2,1)}, u32[]{:S(2)}) copy-start(bf16[512,4096]{1,0:T(8,128)(2,1)} %modes_ref.3) | copy-start | bytes 12582916
  19.3 12.3 %copy-start.3 = (s32[128]{0:T(128)S(1)}, s32[128]{0:T(128)}, u32[]{:S(2)}) copy-start(s32[128]{0:T(128)} %param.15) | copy-start | bytes 1540
  19.6 17.5 %copy-start.1 = (s32[4,512]{1,0:T(4,128)S(1)}, s32[4,512]{1,0:T(4,128)}, u32[]{:S(2)}) copy-start(s32[4,512]{1,0:T(4,128)} %connect_ref.1) | copy-start | bytes 24580
  19.6 17.5 %copy-start.2 = (f32[4,512]{1,0:T(4,128)S(1)}, f32[4,512]{1,0:T(4,128)}, u32[]{:S(2)}) copy-start(f32[4,512]{1,0:T(4,128)} %coef_ref.1) | copy-start | bytes 24580
  31.6 1.9 %collective-permute-start = (bf16[2048,128]{1,0:T(8,128)(2,1)S(1)}, bf16[2048,128]{1,0:T(8,128)(2,1)S(1)}, u32[]{:S(2)}, u32[]{:S(2)}) collective-permute-start(bf16[2048,128]{1,0:T(8,128)(2,1)S(1)} %bitcast.5), channel_id=1, source_target_pairs={{0,1},{1,0},{2,3},{3,2},{4,5},{5,4},{6,7},{7,6},{8,9},{9,8},{10,11... | collective-permute-start | bytes 1572872 | tf_op jit(solution)/shard_map/ppermute | solution.py:286
  33.7 6.9 %collective-permute-start.1 = (bf16[64,128]{1,0:T(8,128)(2,1)S(1)}, bf16[64,128]{1,0:T(8,128)(2,1)S(1)}, u32[]{:S(2)}, u32[]{:S(2)}) collective-permute-start(bf16[64,128]{1,0:T(8,128)(2,1)S(1)} %far.1), channel_id=1, source_target_pairs={{1,2},{3,4},{5,6},{7,8},{9,10},{11,12},{13,14},{15,16},{17,18},{19... | collective-permute-start | bytes 49160 | tf_op jit(solution)/shard_map/ppermute | solution.py:318
  37.1 3.5 %collective-permute-start.2 = (bf16[64,128]{1,0:T(8,128)(2,1)S(1)}, bf16[64,128]{1,0:T(8,128)(2,1)S(1)}, u32[]{:S(2)}, u32[]{:S(2)}) collective-permute-start(bf16[64,128]{1,0:T(8,128)(2,1)S(1)} %near.1), channel_id=1, source_target_pairs={{0,1},{1,0},{2,3},{3,2},{4,5},{5,4},{6,7},{7,6},{8,9},{9,8},{10,11... | collective-permute-start | bytes 49160 | tf_op jit(solution)/shard_map/ppermute | solution.py:317

commit v14 on v13

--- a/solution.py
+++ b/solution.py
@@ -91,7 +91,21 @@
     pl.when(odd == 1)(lambda: work(high, low))
 
 
-def first_kernel(boundary_ref, modes_ref, pseudo_ref, total_ref, part_ref, picked_ref, pick_ref):
+def stress_matrix(connect_ref, coef_ref, start, tall):
+    elems = connect_ref.shape[1]
+    node = lax.broadcasted_iota(jnp.int32, (tall, elems), 0) + start
+    total = jnp.zeros((tall, elems), F32)
+    for corner in range(connect_ref.shape[0]):
+        hit = node == connect_ref[corner : corner + 1, :]
+        total = total + jnp.where(hit, coef_ref[corner : corner + 1, :], 0.0)
+    high = total.astype(BF16)
+    return high, (total - high.astype(F32)).astype(BF16)
+
+
+def first_kernel(
+    boundary_ref, connect_ref, coef_ref, modes_ref, pseudo_ref,
+    total_ref, part_ref, picked_ref, early_ref, pick_ref,
+):
     rows = modes_ref.shape[0]
     exports = boundary_ref.shape[1]
     odd = lax.axis_index(AXES) % 2
@@ -127,6 +141,14 @@
     for_core(pseudo_ref.shape[0], product)
     for_core(pseudo_ref.shape[0], exported)
 
+    @pl.when(odd == 0)
+    def _():
+        for start in range(0, early_ref.shape[1], rim):
+            here = slice(start, start + rim)
+            early_ref[0, here, :], early_ref[1, here, :] = stress_matrix(
+                connect_ref, coef_ref, start + rim, rim
+            )
+
 
 def export_kernel(part_ref, picked_ref, pseudo_ref, export_ref, *, start):
     here = slice(start, start + export_ref.shape[0])
@@ -137,13 +159,13 @@
 
 
 def own_kernel(
-    connect_ref, coef_ref, modes_ref, pseudo_ref, total_ref, stress_ref, rim_ref, own_ref, table_ref
+    connect_ref, coef_ref, modes_ref, pseudo_ref, total_ref, early_ref,
+    stress_ref, rim_ref, own_ref, table_ref,
 ):
     rows = modes_ref.shape[0]
-    elems = connect_ref.shape[1]
     rim = rim_ref.shape[0] // 4
+    early = early_ref.shape[1]
     odd = lax.axis_index(AXES) % 2
-
     depth = pseudo_ref.shape[0]
     other = pl.ds(pl.multiple_of((1 - odd) * depth, depth), depth)
     total = total_ref[...] + jnp.dot(
@@ -151,26 +173,40 @@
     )
     table_ref[...] = total.T.astype(BF16)
 
-    def matrix(start, tall):
-        node = lax.broadcasted_iota(jnp.int32, (tall, elems), 0) + start
-        total = jnp.zeros((tall, elems), F32)
-        for corner in range(connect_ref.shape[0]):
-            hit = node == connect_ref[corner : corner + 1, :]
-            total = total + jnp.where(hit, coef_ref[corner : corner + 1, :], 0.0)
-        high = total.astype(BF16)
-        return high, (total - high.astype(F32)).astype(BF16)
+    def build(first, last):
+        for start in range(first, last, rim):
+            here = slice(start, start + rim)
+            own_ref[0, here, :], own_ref[1, here, :] = stress_matrix(
+                connect_ref, coef_ref, start + rim, rim
+            )
 
     after = rim + rows
     for place, start in ((0, after * odd), (1, after * (1 - odd))):
-        high, low = matrix(start, rim)
+        high, low = stress_matrix(connect_ref, coef_ref, start, rim)
         rim_ref[place * rim : (place + 1) * rim, :] = high
         rim_ref[(place + 2) * rim : (place + 3) * rim, :] = low
-    for start in range(0, rows, rim):
-        here = slice(start, start + rim)
-        own_ref[0, here, :], own_ref[1, here, :] = matrix(start + rim, rim)
-    table = table_ref[...]
-    stress = jnp.dot(table, own_ref[0], preferred_element_type=F32)
-    stress_ref[...] = stress + jnp.dot(table, own_ref[1], preferred_element_type=F32)
+    build(early, rows)
+    table = table_ref[:, early:]
+    stress = jnp.dot(table, own_ref[0, early:, :], preferred_element_type=F32)
+    stress_ref[...] = stress + jnp.dot(
+        table, own_ref[1, early:, :], preferred_element_type=F32
+    )
+
+    def rest(matrix_ref):
+        table = table_ref[:, :early]
+        stress = jnp.dot(table, matrix_ref[0, :early, :], preferred_element_type=F32)
+        stress_ref[...] += stress + jnp.dot(
+            table, matrix_ref[1, :early, :], preferred_element_type=F32
+        )
+
+    @pl.when(odd == 0)
+    def _():
+        rest(early_ref)
+
+    @pl.when(odd == 1)
+    def _():
+        build(0, early)
+        rest(own_ref)
 
 
 def power_kernel(stress_ref, far_ref, near_ref, rim_ref, power_ref):
@@ -289,11 +325,18 @@
         core = lax.axis_index(AXES) % 2
         mine = lax.dynamic_index_in_dim(pseudo, core, 0, keepdims=False)
         theirs = lax.dynamic_index_in_dim(pseudo, 1 - core, 0, keepdims=False)
-    total, part, picked = call(
+    total, part, picked, early = call(
         first_kernel,
         "first",
-        [((rows, width), F32), ((exports, width), F32), ((exports, modes // 2), BF16)],
+        [
+            ((rows, width), F32),
+            ((exports, width), F32),
+            ((exports, modes // 2), BF16),
+            ((2, rows * 3 // 4, elems), BF16),
+        ],
         boundary_rows.reshape(1, exports),
+        connectivity,
+        stress_coef,
         mode_rows,
         mine,
         flops=rows * modes * (width + exports),
@@ -325,6 +368,7 @@
         mode_rows,
         theirs,
         total,
+        early,
         flops=rows * modes * width + 4 * rows * elems * width,
         scratch=[pltpu.VMEM((2, rows, elems), BF16), pltpu.VMEM((width, rows), BF16)],
     )

time: 41.6 us -> 41.6 us (level)
  transfers between devices with their start and end apart: 3 -> 3, of which waited for: 2 -> 2; matrix products, arithmetic and copies ran while one was open for 0% -> 0% of each run, Pallas kernels for 7% -> 8%
where the time goes in v14:
time: 41.6 us; the launch traced here: 41.4 us
  blocking collectives  30.2 us (73%)
  Pallas kernels  4.82 us (12%)
  starting transfers between devices  3.2 us (8%)
  waiting for transfers between devices  2.1 us (5%)
  local copies, waits for them, and re-layouts  0.95 us (2%)
    all_to_all x1, blocking collectives, own_pseudo(): got = lax.all_to_all(sent, AXES, 0, 0)  18.3 us
    all_to_all x1, blocking collectives, local(): lax.all_to_all(own_pseudo(*inputs, copies=8), AXES, 0, 0, axis_index_grou...  11.9 us
    pallas_call x8, Pallas kernels, call(): pl.pallas_call(kernel, out_shape=shapes, in_specs=[whole()] * len(operand...  4.82 us
    ppermute x1, starting transfers between devices, local(): far = lax.ppermute(far, AXES, outer)  3.13 us
    ppermute x1, waiting for transfers between devices, local(): far = lax.ppermute(far, AXES, outer)  2.04 us
    unnamed x18, local copies, waits for them, and re-layouts  0.95 us
  transfers between devices with their start and end apart: 3, of which 2 were waited for; matrix products, arithmetic and copies ran while one was open for 0% of the time, Pallas kernels for 8%

profile of v14, /device:TPU:8, one launch (start us, length us, event | category | flops | bytes accessed | tf_op | source)
XLA Modules:
  0.0 41.4 jit_solution(5343451042191701337)
XLA Ops:
  0.0 0.0 copy-start.7
  0.0 0.0 copy-start.4
  0.0 0.7 %copy-done.7 = bf16[16,128]{1,0:T(8,128)(2,1)S(1)} copy-done((bf16[16,128]{1,0:T(8,128)(2,1)S(1)}, bf16[16,128]{1,0:T(8,128)(2,1)}, u32[]{:S(2)}) %copy-start.7) | copy-done | bytes 4120
  0.7 0.2 copy-done.4
  0.9 0.0 copy-start.5
  0.9 0.0 copy-start.6
  0.9 0.0 copy-start.8
  1.0 18.3 %all_to_all.10.got_ref = bf16[32,48,128]{2,1,0:T(8,128)(2,1)S(1)} all-to-all(bf16[32,48,128]{2,1,0:T(8,128)(2,1)S(1)} %pack.1), channel_id=1, replica_groups=mesh['region'=8,'sub'=4] {'region','sub'}, dimensions={0} | all-to-all | bytes 786432 | tf_op jit(solution)/shard_map/all_to_all | solution.py:284
  19.2 0.0 copy-done.5
  19.2 0.0 copy-done.6
  19.3 0.0 copy-done.8
  19.3 0.0 copy-start
  19.3 0.0 copy-start.1
  19.3 0.0 copy-start.2
  19.3 0.0 copy-start.3
  19.3 0.3 pseudo.1
  19.6 11.9 %all_to_all.11 = bf16[8,256,128]{2,1,0:T(8,128)(2,1)S(1)} all-to-all(bf16[8,256,128]{2,1,0:T(8,128)(2,1)S(1)} %pseudo.1), channel_id=1, replica_groups={{0,2,6,4,12,14,10,8},{1,3,7,5,13,15,11,9},{16,18,22,20,28,30,26,24},{17..., dimensions={0} | all-to-all | bytes 1048576 | tf_op jit(solution)/shard_map/all_to_all | solution.py:320
  31.6 0.0 collective-permute-start
  31.6 0.0 copy-done
  31.6 0.0 copy-done.1
  31.6 0.0 copy-done.2
  31.6 0.0 copy-done.3
  31.6 1.8 %first.1 = (f32[512,128]{1,0:T(8,128)S(1)}, f32[128,128]{1,0:T(8,128)S(1)}, bf16[128,2048]{1,0:T(8,128)(2,1)S(1)}, bf16[2,384,512]{2,1,0:T(8,128)(2,1)S(1)}) custom-call(s32[1,128]{1,0:T(1,128)S(1)} %bitcast.7, s32[4,512]{1,0:T(4,128)S(1)} %copy-done.1, f32[4,512]{1,0:T(4,128)S(1)} %copy-done.2, bf16[512,4096]{1,0:T(8,128)(2,1)S(1)} %copy-done, ...), custom_call_target="tpu_custom_call" | custom-call | flops 536870912 | bytes 6373888 | tf_op jit(solution)/shard_map/first/pallas_call | solution.py:234
  33.4 0.1 collective-permute-done.pseudo_ref
  33.5 0.2 far.1
  33.7 3.1 %collective-permute-start.1 = (bf16[64,128]{1,0:T(8,128)(2,1)S(1)}, bf16[64,128]{1,0:T(8,128)(2,1)S(1)}, u32[]{:S(2)}, u32[]{:S(2)}) collective-permute-start(bf16[64,128]{1,0:T(8,128)(2,1)S(1)} %far.1), channel_id=1, source_target_pairs={{1,2},{3,4},{5,6},{7,8},{9,10},{11,12},{13,14},{15,16},{17,18},{19... | collective-permute-start | bytes 49160 | tf_op jit(solution)/shard_map/ppermute | solution.py:361
  36.9 0.2 near.1
  37.1 0.1 collective-permute-start.2
  37.2 1.4 %own.1 = (f32[128,512]{1,0:T(8,128)S(1)}, bf16[256,512]{1,0:T(8,128)(2,1)S(1)}) custom-call(s32[4,512]{1,0:T(4,128)S(1)} %copy-done.1, f32[4,512]{1,0:T(4,128)S(1)} %copy-done.2, bf16[512,4096]{1,0:T(8,128)(2,1)S(1)} %copy-done, bf16[2048,128]{1,0:T(8,128)(2,1)S(1)} %collective-permute-done.pseudo_ref, f32[512,128]{1,0:T(8,128)S(1)} %get-tuple-element.11.total_ref, ...), custom_call_target="tpu_custom_call" | custom-call | flops 402653184 | bytes 6307840 | tf_op jit(solution)/shard_map/own/pallas_call | solution.py:234
  38.5 2.0 %collective-permute-done.1.far_ref = bf16[64,128]{1,0:T(8,128)(2,1)S(1)} collective-permute-done((bf16[64,128]{1,0:T(8,128)(2,1)S(1)}, bf16[64,128]{1,0:T(8,128)(2,1)S(1)}, u32[]{:S(2)}, u32[]{:S(2)}) %collective-permute-start.1) | collective-permute-done | bytes 16416 | tf_op jit(solution)/shard_map/ppermute | solution.py:361
  40.6 0.0 collective-permute-done.2.near_ref
  40.6 0.8 %power.1 = f32[2,512]{1,0:T(2,128)} custom-call(f32[128,512]{1,0:T(8,128)S(1)} %get-tuple-element.13.stress_ref, bf16[64,128]{1,0:T(8,128)(2,1)S(1)} %collective-permute-done.1.far_ref, bf16[64,128]{1,0:T(8,128)(2,1)S(1)} %collective-permute-done.2.near_ref, bf16[256,512]{1,0:T(8,128)(2,1)S(1)} %get-tuple-element.16.rim_ref), custom_call_target="tpu_custom_call" | custom-call | flops 33554432 | bytes 561152 | tf_op jit(solution)/shard_map/power/pallas_call | solution.py:234
  (2 shorter events, 0.0 us)
Async XLA Ops:
  0.0 0.7 %copy-start.7 = (bf16[16,128]{1,0:T(8,128)(2,1)S(1)}, bf16[16,128]{1,0:T(8,128)(2,1)}, u32[]{:S(2)}) copy-start(bf16[16,128]{1,0:T(8,128)(2,1)} %factor_ref.1) | copy-start | bytes 12292
  0.0 0.9 %copy-start.4 = (bf16[16,4096]{1,0:T(8,128)(2,1)S(1)}, bf16[16,4096]{1,0:T(8,128)(2,1)}, u32[]{:S(2)}) copy-start(bf16[16,4096]{1,0:T(8,128)(2,1)} %rows_ref.1) | copy-start | bytes 393220
  0.9 18.3 %copy-start.5 = (f32[4096]{0:T(1024)S(1)}, f32[4096]{0:T(1024)}, u32[]{:S(2)}) copy-start(f32[4096]{0:T(1024)} %param.12) | copy-start | bytes 49156
  0.9 18.3 %copy-start.6 = (f32[4096]{0:T(1024)S(1)}, f32[4096]{0:T(1024)}, u32[]{:S(2)}) copy-start(f32[4096]{0:T(1024)} %param.13) | copy-start | bytes 49156
  0.9 18.3 %copy-start.8 = (f32[2]{0:T(128)S(1)}, f32[2]{0:T(128)}, u32[]{:S(2)}) copy-start(f32[2]{0:T(128)} %param.14) | copy-start | bytes 28
  19.3 12.3 %copy-start = (bf16[512,4096]{1,0:T(8,128)(2,1)S(1)}, bf16[512,4096]{1,0:T(8,128)(2,1)}, u32[]{:S(2)}) copy-start(bf16[512,4096]{1,0:T(8,128)(2,1)} %modes_ref.3) | copy-start | bytes 12582916
  19.3 12.3 %copy-start.1 = (s32[4,512]{1,0:T(4,128)S(1)}, s32[4,512]{1,0:T(4,128)}, u32[]{:S(2)}) copy-start(s32[4,512]{1,0:T(4,128)} %connect_ref.3) | copy-start | bytes 24580
  19.3 12.3 %copy-start.2 = (f32[4,512]{1,0:T(4,128)S(1)}, f32[4,512]{1,0:T(4,128)}, u32[]{:S(2)}) copy-start(f32[4,512]{1,0:T(4,128)} %coef_ref.3) | copy-start | bytes 24580
  19.3 12.3 %copy-start.3 = (s32[128]{0:T(128)S(1)}, s32[128]{0:T(128)}, u32[]{:S(2)}) copy-start(s32[128]{0:T(128)} %param.15) | copy-start | bytes 1540
  31.6 1.9 %collective-permute-start = (bf16[2048,128]{1,0:T(8,128)(2,1)S(1)}, bf16[2048,128]{1,0:T(8,128)(2,1)S(1)}, u32[]{:S(2)}, u32[]{:S(2)}) collective-permute-start(bf16[2048,128]{1,0:T(8,128)(2,1)S(1)} %bitcast.5), channel_id=1, source_target_pairs={{0,1},{1,0},{2,3},{3,2},{4,5},{5,4},{6,7},{7,6},{8,9},{9,8},{10,11... | collective-permute-start | bytes 1572872 | tf_op jit(solution)/shard_map/ppermute | solution.py:322
  33.7 6.9 %collective-permute-start.1 = (bf16[64,128]{1,0:T(8,128)(2,1)S(1)}, bf16[64,128]{1,0:T(8,128)(2,1)S(1)}, u32[]{:S(2)}, u32[]{:S(2)}) collective-permute-start(bf16[64,128]{1,0:T(8,128)(2,1)S(1)} %far.1), channel_id=1, source_target_pairs={{1,2},{3,4},{5,6},{7,8},{9,10},{11,12},{13,14},{15,16},{17,18},{19... | collective-permute-start | bytes 49160 | tf_op jit(solution)/shard_map/ppermute | solution.py:361
  37.1 3.5 %collective-permute-start.2 = (bf16[64,128]{1,0:T(8,128)(2,1)S(1)}, bf16[64,128]{1,0:T(8,128)(2,1)S(1)}, u32[]{:S(2)}, u32[]{:S(2)}) collective-permute-start(bf16[64,128]{1,0:T(8,128)(2,1)S(1)} %near.1), channel_id=1, source_target_pairs={{0,1},{1,0},{2,3},{3,2},{4,5},{5,4},{6,7},{7,6},{8,9},{9,8},{10,11... | collective-permute-start | bytes 49160 | tf_op jit(solution)/shard_map/ppermute | solution.py:360

commit v15 on v13

--- a/solution.py
+++ b/solution.py
@@ -49,7 +49,9 @@
         sent_ref[device, parts * rows :, :] = factor
 
 
-def pseudo_kernel(line_ref, freq_ref, damping_ref, got_ref, pseudo_ref, *, rows):
+def pseudo_kernel(
+    boundary_ref, line_ref, freq_ref, damping_ref, got_ref, pseudo_ref, pick_ref, *, rows
+):
     devices, tall, width = got_ref.shape
     parts = tall // rows - 1
     lines = line_ref.shape[1]
@@ -82,6 +84,16 @@
         pseudo = jnp.concatenate(pieces, axis=0).T.astype(BF16)
         for copy in range(pseudo_ref.shape[0]):
             pseudo_ref[copy, part * width : (part + 1) * width, :] = pseudo
+    exports, owned = pick_ref.shape
+    rim = exports // 2
+    listed = boundary_ref[...]
+    turned = jnp.concatenate([listed[:, rim:], listed[:, :rim]], axis=1)
+    listed = jnp.where(lax.axis_index(AXES) % 2 == 1, turned, listed)
+    chosen = jnp.broadcast_to(listed, (exports, exports)).astype(F32).T
+    column = lax.broadcasted_iota(jnp.int32, (exports, exports), 1).astype(F32)
+    for start in range(0, owned, exports):
+        pick = (column + start == chosen).astype(F32).astype(BF16)
+        pick_ref[:, start : start + exports] = pick
 
 
 def for_core(depth, work):
@@ -91,22 +103,11 @@
     pl.when(odd == 1)(lambda: work(high, low))
 
 
-def first_kernel(boundary_ref, modes_ref, pseudo_ref, total_ref, part_ref, picked_ref, pick_ref):
-    rows = modes_ref.shape[0]
-    exports = boundary_ref.shape[1]
+def first_kernel(pick_ref, modes_ref, pseudo_ref, total_ref, part_ref, picked_ref):
+    depth = pseudo_ref.shape[0]
     odd = lax.axis_index(AXES) % 2
-    rim = exports // 2
-    listed = boundary_ref[...]
-    turned = jnp.concatenate([listed[:, rim:], listed[:, :rim]], axis=1)
-    listed = jnp.where(odd == 1, turned, listed)
-    chosen = jnp.broadcast_to(listed, (exports, exports)).astype(F32).T
-    column = lax.broadcasted_iota(jnp.int32, (exports, exports), 1).astype(F32)
-    pick_ref[...] = jnp.concatenate(
-        [(column + start == chosen).astype(F32) for start in range(0, rows, exports)], axis=1
-    ).astype(BF16)
-
-    def product(mine, _):
-        total_ref[...] = jnp.dot(modes_ref[:, mine], pseudo_ref[...], preferred_element_type=F32)
+    mine = pl.ds(pl.multiple_of(odd * depth, depth), depth)
+    total_ref[...] = jnp.dot(modes_ref[:, mine], pseudo_ref[...], preferred_element_type=F32)
 
     def exported(_, other):
         pick = pick_ref[...]
@@ -124,31 +125,34 @@
             pick, modes_ref[:, other], preferred_element_type=F32
         ).astype(BF16)
 
-    for_core(pseudo_ref.shape[0], product)
-    for_core(pseudo_ref.shape[0], exported)
-
-
-def export_kernel(part_ref, picked_ref, pseudo_ref, export_ref, *, start):
+    for_core(depth, exported)
+
+
+def export_kernel(part_ref, picked_ref, low_ref, high_ref, export_ref, *, start):
     here = slice(start, start + export_ref.shape[0])
+    cut = low_ref.shape[0]
+    export = part_ref[here, :] + jnp.dot(
+        picked_ref[here, :cut], low_ref[...], preferred_element_type=F32
+    )
     export_ref[...] = (
-        part_ref[here, :]
-        + jnp.dot(picked_ref[here, :], pseudo_ref[...], preferred_element_type=F32)
+        export + jnp.dot(picked_ref[here, cut:], high_ref[...], preferred_element_type=F32)
     ).astype(BF16)
 
 
 def own_kernel(
-    connect_ref, coef_ref, modes_ref, pseudo_ref, total_ref, stress_ref, rim_ref, own_ref, table_ref
+    connect_ref, coef_ref, modes_ref, low_ref, high_ref, total_ref,
+    stress_ref, rim_ref, own_ref, table_ref,
 ):
     rows = modes_ref.shape[0]
     elems = connect_ref.shape[1]
     rim = rim_ref.shape[0] // 4
     odd = lax.axis_index(AXES) % 2
 
-    depth = pseudo_ref.shape[0]
-    other = pl.ds(pl.multiple_of((1 - odd) * depth, depth), depth)
-    total = total_ref[...] + jnp.dot(
-        modes_ref[:, other], pseudo_ref[...], preferred_element_type=F32
-    )
+    cut = low_ref.shape[0]
+    total = total_ref[...]
+    for part, part_ref in enumerate((low_ref, high_ref)):
+        here = pl.ds(pl.multiple_of((2 * (1 - odd) + part) * cut, cut), cut)
+        total = total + jnp.dot(modes_ref[:, here], part_ref[...], preferred_element_type=F32)
     table_ref[...] = total.T.astype(BF16)
 
     def matrix(start, tall):
@@ -229,7 +233,9 @@
     return jnp.concatenate(pieces, axis=1).astype(BF16)
 
 
-def own_pseudo(input_rows, input_factor, mode_freq, mode_damping, line_freq, copies):
+def own_pseudo(
+    input_rows, input_factor, mode_freq, mode_damping, line_freq, boundary_rows, owned, copies
+):
     devices = math.prod(FAST_SHAPE)
     rows, modes = input_rows.shape
     width = input_factor.shape[1]
@@ -249,7 +255,8 @@
     return call(
         functools.partial(pseudo_kernel, rows=rows),
         "pseudo",
-        [((copies, parts * width, width), BF16)],
+        [((copies, parts * width, width), BF16), ((boundary_rows.shape[0], owned), BF16)],
+        boundary_rows.reshape(1, -1),
         line_freq.reshape(1, lines),
         mode_freq.reshape(-1, width),
         mode_damping.reshape(-1, width),
@@ -281,23 +288,28 @@
     if shape == FAST_SHAPE and modes == devices * LANES and input_rows.shape[0] % 16 == 0:
         cycle = [place ^ (place // 2) for place in range(8)]
         groups = [[h * 16 + j * 2 + c for j in cycle] for h in range(2) for c in range(2)]
-        got = lax.all_to_all(own_pseudo(*inputs, copies=8), AXES, 0, 0, axis_index_groups=groups)
+        block, pick = own_pseudo(*inputs, boundary_rows, rows, copies=8)
+        got = lax.all_to_all(block, AXES, 0, 0, axis_index_groups=groups)
         mine = got.reshape(modes // 2, width)
-        theirs = lax.ppermute(mine, AXES, [(i, i ^ 1) for i in range(devices)])
+        cut = modes // 4
+        swap = [(i, i ^ 1) for i in range(devices)]
+        theirs = [lax.ppermute(part, AXES, swap) for part in (mine[:cut], mine[cut:])]
     else:
         pseudo = pseudo_by_sum(*inputs).reshape(2, modes // 2, width)
         core = lax.axis_index(AXES) % 2
+        listed = jnp.where(core == 1, jnp.roll(boundary_rows, rim), boundary_rows)
+        pick = (listed[:, None] == jnp.arange(rows)[None, :]).astype(BF16)
         mine = lax.dynamic_index_in_dim(pseudo, core, 0, keepdims=False)
-        theirs = lax.dynamic_index_in_dim(pseudo, 1 - core, 0, keepdims=False)
+        other = lax.dynamic_index_in_dim(pseudo, 1 - core, 0, keepdims=False)
+        theirs = [other[: modes // 4], other[modes // 4 :]]
     total, part, picked = call(
         first_kernel,
         "first",
         [((rows, width), F32), ((exports, width), F32), ((exports, modes // 2), BF16)],
-        boundary_rows.reshape(1, exports),
+        pick,
         mode_rows,
         mine,
         flops=rows * modes * (width + exports),
-        scratch=[pltpu.VMEM((exports, rows), BF16)],
     )
     far, near = (
         call(
@@ -306,7 +318,7 @@
             [((rim, width), BF16)],
             part,
             picked,
-            theirs,
+            *theirs,
             flops=rim * modes * width,
         )
         for name, start in (("far", 0), ("near", rim))
@@ -323,7 +335,7 @@
         connectivity,
         stress_coef,
         mode_rows,
-        theirs,
+        *theirs,
         total,
         flops=rows * modes * width + 4 * rows * elems * width,
         scratch=[pltpu.VMEM((2, rows, elems), BF16), pltpu.VMEM((width, rows), BF16)],

time: 41.6 us -> 42.1 us (1.012)
  starting transfers between devices: 3.2 us -> 4.13 us
    ppermute x1 -> x2, starting transfers between devices: 0.01 us -> 0.57 us  [local(): lax.ppermute(part, AXES, swap)]
  transfers between devices with their start and end apart: 3 -> 4, of which waited for: 2 -> 2; matrix products, arithmetic and copies ran while one was open for 0% -> 0% of each run, Pallas kernels for 7% -> 7%
where the time goes in v15:
time: 42.1 us; the launch traced here: 41.9 us
  blocking collectives  30.2 us (72%)
  Pallas kernels  4.49 us (11%)
  starting transfers between devices  4.13 us (10%)
  waiting for transfers between devices  2 us (5%)
  local copies, waits for them, and re-layouts  0.97 us (2%)
    all_to_all x1, blocking collectives, own_pseudo(): got = lax.all_to_all(sent, AXES, 0, 0)  18.3 us
    all_to_all x1, blocking collectives, local(): got = lax.all_to_all(block, AXES, 0, 0, axis_index_groups=groups)  11.9 us
    pallas_call x8, Pallas kernels, call(): pl.pallas_call(kernel, out_shape=shapes, in_specs=[whole()] * len(operand...  4.49 us
    ppermute x1, starting transfers between devices, local(): far = lax.ppermute(far, AXES, outer)  3.37 us
    ppermute x1, waiting for transfers between devices, local(): far = lax.ppermute(far, AXES, outer)  1.84 us
    unnamed x18, local copies, waits for them, and re-layouts  0.93 us
  transfers between devices with their start and end apart: 4, of which 2 were waited for; matrix products, arithmetic and copies ran while one was open for 0% of the time, Pallas kernels for 7%

profile of v15, /device:TPU:8, one launch (start us, length us, event | category | flops | bytes accessed | tf_op | source)
XLA Modules:
  0.0 41.9 jit_solution(7834758194075130282)
XLA Ops:
  0.0 0.0 copy-start.3
  0.0 0.0 copy-start.6
  0.0 0.9 %copy-done.3 = bf16[16,4096]{1,0:T(8,128)(2,1)S(1)} copy-done((bf16[16,4096]{1,0:T(8,128)(2,1)S(1)}, bf16[16,4096]{1,0:T(8,128)(2,1)}, u32[]{:S(2)}) %copy-start.3) | copy-done | bytes 131096
  0.9 0.0 copy-done.6
  0.9 0.0 copy-start.4
  0.9 0.0 copy-start.5
  0.9 0.0 copy-start.7
  0.9 0.0 copy-start.8
  1.0 18.3 %all_to_all.10.got_ref = bf16[32,48,128]{2,1,0:T(8,128)(2,1)S(1)} all-to-all(bf16[32,48,128]{2,1,0:T(8,128)(2,1)S(1)} %pack.1), channel_id=1, replica_groups=mesh['region'=8,'sub'=4] {'region','sub'}, dimensions={0} | all-to-all | bytes 786432 | tf_op jit(solution)/shard_map/all_to_all | solution.py:254
  19.3 0.0 copy-done.4
  19.3 0.0 copy-done.5
  19.3 0.0 copy-done.7
  19.3 0.0 copy-done.8
  19.3 0.0 copy-start
  19.3 0.4 pseudo.1
  19.7 11.9 %all_to_all.11 = bf16[8,256,128]{2,1,0:T(8,128)(2,1)S(1)} all-to-all(bf16[8,256,128]{2,1,0:T(8,128)(2,1)S(1)} %get-tuple-element.12), channel_id=1, replica_groups={{0,2,6,4,12,14,10,8},{1,3,7,5,13,15,11,9},{16,18,22,20,28,30,26,24},{17..., dimensions={0} | all-to-all | bytes 1048576 | tf_op jit(solution)/shard_map/all_to_all | solution.py:292
  31.6 0.0 copy-start.1
  31.6 0.0 copy-start.2
  31.6 0.1 collective-permute-start
  31.7 0.5 %collective-permute-start.1 = (bf16[1024,128]{1,0:T(8,128)(2,1)S(1)}, bf16[1024,128]{1,0:T(8,128)(2,1)S(1)}, u32[]{:S(2)}, u32[]{:S(2)}) collective-permute-start(bf16[1024,128]{1,0:T(8,128)(2,1)S(1)} %bitcast.12), channel_id=1, source_target_pairs={{0,1},{1,0},{2,3},{3,2},{4,5},{5,4},{6,7},{7,6},{8,9},{9,8},{10,11... | collective-permute-start | bytes 786440 | tf_op jit(solution)/shard_map/ppermute | solution.py:296
  32.2 0.0 copy-done
  32.2 1.2 %first.1 = (f32[512,128]{1,0:T(8,128)S(1)}, f32[128,128]{1,0:T(8,128)S(1)}, bf16[128,2048]{1,0:T(8,128)(2,1)S(1)}) custom-call(bf16[128,512]{1,0:T(8,128)(2,1)S(1)} %get-tuple-element.13.pick_ref, bf16[512,4096]{1,0:T(8,128)(2,1)S(1)} %copy-done, bf16[2048,128]{1,0:T(8,128)(2,1)S(1)} %bitcast.7), custom_call_target="tpu_custom_call" | custom-call | flops 536870912 | bytes 5701632 | tf_op jit(solution)/shard_map/first/pallas_call | solution.py:202
  33.4 0.0 collective-permute-done.low_ref
  33.5 0.2 collective-permute-done.1.high_ref
  33.6 0.2 near.1
  33.8 0.2 collective-permute-start.3
  34.0 0.2 far.1
  34.3 3.4 %collective-permute-start.2 = (bf16[64,128]{1,0:T(8,128)(2,1)S(1)}, bf16[64,128]{1,0:T(8,128)(2,1)S(1)}, u32[]{:S(2)}, u32[]{:S(2)}) collective-permute-start(bf16[64,128]{1,0:T(8,128)(2,1)S(1)} %far.1), channel_id=1, source_target_pairs={{1,2},{3,4},{5,6},{7,8},{9,10},{11,12},{13,14},{15,16},{17,18},{19... | collective-permute-start | bytes 49160 | tf_op jit(solution)/shard_map/ppermute | solution.py:330
  37.6 0.0 copy-done.1
  37.7 0.0 copy-done.2
  37.7 1.6 %own.1 = (f32[128,512]{1,0:T(8,128)S(1)}, bf16[256,512]{1,0:T(8,128)(2,1)S(1)}) custom-call(s32[4,512]{1,0:T(4,128)S(1)} %copy-done.1, f32[4,512]{1,0:T(4,128)S(1)} %copy-done.2, bf16[512,4096]{1,0:T(8,128)(2,1)S(1)} %copy-done, bf16[1024,128]{1,0:T(8,128)(2,1)S(1)} %collective-permute-done.low_ref, bf16[1024,128]{1,0:T(8,128)(2,1)S(1)} %collective-permute-done.1.high_ref, ...), custom_call_target="tpu_custom_call" | custom-call | flops 402653184 | bytes 5521408 | tf_op jit(solution)/shard_map/own/pallas_call | solution.py:202
  39.3 0.0 collective-permute-done.3.near_ref
  39.3 1.8 %collective-permute-done.2.far_ref = bf16[64,128]{1,0:T(8,128)(2,1)S(1)} collective-permute-done((bf16[64,128]{1,0:T(8,128)(2,1)S(1)}, bf16[64,128]{1,0:T(8,128)(2,1)S(1)}, u32[]{:S(2)}, u32[]{:S(2)}) %collective-permute-start.2) | collective-permute-done | bytes 16416 | tf_op jit(solution)/shard_map/ppermute | solution.py:330
  41.1 0.8 %power.1 = f32[2,512]{1,0:T(2,128)} custom-call(f32[128,512]{1,0:T(8,128)S(1)} %get-tuple-element.15.stress_ref, bf16[64,128]{1,0:T(8,128)(2,1)S(1)} %collective-permute-done.2.far_ref, bf16[64,128]{1,0:T(8,128)(2,1)S(1)} %collective-permute-done.3.near_ref, bf16[256,512]{1,0:T(8,128)(2,1)S(1)} %get-tuple-element.18.rim_ref), custom_call_target="tpu_custom_call" | custom-call | flops 33554432 | bytes 561152 | tf_op jit(solution)/shard_map/power/pallas_call | solution.py:202
  (3 shorter events, 0.1 us)
Async XLA Ops:
  0.0 0.9 %copy-start.3 = (bf16[16,4096]{1,0:T(8,128)(2,1)S(1)}, bf16[16,4096]{1,0:T(8,128)(2,1)}, u32[]{:S(2)}) copy-start(bf16[16,4096]{1,0:T(8,128)(2,1)} %rows_ref.1) | copy-start | bytes 393220
  0.0 0.9 %copy-start.6 = (bf16[16,128]{1,0:T(8,128)(2,1)S(1)}, bf16[16,128]{1,0:T(8,128)(2,1)}, u32[]{:S(2)}) copy-start(bf16[16,128]{1,0:T(8,128)(2,1)} %factor_ref.1) | copy-start | bytes 12292
  0.9 18.3 %copy-start.4 = (f32[4096]{0:T(1024)S(1)}, f32[4096]{0:T(1024)}, u32[]{:S(2)}) copy-start(f32[4096]{0:T(1024)} %param.12) | copy-start | bytes 49156
  0.9 18.3 %copy-start.5 = (f32[4096]{0:T(1024)S(1)}, f32[4096]{0:T(1024)}, u32[]{:S(2)}) copy-start(f32[4096]{0:T(1024)} %param.13) | copy-start | bytes 49156
  0.9 18.3 %copy-start.7 = (s32[128]{0:T(128)S(1)}, s32[128]{0:T(128)}, u32[]{:S(2)}) copy-start(s32[128]{0:T(128)} %param.15) | copy-start | bytes 1540
  0.9 18.3 %copy-start.8 = (f32[2]{0:T(128)S(1)}, f32[2]{0:T(128)}, u32[]{:S(2)}) copy-start(f32[2]{0:T(128)} %param.14) | copy-start | bytes 28
  19.3 12.9 %copy-start = (bf16[512,4096]{1,0:T(8,128)(2,1)S(1)}, bf16[512,4096]{1,0:T(8,128)(2,1)}, u32[]{:S(2)}) copy-start(bf16[512,4096]{1,0:T(8,128)(2,1)} %modes_ref.3) | copy-start | bytes 12582916
  31.6 6.0 %copy-start.1 = (s32[4,512]{1,0:T(4,128)S(1)}, s32[4,512]{1,0:T(4,128)}, u32[]{:S(2)}) copy-start(s32[4,512]{1,0:T(4,128)} %connect_ref.1) | copy-start | bytes 24580
  31.6 6.1 %copy-start.2 = (f32[4,512]{1,0:T(4,128)S(1)}, f32[4,512]{1,0:T(4,128)}, u32[]{:S(2)}) copy-start(f32[4,512]{1,0:T(4,128)} %coef_ref.1) | copy-start | bytes 24580
  31.6 1.8 %collective-permute-start = (bf16[1024,128]{1,0:T(8,128)(2,1)S(1)}, bf16[1024,128]{1,0:T(8,128)(2,1)S(1)}, u32[]{:S(2)}, u32[]{:S(2)}) collective-permute-start(bf16[1024,128]{1,0:T(8,128)(2,1)S(1)} %bitcast.13), channel_id=1, source_target_pairs={{0,1},{1,0},{2,3},{3,2},{4,5},{5,4},{6,7},{7,6},{8,9},{9,8},{10,11... | collective-permute-start | bytes 786440 | tf_op jit(solution)/shard_map/ppermute | solution.py:296
  31.7 1.9 %collective-permute-start.1 = (bf16[1024,128]{1,0:T(8,128)(2,1)S(1)}, bf16[1024,128]{1,0:T(8,128)(2,1)S(1)}, u32[]{:S(2)}, u32[]{:S(2)}) collective-permute-start(bf16[1024,128]{1,0:T(8,128)(2,1)S(1)} %bitcast.12), channel_id=1, source_target_pairs={{0,1},{1,0},{2,3},{3,2},{4,5},{5,4},{6,7},{7,6},{8,9},{9,8},{10,11... | collective-permute-start | bytes 786440 | tf_op jit(solution)/shard_map/ppermute | solution.py:296
  33.8 5.4 %collective-permute-start.3 = (bf16[64,128]{1,0:T(8,128)(2,1)S(1)}, bf16[64,128]{1,0:T(8,128)(2,1)S(1)}, u32[]{:S(2)}, u32[]{:S(2)}) collective-permute-start(bf16[64,128]{1,0:T(8,128)(2,1)S(1)} %near.1), channel_id=1, source_target_pairs={{0,1},{1,0},{2,3},{3,2},{4,5},{5,4},{6,7},{7,6},{8,9},{9,8},{10,11... | collective-permute-start | bytes 49160 | tf_op jit(solution)/shard_map/ppermute | solution.py:329
  34.3 6.9 %collective-permute-start.2 = (bf16[64,128]{1,0:T(8,128)(2,1)S(1)}, bf16[64,128]{1,0:T(8,128)(2,1)S(1)}, u32[]{:S(2)}, u32[]{:S(2)}) collective-permute-start(bf16[64,128]{1,0:T(8,128)(2,1)S(1)} %far.1), channel_id=1, source_target_pairs={{1,2},{3,4},{5,6},{7,8},{9,10},{11,12},{13,14},{15,16},{17,18},{19... | collective-permute-start | bytes 49160 | tf_op jit(solution)/shard_map/ppermute | solution.py:330

commit v16 on v15

--- a/solution.py
+++ b/solution.py
@@ -128,31 +128,27 @@
     for_core(depth, exported)
 
 
-def export_kernel(part_ref, picked_ref, low_ref, high_ref, export_ref, *, start):
+def export_kernel(part_ref, picked_ref, pseudo_ref, export_ref, *, start):
     here = slice(start, start + export_ref.shape[0])
-    cut = low_ref.shape[0]
-    export = part_ref[here, :] + jnp.dot(
-        picked_ref[here, :cut], low_ref[...], preferred_element_type=F32
-    )
     export_ref[...] = (
-        export + jnp.dot(picked_ref[here, cut:], high_ref[...], preferred_element_type=F32)
+        part_ref[here, :]
+        + jnp.dot(picked_ref[here, :], pseudo_ref[...], preferred_element_type=F32)
     ).astype(BF16)
 
 
 def own_kernel(
-    connect_ref, coef_ref, modes_ref, low_ref, high_ref, total_ref,
-    stress_ref, rim_ref, own_ref, table_ref,
+    connect_ref, coef_ref, modes_ref, pseudo_ref, total_ref, stress_ref, rim_ref, own_ref, table_ref
 ):
     rows = modes_ref.shape[0]
     elems = connect_ref.shape[1]
     rim = rim_ref.shape[0] // 4
     odd = lax.axis_index(AXES) % 2
 
-    cut = low_ref.shape[0]
-    total = total_ref[...]
-    for part, part_ref in enumerate((low_ref, high_ref)):
-        here = pl.ds(pl.multiple_of((2 * (1 - odd) + part) * cut, cut), cut)
-        total = total + jnp.dot(modes_ref[:, here], part_ref[...], preferred_element_type=F32)
+    depth = pseudo_ref.shape[0]
+    other = pl.ds(pl.multiple_of((1 - odd) * depth, depth), depth)
+    total = total_ref[...] + jnp.dot(
+        modes_ref[:, other], pseudo_ref[...], preferred_element_type=F32
+    )
     table_ref[...] = total.T.astype(BF16)
 
     def matrix(start, tall):
@@ -291,17 +287,14 @@
         block, pick = own_pseudo(*inputs, boundary_rows, rows, copies=8)
         got = lax.all_to_all(block, AXES, 0, 0, axis_index_groups=groups)
         mine = got.reshape(modes // 2, width)
-        cut = modes // 4
-        swap = [(i, i ^ 1) for i in range(devices)]
-        theirs = [lax.ppermute(part, AXES, swap) for part in (mine[:cut], mine[cut:])]
+        theirs = lax.ppermute(mine, AXES, [(i, i ^ 1) for i in range(devices)])
     else:
         pseudo = pseudo_by_sum(*inputs).reshape(2, modes // 2, width)
         core = lax.axis_index(AXES) % 2
         listed = jnp.where(core == 1, jnp.roll(boundary_rows, rim), boundary_rows)
         pick = (listed[:, None] == jnp.arange(rows)[None, :]).astype(BF16)
         mine = lax.dynamic_index_in_dim(pseudo, core, 0, keepdims=False)
-        other = lax.dynamic_index_in_dim(pseudo, 1 - core, 0, keepdims=False)
-        theirs = [other[: modes // 4], other[modes // 4 :]]
+        theirs = lax.dynamic_index_in_dim(pseudo, 1 - core, 0, keepdims=False)
     total, part, picked = call(
         first_kernel,
         "first",
@@ -318,7 +311,7 @@
             [((rim, width), BF16)],
             part,
             picked,
-            *theirs,
+            theirs,
             flops=rim * modes * width,
         )
         for name, start in (("far", 0), ("near", rim))
@@ -335,7 +328,7 @@
         connectivity,
         stress_coef,
         mode_rows,
-        *theirs,
+        theirs,
         total,
         flops=rows * modes * width + 4 * rows * elems * width,
         scratch=[pltpu.VMEM((2, rows, elems), BF16), pltpu.VMEM((width, rows), BF16)],

time: 42.1 us -> 42.1 us (level)
  waiting for transfers between devices: 2 us -> 2.68 us
  starting transfers between devices: 4.13 us -> 3.57 us
    ppermute x2 -> x1, starting transfers between devices: 0.57 us -> 0.01 us  [local(): theirs = lax.ppermute(mine, AXES, [(i, i ^ 1) for i in range(devices)])]
    ppermute x2 -> x1, waiting for transfers between devices: 0.16 us -> 0.68 us  [local(): theirs = lax.ppermute(mine, AXES, [(i, i ^ 1) for i in range(devices)])]
  transfers between devices with their start and end apart: 4 -> 3, of which waited for: 2 -> 2; matrix products, arithmetic and copies ran while one was open for 0% -> 0% of each run, Pallas kernels for 7% -> 7%
where the time goes in v16:
time: 42.1 us; the launch traced here: 41.9 us
  blocking collectives  30.2 us (72%)
  Pallas kernels  4.33 us (10%)
  starting transfers between devices  3.57 us (8%)
  waiting for transfers between devices  2.68 us (6%)
  local copies, waits for them, and re-layouts  0.94 us (2%)
    all_to_all x1, blocking collectives, own_pseudo(): got = lax.all_to_all(sent, AXES, 0, 0)  18.3 us
    all_to_all x1, blocking collectives, local(): got = lax.all_to_all(block, AXES, 0, 0, axis_index_groups=groups)  11.9 us
    pallas_call x8, Pallas kernels, call(): pl.pallas_call(kernel, out_shape=shapes, in_specs=[whole()] * len(operand...  4.33 us
    ppermute x1, starting transfers between devices, local(): far = lax.ppermute(far, AXES, outer)  3.37 us
    ppermute x1, waiting for transfers between devices, local(): far = lax.ppermute(far, AXES, outer)  2 us
    unnamed x18, local copies, waits for them, and re-layouts  0.94 us
  transfers between devices with their start and end apart: 3, of which 2 were waited for; matrix products, arithmetic and copies ran while one was open for 0% of the time, Pallas kernels for 7%

profile of v16, /device:TPU:8, one launch (start us, length us, event | category | flops | bytes accessed | tf_op | source)
XLA Modules:
  0.0 41.9 jit_solution(17376042922637592463)
XLA Ops:
  0.0 0.0 copy-start.3
  0.0 0.0 copy-start.6
  0.0 0.9 %copy-done.3 = bf16[16,4096]{1,0:T(8,128)(2,1)S(1)} copy-done((bf16[16,4096]{1,0:T(8,128)(2,1)S(1)}, bf16[16,4096]{1,0:T(8,128)(2,1)}, u32[]{:S(2)}) %copy-start.3) | copy-done | bytes 131096
  0.9 0.0 copy-done.6
  0.9 0.0 copy-start.4
  0.9 0.0 copy-start.5
  0.9 0.0 copy-start.7
  0.9 0.0 copy-start.8
  1.0 18.3 %all_to_all.10.got_ref = bf16[32,48,128]{2,1,0:T(8,128)(2,1)S(1)} all-to-all(bf16[32,48,128]{2,1,0:T(8,128)(2,1)S(1)} %pack.1), channel_id=1, replica_groups=mesh['region'=8,'sub'=4] {'region','sub'}, dimensions={0} | all-to-all | bytes 786432 | tf_op jit(solution)/shard_map/all_to_all | solution.py:250
  19.3 0.0 copy-done.4
  19.3 0.0 copy-done.5
  19.3 0.0 copy-done.7
  19.3 0.0 copy-done.8
  19.3 0.0 copy-start
  19.3 0.4 pseudo.1
  19.7 0.0 copy-start.1
  19.7 0.0 copy-start.2
  19.7 11.9 %all_to_all.11 = bf16[8,256,128]{2,1,0:T(8,128)(2,1)S(1)} all-to-all(bf16[8,256,128]{2,1,0:T(8,128)(2,1)S(1)} %get-tuple-element.12), channel_id=1, replica_groups={{0,2,6,4,12,14,10,8},{1,3,7,5,13,15,11,9},{16,18,22,20,28,30,26,24},{17..., dimensions={0} | all-to-all | bytes 1048576 | tf_op jit(solution)/shard_map/all_to_all | solution.py:288
  31.6 0.0 collective-permute-start
  31.6 0.0 copy-done
  31.6 1.2 %first.1 = (f32[512,128]{1,0:T(8,128)S(1)}, f32[128,128]{1,0:T(8,128)S(1)}, bf16[128,2048]{1,0:T(8,128)(2,1)S(1)}) custom-call(bf16[128,512]{1,0:T(8,128)(2,1)S(1)} %get-tuple-element.13.pick_ref, bf16[512,4096]{1,0:T(8,128)(2,1)S(1)} %copy-done, bf16[2048,128]{1,0:T(8,128)(2,1)S(1)} %bitcast.6), custom_call_target="tpu_custom_call" | custom-call | flops 536870912 | bytes 5701632 | tf_op jit(solution)/shard_map/first/pallas_call | solution.py:198
  32.9 0.7 %collective-permute-done.pseudo_ref = bf16[2048,128]{1,0:T(8,128)(2,1)S(1)} collective-permute-done((bf16[2048,128]{1,0:T(8,128)(2,1)S(1)}, bf16[2048,128]{1,0:T(8,128)(2,1)S(1)}, u32[]{:S(2)}, u32[]{:S(2)}) %collective-permute-start) | collective-permute-done | bytes 524320 | tf_op jit(solution)/shard_map/ppermute | solution.py:290
  33.5 0.2 near.1
  33.8 0.2 collective-permute-start.2
  34.0 0.2 far.1
  34.2 3.4 %collective-permute-start.1 = (bf16[64,128]{1,0:T(8,128)(2,1)S(1)}, bf16[64,128]{1,0:T(8,128)(2,1)S(1)}, u32[]{:S(2)}, u32[]{:S(2)}) collective-permute-start(bf16[64,128]{1,0:T(8,128)(2,1)S(1)} %far.1), channel_id=1, source_target_pairs={{1,2},{3,4},{5,6},{7,8},{9,10},{11,12},{13,14},{15,16},{17,18},{19... | collective-permute-start | bytes 49160 | tf_op jit(solution)/shard_map/ppermute | solution.py:323
  37.6 0.0 copy-done.1
  37.6 0.0 copy-done.2
  37.6 1.4 %own.1 = (f32[128,512]{1,0:T(8,128)S(1)}, bf16[256,512]{1,0:T(8,128)(2,1)S(1)}) custom-call(s32[4,512]{1,0:T(4,128)S(1)} %copy-done.1, f32[4,512]{1,0:T(4,128)S(1)} %copy-done.2, bf16[512,4096]{1,0:T(8,128)(2,1)S(1)} %copy-done, bf16[2048,128]{1,0:T(8,128)(2,1)S(1)} %collective-permute-done.pseudo_ref, f32[512,128]{1,0:T(8,128)S(1)} %get-tuple-element.14.total_ref), custom_call_target="tpu_custom_call" | custom-call | flops 402653184 | bytes 5521408 | tf_op jit(solution)/shard_map/own/pallas_call | solution.py:198
  39.0 0.0 collective-permute-done.2.near_ref
  39.0 2.0 %collective-permute-done.1.far_ref = bf16[64,128]{1,0:T(8,128)(2,1)S(1)} collective-permute-done((bf16[64,128]{1,0:T(8,128)(2,1)S(1)}, bf16[64,128]{1,0:T(8,128)(2,1)S(1)}, u32[]{:S(2)}, u32[]{:S(2)}) %collective-permute-start.1) | collective-permute-done | bytes 16416 | tf_op jit(solution)/shard_map/ppermute | solution.py:323
  41.0 0.8 %power.1 = f32[2,512]{1,0:T(2,128)} custom-call(f32[128,512]{1,0:T(8,128)S(1)} %get-tuple-element.15.stress_ref, bf16[64,128]{1,0:T(8,128)(2,1)S(1)} %collective-permute-done.1.far_ref, bf16[64,128]{1,0:T(8,128)(2,1)S(1)} %collective-permute-done.2.near_ref, bf16[256,512]{1,0:T(8,128)(2,1)S(1)} %get-tuple-element.18.rim_ref), custom_call_target="tpu_custom_call" | custom-call | flops 33554432 | bytes 561152 | tf_op jit(solution)/shard_map/power/pallas_call | solution.py:198
  (2 shorter events, 0.0 us)
Async XLA Ops:
  0.0 0.9 %copy-start.3 = (bf16[16,4096]{1,0:T(8,128)(2,1)S(1)}, bf16[16,4096]{1,0:T(8,128)(2,1)}, u32[]{:S(2)}) copy-start(bf16[16,4096]{1,0:T(8,128)(2,1)} %rows_ref.1) | copy-start | bytes 393220
  0.0 0.9 %copy-start.6 = (bf16[16,128]{1,0:T(8,128)(2,1)S(1)}, bf16[16,128]{1,0:T(8,128)(2,1)}, u32[]{:S(2)}) copy-start(bf16[16,128]{1,0:T(8,128)(2,1)} %factor_ref.1) | copy-start | bytes 12292
  0.9 18.3 %copy-start.4 = (f32[4096]{0:T(1024)S(1)}, f32[4096]{0:T(1024)}, u32[]{:S(2)}) copy-start(f32[4096]{0:T(1024)} %param.12) | copy-start | bytes 49156
  0.9 18.3 %copy-start.5 = (f32[4096]{0:T(1024)S(1)}, f32[4096]{0:T(1024)}, u32[]{:S(2)}) copy-start(f32[4096]{0:T(1024)} %param.13) | copy-start | bytes 49156
  0.9 18.3 %copy-start.7 = (s32[128]{0:T(128)S(1)}, s32[128]{0:T(128)}, u32[]{:S(2)}) copy-start(s32[128]{0:T(128)} %param.15) | copy-start | bytes 1540
  0.9 18.3 %copy-start.8 = (f32[2]{0:T(128)S(1)}, f32[2]{0:T(128)}, u32[]{:S(2)}) copy-start(f32[2]{0:T(128)} %param.14) | copy-start | bytes 28
  19.3 12.4 %copy-start = (bf16[512,4096]{1,0:T(8,128)(2,1)S(1)}, bf16[512,4096]{1,0:T(8,128)(2,1)}, u32[]{:S(2)}) copy-start(bf16[512,4096]{1,0:T(8,128)(2,1)} %modes_ref.3) | copy-start | bytes 12582916
  19.7 17.9 %copy-start.1 = (s32[4,512]{1,0:T(4,128)S(1)}, s32[4,512]{1,0:T(4,128)}, u32[]{:S(2)}) copy-start(s32[4,512]{1,0:T(4,128)} %connect_ref.1) | copy-start | bytes 24580
  19.7 17.9 %copy-start.2 = (f32[4,512]{1,0:T(4,128)S(1)}, f32[4,512]{1,0:T(4,128)}, u32[]{:S(2)}) copy-start(f32[4,512]{1,0:T(4,128)} %coef_ref.1) | copy-start | bytes 24580
  31.6 1.9 %collective-permute-start = (bf16[2048,128]{1,0:T(8,128)(2,1)S(1)}, bf16[2048,128]{1,0:T(8,128)(2,1)S(1)}, u32[]{:S(2)}, u32[]{:S(2)}) collective-permute-start(bf16[2048,128]{1,0:T(8,128)(2,1)S(1)} %bitcast.5), channel_id=1, source_target_pairs={{0,1},{1,0},{2,3},{3,2},{4,5},{5,4},{6,7},{7,6},{8,9},{9,8},{10,11... | collective-permute-start | bytes 1572872 | tf_op jit(solution)/shard_map/ppermute | solution.py:290
  33.8 5.3 %collective-permute-start.2 = (bf16[64,128]{1,0:T(8,128)(2,1)S(1)}, bf16[64,128]{1,0:T(8,128)(2,1)S(1)}, u32[]{:S(2)}, u32[]{:S(2)}) collective-permute-start(bf16[64,128]{1,0:T(8,128)(2,1)S(1)} %near.1), channel_id=1, source_target_pairs={{0,1},{1,0},{2,3},{3,2},{4,5},{5,4},{6,7},{7,6},{8,9},{9,8},{10,11... | collective-permute-start | bytes 49160 | tf_op jit(solution)/shard_map/ppermute | solution.py:322
  34.2 6.9 %collective-permute-start.1 = (bf16[64,128]{1,0:T(8,128)(2,1)S(1)}, bf16[64,128]{1,0:T(8,128)(2,1)S(1)}, u32[]{:S(2)}, u32[]{:S(2)}) collective-permute-start(bf16[64,128]{1,0:T(8,128)(2,1)S(1)} %far.1), channel_id=1, source_target_pairs={{1,2},{3,4},{5,6},{7,8},{9,10},{11,12},{13,14},{15,16},{17,18},{19... | collective-permute-start | bytes 49160 | tf_op jit(solution)/shard_map/ppermute | solution.py:323

commit v17 on v16

--- a/solution.py
+++ b/solution.py
@@ -128,7 +128,8 @@
     for_core(depth, exported)
 
 
-def export_kernel(part_ref, picked_ref, pseudo_ref, export_ref, *, start):
+def export_kernel(part_ref, picked_ref, pseudo_ref, *refs, start):
+    export_ref = refs[-1]
     here = slice(start, start + export_ref.shape[0])
     export_ref[...] = (
         part_ref[here, :]
@@ -304,18 +305,20 @@
         mine,
         flops=rows * modes * (width + exports),
     )
-    far, near = (
-        call(
+    def export(name, start, *after):
+        return call(
             functools.partial(export_kernel, start=start),
             name,
             [((rim, width), BF16)],
             part,
             picked,
             theirs,
+            *after,
             flops=rim * modes * width,
         )
-        for name, start in (("far", 0), ("near", rim))
-    )
+
+    far = export("far", 0)
+    near = export("near", rim, far)
     inner = [(i, i ^ 1) for i in range(devices)]
     outer = [(i, i + 1) for i in range(1, devices - 1, 2)]
     outer += [(j, i) for i, j in outer]

time: 42.1 us -> 41.6 us (0.988)
  no operation moved by 1% of the time
where the time goes in v17:
time: 41.6 us; the launch traced here: 41.4 us
  blocking collectives  30.2 us (73%)
  Pallas kernels  4.34 us (10%)
  starting transfers between devices  3.2 us (8%)
  waiting for transfers between devices  2.6 us (6%)
  local copies, waits for them, and re-layouts  0.94 us (2%)
    all_to_all x1, blocking collectives, own_pseudo(): got = lax.all_to_all(sent, AXES, 0, 0)  18.3 us
    all_to_all x1, blocking collectives, local(): got = lax.all_to_all(block, AXES, 0, 0, axis_index_groups=groups)  11.9 us
    pallas_call x8, Pallas kernels, call(): pl.pallas_call(kernel, out_shape=shapes, in_specs=[whole()] * len(operand...  4.34 us
    ppermute x1, starting transfers between devices, local(): far = lax.ppermute(far, AXES, outer)  3.13 us
    ppermute x1, waiting for transfers between devices, local(): far = lax.ppermute(far, AXES, outer)  1.93 us
    unnamed x18, local copies, waits for them, and re-layouts  0.94 us
  transfers between devices with their start and end apart: 3, of which 2 were waited for; matrix products, arithmetic and copies ran while one was open for 0% of the time, Pallas kernels for 7%

profile of v17, /device:TPU:8, one launch (start us, length us, event | category | flops | bytes accessed | tf_op | source)
XLA Modules:
  0.0 41.4 jit_solution(2477251016083042726)
XLA Ops:
  0.0 0.0 copy-start.3
  0.0 0.0 copy-start.6
  0.0 0.9 %copy-done.3 = bf16[16,4096]{1,0:T(8,128)(2,1)S(1)} copy-done((bf16[16,4096]{1,0:T(8,128)(2,1)S(1)}, bf16[16,4096]{1,0:T(8,128)(2,1)}, u32[]{:S(2)}) %copy-start.3) | copy-done | bytes 131096
  0.9 0.0 copy-done.6
  0.9 0.0 copy-start.4
  0.9 0.0 copy-start.5
  0.9 0.0 copy-start.7
  0.9 0.0 copy-start.8
  1.0 18.3 %all_to_all.10.got_ref = bf16[32,48,128]{2,1,0:T(8,128)(2,1)S(1)} all-to-all(bf16[32,48,128]{2,1,0:T(8,128)(2,1)S(1)} %pack.1), channel_id=1, replica_groups=mesh['region'=8,'sub'=4] {'region','sub'}, dimensions={0} | all-to-all | bytes 786432 | tf_op jit(solution)/shard_map/all_to_all | solution.py:251
  19.3 0.0 copy-done.4
  19.3 0.0 copy-done.5
  19.3 0.0 copy-done.7
  19.3 0.0 copy-done.8
  19.3 0.0 copy-start
  19.3 0.4 pseudo.1
  19.7 0.0 copy-start.1
  19.7 0.0 copy-start.2
  19.7 11.9 %all_to_all.11 = bf16[8,256,128]{2,1,0:T(8,128)(2,1)S(1)} all-to-all(bf16[8,256,128]{2,1,0:T(8,128)(2,1)S(1)} %get-tuple-element.12), channel_id=1, replica_groups={{0,2,6,4,12,14,10,8},{1,3,7,5,13,15,11,9},{16,18,22,20,28,30,26,24},{17..., dimensions={0} | all-to-all | bytes 1048576 | tf_op jit(solution)/shard_map/all_to_all | solution.py:289
  31.6 0.0 collective-permute-start
  31.6 0.0 copy-done
  31.6 1.2 %first.1 = (f32[512,128]{1,0:T(8,128)S(1)}, f32[128,128]{1,0:T(8,128)S(1)}, bf16[128,2048]{1,0:T(8,128)(2,1)S(1)}) custom-call(bf16[128,512]{1,0:T(8,128)(2,1)S(1)} %get-tuple-element.13.pick_ref, bf16[512,4096]{1,0:T(8,128)(2,1)S(1)} %copy-done, bf16[2048,128]{1,0:T(8,128)(2,1)S(1)} %bitcast.6), custom_call_target="tpu_custom_call" | custom-call | flops 536870912 | bytes 5701632 | tf_op jit(solution)/shard_map/first/pallas_call | solution.py:199
  32.9 0.7 %collective-permute-done.pseudo_ref = bf16[2048,128]{1,0:T(8,128)(2,1)S(1)} collective-permute-done((bf16[2048,128]{1,0:T(8,128)(2,1)S(1)}, bf16[2048,128]{1,0:T(8,128)(2,1)S(1)}, u32[]{:S(2)}, u32[]{:S(2)}) %collective-permute-start) | collective-permute-done | bytes 524320 | tf_op jit(solution)/shard_map/ppermute | solution.py:291
  33.5 0.2 far.1.refs_0_
  33.8 3.1 %collective-permute-start.1 = (bf16[64,128]{1,0:T(8,128)(2,1)S(1)}, bf16[64,128]{1,0:T(8,128)(2,1)S(1)}, u32[]{:S(2)}, u32[]{:S(2)}) collective-permute-start(bf16[64,128]{1,0:T(8,128)(2,1)S(1)} %far.1.refs_0_), channel_id=1, source_target_pairs={{1,2},{3,4},{5,6},{7,8},{9,10},{11,12},{13,14},{15,16},{17,18},{19... | collective-permute-start | bytes 49160 | tf_op jit(solution)/shard_map/ppermute | solution.py:326
  36.9 0.2 near.1
  37.1 0.1 collective-permute-start.2
  37.2 0.0 copy-done.1
  37.2 0.0 copy-done.2
  37.2 1.5 %own.1 = (f32[128,512]{1,0:T(8,128)S(1)}, bf16[256,512]{1,0:T(8,128)(2,1)S(1)}) custom-call(s32[4,512]{1,0:T(4,128)S(1)} %copy-done.1, f32[4,512]{1,0:T(4,128)S(1)} %copy-done.2, bf16[512,4096]{1,0:T(8,128)(2,1)S(1)} %copy-done, bf16[2048,128]{1,0:T(8,128)(2,1)S(1)} %collective-permute-done.pseudo_ref, f32[512,128]{1,0:T(8,128)S(1)} %get-tuple-element.14.total_ref), custom_call_target="tpu_custom_call" | custom-call | flops 402653184 | bytes 5521408 | tf_op jit(solution)/shard_map/own/pallas_call | solution.py:199
  38.7 0.0 collective-permute-done.2.near_ref
  38.7 1.9 %collective-permute-done.1.far_ref = bf16[64,128]{1,0:T(8,128)(2,1)S(1)} collective-permute-done((bf16[64,128]{1,0:T(8,128)(2,1)S(1)}, bf16[64,128]{1,0:T(8,128)(2,1)S(1)}, u32[]{:S(2)}, u32[]{:S(2)}) %collective-permute-start.1) | collective-permute-done | bytes 16416 | tf_op jit(solution)/shard_map/ppermute | solution.py:326
  40.6 0.8 %power.1 = f32[2,512]{1,0:T(2,128)} custom-call(f32[128,512]{1,0:T(8,128)S(1)} %get-tuple-element.15.stress_ref, bf16[64,128]{1,0:T(8,128)(2,1)S(1)} %collective-permute-done.1.far_ref, bf16[64,128]{1,0:T(8,128)(2,1)S(1)} %collective-permute-done.2.near_ref, bf16[256,512]{1,0:T(8,128)(2,1)S(1)} %get-tuple-element.18.rim_ref), custom_call_target="tpu_custom_call" | custom-call | flops 33554432 | bytes 561152 | tf_op jit(solution)/shard_map/power/pallas_call | solution.py:199
  (2 shorter events, 0.0 us)
Async XLA Ops:
  0.0 0.9 %copy-start.3 = (bf16[16,4096]{1,0:T(8,128)(2,1)S(1)}, bf16[16,4096]{1,0:T(8,128)(2,1)}, u32[]{:S(2)}) copy-start(bf16[16,4096]{1,0:T(8,128)(2,1)} %rows_ref.1) | copy-start | bytes 393220
  0.0 0.9 %copy-start.6 = (bf16[16,128]{1,0:T(8,128)(2,1)S(1)}, bf16[16,128]{1,0:T(8,128)(2,1)}, u32[]{:S(2)}) copy-start(bf16[16,128]{1,0:T(8,128)(2,1)} %factor_ref.1) | copy-start | bytes 12292
  0.9 18.3 %copy-start.4 = (f32[4096]{0:T(1024)S(1)}, f32[4096]{0:T(1024)}, u32[]{:S(2)}) copy-start(f32[4096]{0:T(1024)} %param.12) | copy-start | bytes 49156
  0.9 18.3 %copy-start.5 = (f32[4096]{0:T(1024)S(1)}, f32[4096]{0:T(1024)}, u32[]{:S(2)}) copy-start(f32[4096]{0:T(1024)} %param.13) | copy-start | bytes 49156
  0.9 18.3 %copy-start.7 = (s32[128]{0:T(128)S(1)}, s32[128]{0:T(128)}, u32[]{:S(2)}) copy-start(s32[128]{0:T(128)} %param.15) | copy-start | bytes 1540
  0.9 18.3 %copy-start.8 = (f32[2]{0:T(128)S(1)}, f32[2]{0:T(128)}, u32[]{:S(2)}) copy-start(f32[2]{0:T(128)} %param.14) | copy-start | bytes 28
  19.3 12.4 %copy-start = (bf16[512,4096]{1,0:T(8,128)(2,1)S(1)}, bf16[512,4096]{1,0:T(8,128)(2,1)}, u32[]{:S(2)}) copy-start(bf16[512,4096]{1,0:T(8,128)(2,1)} %modes_ref.3) | copy-start | bytes 12582916
  19.7 17.5 %copy-start.1 = (s32[4,512]{1,0:T(4,128)S(1)}, s32[4,512]{1,0:T(4,128)}, u32[]{:S(2)}) copy-start(s32[4,512]{1,0:T(4,128)} %connect_ref.1) | copy-start | bytes 24580
  19.7 17.5 %copy-start.2 = (f32[4,512]{1,0:T(4,128)S(1)}, f32[4,512]{1,0:T(4,128)}, u32[]{:S(2)}) copy-start(f32[4,512]{1,0:T(4,128)} %coef_ref.1) | copy-start | bytes 24580
  31.6 1.9 %collective-permute-start = (bf16[2048,128]{1,0:T(8,128)(2,1)S(1)}, bf16[2048,128]{1,0:T(8,128)(2,1)S(1)}, u32[]{:S(2)}, u32[]{:S(2)}) collective-permute-start(bf16[2048,128]{1,0:T(8,128)(2,1)S(1)} %bitcast.5), channel_id=1, source_target_pairs={{0,1},{1,0},{2,3},{3,2},{4,5},{5,4},{6,7},{7,6},{8,9},{9,8},{10,11... | collective-permute-start | bytes 1572872 | tf_op jit(solution)/shard_map/ppermute | solution.py:291
  33.8 6.9 %collective-permute-start.1 = (bf16[64,128]{1,0:T(8,128)(2,1)S(1)}, bf16[64,128]{1,0:T(8,128)(2,1)S(1)}, u32[]{:S(2)}, u32[]{:S(2)}) collective-permute-start(bf16[64,128]{1,0:T(8,128)(2,1)S(1)} %far.1.refs_0_), channel_id=1, source_target_pairs={{1,2},{3,4},{5,6},{7,8},{9,10},{11,12},{13,14},{15,16},{17,18},{19... | collective-permute-start | bytes 49160 | tf_op jit(solution)/shard_map/ppermute | solution.py:326
  37.1 1.6 %collective-permute-start.2 = (bf16[64,128]{1,0:T(8,128)(2,1)S(1)}, bf16[64,128]{1,0:T(8,128)(2,1)S(1)}, u32[]{:S(2)}, u32[]{:S(2)}) collective-permute-start(bf16[64,128]{1,0:T(8,128)(2,1)S(1)} %near.1), channel_id=1, source_target_pairs={{0,1},{1,0},{2,3},{3,2},{4,5},{5,4},{6,7},{7,6},{8,9},{9,8},{10,11... | collective-permute-start | bytes 49160 | tf_op jit(solution)/shard_map/ppermute | solution.py:325

commit v18 on v8

--- a/solution.py
+++ b/solution.py
@@ -33,6 +33,11 @@
     return device % 2 * 8 + (chip ^ (chip // 2) ^ (chip // 4))
 
 
+def exchange_order(devices):
+    chips = [place ^ (place // 2) for place in range(devices // 2)]
+    return [2 * chip + core for chip in chips for core in range(2)]
+
+
 def ones_kernel(ones_ref):
     ones_ref[...] = jnp.ones_like(ones_ref)
 
@@ -42,11 +47,11 @@
     rows = rows_ref.shape[0]
     parts = sent_ref.shape[1] // rows - 1
     factor = factor_ref[...] * ones_ref[0:1, :].astype(BF16)
-    for device in range(devices):
+    for place, device in enumerate(exchange_order(devices)):
         for part in range(parts):
             here = (slab_of(device) * parts + part) * width
-            sent_ref[device, part * rows : (part + 1) * rows, :] = rows_ref[:, here : here + width]
-        sent_ref[device, parts * rows :, :] = factor
+            sent_ref[place, part * rows : (part + 1) * rows, :] = rows_ref[:, here : here + width]
+        sent_ref[place, parts * rows :, :] = factor
 
 
 def pseudo_kernel(line_ref, freq_ref, damping_ref, got_ref, pseudo_ref, *, rows):
@@ -249,7 +254,7 @@
         input_factor,
         flops=LONG,
     )
-    got = lax.all_to_all(sent, AXES, 0, 0)
+    got = lax.all_to_all(sent, AXES, 0, 0, axis_index_groups=[exchange_order(devices)])
     return call(
         functools.partial(pseudo_kernel, rows=rows),
         "pseudo",

time: 41.7 us -> 41.7 us (level)
    all_to_all x1, blocking collectives: 18.3 us -> 17.3 us  [own_pseudo(): lax.all_to_all(sent, AXES, 0, 0, axis_index_groups=[exchange_order(device...]
    all_to_all x1, blocking collectives: 11.9 us -> 12.9 us  [local(): lax.all_to_all(own_pseudo(*inputs, copies=8), AXES, 0, 0, axis_index_grou...]
where the time goes in v18:
time: 41.7 us; the launch traced here: 41.5 us
  blocking collectives  30.2 us (72%)
  Pallas kernels  4.32 us (10%)
  starting transfers between devices  3.2 us (8%)
  waiting for transfers between devices  2.7 us (6%)
  local copies, waits for them, and re-layouts  0.95 us (2%)
    all_to_all x1, blocking collectives, own_pseudo(): lax.all_to_all(sent, AXES, 0, 0, axis_index_groups=[exchange_order(device...  17.3 us
    all_to_all x1, blocking collectives, local(): lax.all_to_all(own_pseudo(*inputs, copies=8), AXES, 0, 0, axis_index_grou...  12.9 us
    pallas_call x7, Pallas kernels, call(): pl.pallas_call(kernel, out_shape=shapes, in_specs=[whole()] * len(operand...  4.32 us
    ppermute x1, starting transfers between devices, local(): far = lax.ppermute(far, AXES, outer)  3.13 us
    ppermute x1, waiting for transfers between devices, local(): far = lax.ppermute(far, AXES, outer)  2.15 us
    unnamed x18, local copies, waits for them, and re-layouts  0.95 us
  transfers between devices with their start and end apart: 3, of which 2 were waited for; matrix products, arithmetic and copies ran while one was open for 0% of the time, Pallas kernels for 7%

profile of v18, /device:TPU:8, one launch (start us, length us, event | category | flops | bytes accessed | tf_op | source)
XLA Modules:
  0.0 41.5 jit_solution(12429939220384035241)
XLA Ops:
  0.0 0.0 copy-start.7
  0.0 0.0 copy-start.4
  0.0 0.7 %copy-done.7 = bf16[16,128]{1,0:T(8,128)(2,1)S(1)} copy-done((bf16[16,128]{1,0:T(8,128)(2,1)S(1)}, bf16[16,128]{1,0:T(8,128)(2,1)}, u32[]{:S(2)}) %copy-start.7) | copy-done | bytes 4120
  0.7 0.2 copy-done.4
  0.9 0.0 copy-start.5
  0.9 0.0 copy-start.6
  0.9 0.0 copy-start.8
  1.0 17.3 %all_to_all.10.got_ref = bf16[32,48,128]{2,1,0:T(8,128)(2,1)S(1)} all-to-all(bf16[32,48,128]{2,1,0:T(8,128)(2,1)S(1)} %pack.1), channel_id=1, replica_groups={{0,1,2,3,6,7,4,5,12,13,14,15,10,11,8,9,24,25,26,27,30,31,28,29,20,21,22..., dimensions={0} | all-to-all | bytes 786432 | tf_op jit(solution)/shard_map/all_to_all | solution.py:257
  18.3 0.0 copy-done.5
  18.3 0.0 copy-done.6
  18.3 0.0 copy-done.8
  18.3 0.0 copy-start
  18.3 0.0 copy-start.3
  18.4 0.3 pseudo.1
  18.7 0.0 copy-start.1
  18.7 0.0 copy-start.2
  18.7 12.9 %all_to_all.11 = bf16[8,256,128]{2,1,0:T(8,128)(2,1)S(1)} all-to-all(bf16[8,256,128]{2,1,0:T(8,128)(2,1)S(1)} %pseudo.1), channel_id=1, replica_groups={{0,2,6,4,12,14,10,8},{1,3,7,5,13,15,11,9},{16,18,22,20,28,30,26,24},{17..., dimensions={0} | all-to-all | bytes 1048576 | tf_op jit(solution)/shard_map/all_to_all | solution.py:293
  31.6 0.0 collective-permute-start
  31.6 0.0 copy-done
  31.6 0.0 copy-done.3
  31.6 1.4 %first.1 = (f32[512,128]{1,0:T(8,128)S(1)}, f32[128,128]{1,0:T(8,128)S(1)}, bf16[128,2048]{1,0:T(8,128)(2,1)S(1)}) custom-call(s32[1,128]{1,0:T(1,128)S(1)} %bitcast.7, bf16[512,4096]{1,0:T(8,128)(2,1)S(1)} %copy-done, bf16[2048,128]{1,0:T(8,128)(2,1)S(1)} %bitcast.6), custom_call_target="tpu_custom_call" | custom-call | flops 536870912 | bytes 5571072 | tf_op jit(solution)/shard_map/first/pallas_call | solution.py:207
  33.0 0.5 %collective-permute-done.pseudo_ref = bf16[2048,128]{1,0:T(8,128)(2,1)S(1)} collective-permute-done((bf16[2048,128]{1,0:T(8,128)(2,1)S(1)}, bf16[2048,128]{1,0:T(8,128)(2,1)S(1)}, u32[]{:S(2)}, u32[]{:S(2)}) %collective-permute-start) | collective-permute-done | bytes 524320 | tf_op jit(solution)/shard_map/ppermute | solution.py:295
  33.5 0.3 export.1
  33.8 3.1 %collective-permute-start.1 = (bf16[64,128]{1,0:T(8,128)(2,1)S(1)}, bf16[64,128]{1,0:T(8,128)(2,1)S(1)}, u32[]{:S(2)}, u32[]{:S(2)}) collective-permute-start(bf16[64,128]{1,0:T(8,128)(2,1)S(1)} %get-tuple-element.16), channel_id=1, source_target_pairs={{1,2},{3,4},{5,6},{7,8},{9,10},{11,12},{13,14},{15,16},{17,18},{19... | collective-permute-start | bytes 49160 | tf_op jit(solution)/shard_map/ppermute | solution.py:324
  37.0 0.1 collective-permute-start.2
  37.0 0.0 copy-done.1
  37.0 0.0 copy-done.2
  37.1 1.5 %own.1 = (f32[128,512]{1,0:T(8,128)S(1)}, bf16[256,512]{1,0:T(8,128)(2,1)S(1)}) custom-call(s32[4,512]{1,0:T(4,128)S(1)} %copy-done.1, f32[4,512]{1,0:T(4,128)S(1)} %copy-done.2, bf16[512,4096]{1,0:T(8,128)(2,1)S(1)} %copy-done, bf16[2048,128]{1,0:T(8,128)(2,1)S(1)} %collective-permute-done.pseudo_ref, f32[512,128]{1,0:T(8,128)S(1)} %get-tuple-element.12.total_ref), custom_call_target="tpu_custom_call" | custom-call | flops 402653184 | bytes 5521408 | tf_op jit(solution)/shard_map/own/pallas_call | solution.py:207
  38.5 2.2 %collective-permute-done.1.far_ref = bf16[64,128]{1,0:T(8,128)(2,1)S(1)} collective-permute-done((bf16[64,128]{1,0:T(8,128)(2,1)S(1)}, bf16[64,128]{1,0:T(8,128)(2,1)S(1)}, u32[]{:S(2)}, u32[]{:S(2)}) %collective-permute-start.1) | collective-permute-done | bytes 16416 | tf_op jit(solution)/shard_map/ppermute | solution.py:324
  40.7 0.0 collective-permute-done.2.near_ref
  40.7 0.8 %power.1 = f32[2,512]{1,0:T(2,128)} custom-call(f32[128,512]{1,0:T(8,128)S(1)} %get-tuple-element.13.stress_ref, bf16[64,128]{1,0:T(8,128)(2,1)S(1)} %collective-permute-done.1.far_ref, bf16[64,128]{1,0:T(8,128)(2,1)S(1)} %collective-permute-done.2.near_ref, bf16[256,512]{1,0:T(8,128)(2,1)S(1)} %get-tuple-element.18.rim_ref), custom_call_target="tpu_custom_call" | custom-call | flops 33554432 | bytes 561152 | tf_op jit(solution)/shard_map/power/pallas_call | solution.py:207
  (2 shorter events, 0.0 us)
Async XLA Ops:
  0.0 0.7 %copy-start.7 = (bf16[16,128]{1,0:T(8,128)(2,1)S(1)}, bf16[16,128]{1,0:T(8,128)(2,1)}, u32[]{:S(2)}) copy-start(bf16[16,128]{1,0:T(8,128)(2,1)} %factor_ref.1) | copy-start | bytes 12292
  0.0 0.9 %copy-start.4 = (bf16[16,4096]{1,0:T(8,128)(2,1)S(1)}, bf16[16,4096]{1,0:T(8,128)(2,1)}, u32[]{:S(2)}) copy-start(bf16[16,4096]{1,0:T(8,128)(2,1)} %rows_ref.1) | copy-start | bytes 393220
  0.9 17.4 %copy-start.5 = (f32[4096]{0:T(1024)S(1)}, f32[4096]{0:T(1024)}, u32[]{:S(2)}) copy-start(f32[4096]{0:T(1024)} %param.12) | copy-start | bytes 49156
  0.9 17.4 %copy-start.6 = (f32[4096]{0:T(1024)S(1)}, f32[4096]{0:T(1024)}, u32[]{:S(2)}) copy-start(f32[4096]{0:T(1024)} %param.13) | copy-start | bytes 49156
  0.9 17.4 %copy-start.8 = (f32[2]{0:T(128)S(1)}, f32[2]{0:T(128)}, u32[]{:S(2)}) copy-start(f32[2]{0:T(128)} %param.14) | copy-start | bytes 28
  18.3 13.3 %copy-start = (bf16[512,4096]{1,0:T(8,128)(2,1)S(1)}, bf16[512,4096]{1,0:T(8,128)(2,1)}, u32[]{:S(2)}) copy-start(bf16[512,4096]{1,0:T(8,128)(2,1)} %modes_ref.3) | copy-start | bytes 12582916
  18.3 13.2 %copy-start.3 = (s32[128]{0:T(128)S(1)}, s32[128]{0:T(128)}, u32[]{:S(2)}) copy-start(s32[128]{0:T(128)} %param.15) | copy-start | bytes 1540
  18.7 18.3 %copy-start.1 = (s32[4,512]{1,0:T(4,128)S(1)}, s32[4,512]{1,0:T(4,128)}, u32[]{:S(2)}) copy-start(s32[4,512]{1,0:T(4,128)} %connect_ref.1) | copy-start | bytes 24580
  18.7 18.3 %copy-start.2 = (f32[4,512]{1,0:T(4,128)S(1)}, f32[4,512]{1,0:T(4,128)}, u32[]{:S(2)}) copy-start(f32[4,512]{1,0:T(4,128)} %coef_ref.1) | copy-start | bytes 24580
  31.6 1.9 %collective-permute-start = (bf16[2048,128]{1,0:T(8,128)(2,1)S(1)}, bf16[2048,128]{1,0:T(8,128)(2,1)S(1)}, u32[]{:S(2)}, u32[]{:S(2)}) collective-permute-start(bf16[2048,128]{1,0:T(8,128)(2,1)S(1)} %bitcast.5), channel_id=1, source_target_pairs={{0,1},{1,0},{2,3},{3,2},{4,5},{5,4},{6,7},{7,6},{8,9},{9,8},{10,11... | collective-permute-start | bytes 1572872 | tf_op jit(solution)/shard_map/ppermute | solution.py:295
  33.8 6.9 %collective-permute-start.1 = (bf16[64,128]{1,0:T(8,128)(2,1)S(1)}, bf16[64,128]{1,0:T(8,128)(2,1)S(1)}, u32[]{:S(2)}, u32[]{:S(2)}) collective-permute-start(bf16[64,128]{1,0:T(8,128)(2,1)S(1)} %get-tuple-element.16), channel_id=1, source_target_pairs={{1,2},{3,4},{5,6},{7,8},{9,10},{11,12},{13,14},{15,16},{17,18},{19... | collective-permute-start | bytes 49160 | tf_op jit(solution)/shard_map/ppermute | solution.py:324
  37.0 3.7 %collective-permute-start.2 = (bf16[64,128]{1,0:T(8,128)(2,1)S(1)}, bf16[64,128]{1,0:T(8,128)(2,1)S(1)}, u32[]{:S(2)}, u32[]{:S(2)}) collective-permute-start(bf16[64,128]{1,0:T(8,128)(2,1)S(1)} %get-tuple-element.17), channel_id=1, source_target_pairs={{0,1},{1,0},{2,3},{3,2},{4,5},{5,4},{6,7},{7,6},{8,9},{9,8},{10,11... | collective-permute-start | bytes 49160 | tf_op jit(solution)/shard_map/ppermute | solution.py:323

commit v19 on v16

--- a/solution.py
+++ b/solution.py
@@ -128,12 +128,13 @@
     for_core(depth, exported)
 
 
-def export_kernel(part_ref, picked_ref, pseudo_ref, export_ref, *, start):
-    here = slice(start, start + export_ref.shape[0])
-    export_ref[...] = (
-        part_ref[here, :]
-        + jnp.dot(picked_ref[here, :], pseudo_ref[...], preferred_element_type=F32)
-    ).astype(BF16)
+def export_kernel(part_ref, picked_ref, pseudo_ref, far_ref, near_ref):
+    export = part_ref[...] + jnp.dot(
+        picked_ref[...], pseudo_ref[...], preferred_element_type=F32
+    )
+    rim = far_ref.shape[0]
+    far_ref[...] = export[:rim].astype(BF16)
+    near_ref[...] = export[rim:].astype(BF16)
 
 
 def own_kernel(
@@ -304,17 +305,14 @@
         mine,
         flops=rows * modes * (width + exports),
     )
-    far, near = (
-        call(
-            functools.partial(export_kernel, start=start),
-            name,
-            [((rim, width), BF16)],
-            part,
-            picked,
-            theirs,
-            flops=rim * modes * width,
-        )
-        for name, start in (("far", 0), ("near", rim))
+    far, near = call(
+        export_kernel,
+        "export",
+        [((rim, width), BF16)] * 2,
+        part,
+        picked,
+        theirs,
+        flops=exports * modes * width,
     )
     inner = [(i, i ^ 1) for i in range(devices)]
     outer = [(i, i + 1) for i in range(1, devices - 1, 2)]

time: 42.1 us -> 41.7 us (level)
    pallas_call x8 -> x7, Pallas kernels: 4.33 us -> 4.18 us  [call(): pl.pallas_call(kernel, out_shape=shapes, in_specs=[whole()] * len(operand...]
  transfers between devices with their start and end apart: 3 -> 3, of which waited for: 2 -> 2; matrix products, arithmetic and copies ran while one was open for 0% -> 0% of each run, Pallas kernels for 7% -> 6%
where the time goes in v19:
time: 41.7 us; the launch traced here: 41.5 us
  blocking collectives  30.2 us (72%)
  Pallas kernels  4.18 us (10%)
  starting transfers between devices  3.2 us (8%)
  waiting for transfers between devices  2.85 us (7%)
  local copies, waits for them, and re-layouts  0.94 us (2%)
    all_to_all x1, blocking collectives, own_pseudo(): got = lax.all_to_all(sent, AXES, 0, 0)  18.3 us
    all_to_all x1, blocking collectives, local(): got = lax.all_to_all(block, AXES, 0, 0, axis_index_groups=groups)  11.9 us
    pallas_call x7, Pallas kernels, call(): pl.pallas_call(kernel, out_shape=shapes, in_specs=[whole()] * len(operand...  4.18 us
    ppermute x1, starting transfers between devices, local(): far = lax.ppermute(far, AXES, outer)  3.13 us
    ppermute x1, waiting for transfers between devices, local(): far = lax.ppermute(far, AXES, outer)  2.17 us
    unnamed x18, local copies, waits for them, and re-layouts  0.94 us
  transfers between devices with their start and end apart: 3, of which 2 were waited for; matrix products, arithmetic and copies ran while one was open for 0% of the time, Pallas kernels for 6%

profile of v19, /device:TPU:8, one launch (start us, length us, event | category | flops | bytes accessed | tf_op | source)
XLA Modules:
  0.0 41.5 jit_solution(11475038539308343849)
XLA Ops:
  0.0 0.0 copy-start.3
  0.0 0.0 copy-start.6
  0.0 0.9 %copy-done.3 = bf16[16,4096]{1,0:T(8,128)(2,1)S(1)} copy-done((bf16[16,4096]{1,0:T(8,128)(2,1)S(1)}, bf16[16,4096]{1,0:T(8,128)(2,1)}, u32[]{:S(2)}) %copy-start.3) | copy-done | bytes 131096
  0.9 0.0 copy-done.6
  0.9 0.0 copy-start.4
  0.9 0.0 copy-start.5
  0.9 0.0 copy-start.7
  0.9 0.0 copy-start.8
  1.0 18.3 %all_to_all.10.got_ref = bf16[32,48,128]{2,1,0:T(8,128)(2,1)S(1)} all-to-all(bf16[32,48,128]{2,1,0:T(8,128)(2,1)S(1)} %pack.1), channel_id=1, replica_groups=mesh['region'=8,'sub'=4] {'region','sub'}, dimensions={0} | all-to-all | bytes 786432 | tf_op jit(solution)/shard_map/all_to_all | solution.py:251
  19.3 0.0 copy-done.4
  19.3 0.0 copy-done.5
  19.3 0.0 copy-done.7
  19.3 0.0 copy-done.8
  19.3 0.0 copy-start
  19.3 0.4 pseudo.1
  19.7 0.0 copy-start.1
  19.7 0.0 copy-start.2
  19.7 11.9 %all_to_all.11 = bf16[8,256,128]{2,1,0:T(8,128)(2,1)S(1)} all-to-all(bf16[8,256,128]{2,1,0:T(8,128)(2,1)S(1)} %get-tuple-element.14), channel_id=1, replica_groups={{0,2,6,4,12,14,10,8},{1,3,7,5,13,15,11,9},{16,18,22,20,28,30,26,24},{17..., dimensions={0} | all-to-all | bytes 1048576 | tf_op jit(solution)/shard_map/all_to_all | solution.py:289
  31.6 0.0 collective-permute-start
  31.6 0.0 copy-done
  31.6 1.2 %first.1 = (f32[512,128]{1,0:T(8,128)S(1)}, f32[128,128]{1,0:T(8,128)S(1)}, bf16[128,2048]{1,0:T(8,128)(2,1)S(1)}) custom-call(bf16[128,512]{1,0:T(8,128)(2,1)S(1)} %get-tuple-element.15.pick_ref, bf16[512,4096]{1,0:T(8,128)(2,1)S(1)} %copy-done, bf16[2048,128]{1,0:T(8,128)(2,1)S(1)} %bitcast.6), custom_call_target="tpu_custom_call" | custom-call | flops 536870912 | bytes 5701632 | tf_op jit(solution)/shard_map/first/pallas_call | solution.py:199
  32.9 0.7 %collective-permute-done.pseudo_ref = bf16[2048,128]{1,0:T(8,128)(2,1)S(1)} collective-permute-done((bf16[2048,128]{1,0:T(8,128)(2,1)S(1)}, bf16[2048,128]{1,0:T(8,128)(2,1)S(1)}, u32[]{:S(2)}, u32[]{:S(2)}) %collective-permute-start) | collective-permute-done | bytes 524320 | tf_op jit(solution)/shard_map/ppermute | solution.py:291
  33.5 0.3 export.1
  33.8 3.1 %collective-permute-start.1 = (bf16[64,128]{1,0:T(8,128)(2,1)S(1)}, bf16[64,128]{1,0:T(8,128)(2,1)S(1)}, u32[]{:S(2)}, u32[]{:S(2)}) collective-permute-start(bf16[64,128]{1,0:T(8,128)(2,1)S(1)} %get-tuple-element.20), channel_id=1, source_target_pairs={{1,2},{3,4},{5,6},{7,8},{9,10},{11,12},{13,14},{15,16},{17,18},{19... | collective-permute-start | bytes 49160 | tf_op jit(solution)/shard_map/ppermute | solution.py:321
  37.0 0.1 collective-permute-start.2
  37.0 0.0 copy-done.1
  37.0 0.0 copy-done.2
  37.1 1.4 %own.1 = (f32[128,512]{1,0:T(8,128)S(1)}, bf16[256,512]{1,0:T(8,128)(2,1)S(1)}) custom-call(s32[4,512]{1,0:T(4,128)S(1)} %copy-done.1, f32[4,512]{1,0:T(4,128)S(1)} %copy-done.2, bf16[512,4096]{1,0:T(8,128)(2,1)S(1)} %copy-done, bf16[2048,128]{1,0:T(8,128)(2,1)S(1)} %collective-permute-done.pseudo_ref, f32[512,128]{1,0:T(8,128)S(1)} %get-tuple-element.16.total_ref), custom_call_target="tpu_custom_call" | custom-call | flops 402653184 | bytes 5521408 | tf_op jit(solution)/shard_map/own/pallas_call | solution.py:199
  38.5 2.2 %collective-permute-done.1.far_ref = bf16[64,128]{1,0:T(8,128)(2,1)S(1)} collective-permute-done((bf16[64,128]{1,0:T(8,128)(2,1)S(1)}, bf16[64,128]{1,0:T(8,128)(2,1)S(1)}, u32[]{:S(2)}, u32[]{:S(2)}) %collective-permute-start.1) | collective-permute-done | bytes 16416 | tf_op jit(solution)/shard_map/ppermute | solution.py:321
  40.7 0.0 collective-permute-done.2.near_ref
  40.7 0.8 %power.1 = f32[2,512]{1,0:T(2,128)} custom-call(f32[128,512]{1,0:T(8,128)S(1)} %get-tuple-element.17.stress_ref, bf16[64,128]{1,0:T(8,128)(2,1)S(1)} %collective-permute-done.1.far_ref, bf16[64,128]{1,0:T(8,128)(2,1)S(1)} %collective-permute-done.2.near_ref, bf16[256,512]{1,0:T(8,128)(2,1)S(1)} %get-tuple-element.22.rim_ref), custom_call_target="tpu_custom_call" | custom-call | flops 33554432 | bytes 561152 | tf_op jit(solution)/shard_map/power/pallas_call | solution.py:199
  (2 shorter events, 0.0 us)
Async XLA Ops:
  0.0 0.9 %copy-start.3 = (bf16[16,4096]{1,0:T(8,128)(2,1)S(1)}, bf16[16,4096]{1,0:T(8,128)(2,1)}, u32[]{:S(2)}) copy-start(bf16[16,4096]{1,0:T(8,128)(2,1)} %rows_ref.1) | copy-start | bytes 393220
  0.0 0.9 %copy-start.6 = (bf16[16,128]{1,0:T(8,128)(2,1)S(1)}, bf16[16,128]{1,0:T(8,128)(2,1)}, u32[]{:S(2)}) copy-start(bf16[16,128]{1,0:T(8,128)(2,1)} %factor_ref.1) | copy-start | bytes 12292
  0.9 18.3 %copy-start.4 = (f32[4096]{0:T(1024)S(1)}, f32[4096]{0:T(1024)}, u32[]{:S(2)}) copy-start(f32[4096]{0:T(1024)} %param.12) | copy-start | bytes 49156
  0.9 18.3 %copy-start.5 = (f32[4096]{0:T(1024)S(1)}, f32[4096]{0:T(1024)}, u32[]{:S(2)}) copy-start(f32[4096]{0:T(1024)} %param.13) | copy-start | bytes 49156
  0.9 18.3 %copy-start.7 = (s32[128]{0:T(128)S(1)}, s32[128]{0:T(128)}, u32[]{:S(2)}) copy-start(s32[128]{0:T(128)} %param.15) | copy-start | bytes 1540
  0.9 18.3 %copy-start.8 = (f32[2]{0:T(128)S(1)}, f32[2]{0:T(128)}, u32[]{:S(2)}) copy-start(f32[2]{0:T(128)} %param.14) | copy-start | bytes 28
  19.3 12.4 %copy-start = (bf16[512,4096]{1,0:T(8,128)(2,1)S(1)}, bf16[512,4096]{1,0:T(8,128)(2,1)}, u32[]{:S(2)}) copy-start(bf16[512,4096]{1,0:T(8,128)(2,1)} %modes_ref.3) | copy-start | bytes 12582916
  19.7 17.4 %copy-start.1 = (s32[4,512]{1,0:T(4,128)S(1)}, s32[4,512]{1,0:T(4,128)}, u32[]{:S(2)}) copy-start(s32[4,512]{1,0:T(4,128)} %connect_ref.1) | copy-start | bytes 24580
  19.7 17.4 %copy-start.2 = (f32[4,512]{1,0:T(4,128)S(1)}, f32[4,512]{1,0:T(4,128)}, u32[]{:S(2)}) copy-start(f32[4,512]{1,0:T(4,128)} %coef_ref.1) | copy-start | bytes 24580
  31.6 1.9 %collective-permute-start = (bf16[2048,128]{1,0:T(8,128)(2,1)S(1)}, bf16[2048,128]{1,0:T(8,128)(2,1)S(1)}, u32[]{:S(2)}, u32[]{:S(2)}) collective-permute-start(bf16[2048,128]{1,0:T(8,128)(2,1)S(1)} %bitcast.5), channel_id=1, source_target_pairs={{0,1},{1,0},{2,3},{3,2},{4,5},{5,4},{6,7},{7,6},{8,9},{9,8},{10,11... | collective-permute-start | bytes 1572872 | tf_op jit(solution)/shard_map/ppermute | solution.py:291
  33.8 6.9 %collective-permute-start.1 = (bf16[64,128]{1,0:T(8,128)(2,1)S(1)}, bf16[64,128]{1,0:T(8,128)(2,1)S(1)}, u32[]{:S(2)}, u32[]{:S(2)}) collective-permute-start(bf16[64,128]{1,0:T(8,128)(2,1)S(1)} %get-tuple-element.20), channel_id=1, source_target_pairs={{1,2},{3,4},{5,6},{7,8},{9,10},{11,12},{13,14},{15,16},{17,18},{19... | collective-permute-start | bytes 49160 | tf_op jit(solution)/shard_map/ppermute | solution.py:321
  37.0 3.7 %collective-permute-start.2 = (bf16[64,128]{1,0:T(8,128)(2,1)S(1)}, bf16[64,128]{1,0:T(8,128)(2,1)S(1)}, u32[]{:S(2)}, u32[]{:S(2)}) collective-permute-start(bf16[64,128]{1,0:T(8,128)(2,1)S(1)} %get-tuple-element.21), channel_id=1, source_target_pairs={{0,1},{1,0},{2,3},{3,2},{4,5},{5,4},{6,7},{7,6},{8,9},{9,8},{10,11... | collective-permute-start | bytes 49160 | tf_op jit(solution)/shard_map/ppermute | solution.py:320

commit v20 on v8

--- a/solution.py
+++ b/solution.py
@@ -124,15 +124,9 @@
 
 
 def export_kernel(part_ref, picked_ref, pseudo_ref, far_ref, near_ref):
-    exports = part_ref.shape[0]
-    cut = pseudo_ref.shape[0] // 2
-    width = pseudo_ref.shape[1]
-    both = jnp.dot(
-        jnp.concatenate([picked_ref[:, :cut], picked_ref[:, cut:]], axis=0),
-        jnp.concatenate([pseudo_ref[:cut], pseudo_ref[cut:]], axis=1),
-        preferred_element_type=F32,
-    )
-    export = part_ref[...] + both[:exports, :width] + both[exports:, width:]
+    export = part_ref[...] + jnp.dot(
+        picked_ref[...], pseudo_ref[...], preferred_element_type=F32
+    )
     export = export.astype(BF16)
     odd = lax.axis_index(AXES) % 2 == 1
     rim = far_ref.shape[0]

time: 41.7 us -> 41.7 us (level)
  no operation moved by 1% of the time
where the time goes in v20:
time: 41.7 us; the launch traced here: 41.5 us
  blocking collectives  30.2 us (72%)
  Pallas kernels  4.29 us (10%)
  starting transfers between devices  3.2 us (8%)
  waiting for transfers between devices  2.7 us (6%)
  local copies, waits for them, and re-layouts  0.95 us (2%)
    all_to_all x1, blocking collectives, own_pseudo(): got = lax.all_to_all(sent, AXES, 0, 0)  18.3 us
    all_to_all x1, blocking collectives, local(): lax.all_to_all(own_pseudo(*inputs, copies=8), AXES, 0, 0, axis_index_grou...  11.9 us
    pallas_call x7, Pallas kernels, call(): pl.pallas_call(kernel, out_shape=shapes, in_specs=[whole()] * len(operand...  4.29 us
    ppermute x1, starting transfers between devices, local(): far = lax.ppermute(far, AXES, outer)  3.13 us
    ppermute x1, waiting for transfers between devices, local(): far = lax.ppermute(far, AXES, outer)  2.16 us
    unnamed x18, local copies, waits for them, and re-layouts  0.95 us
  transfers between devices with their start and end apart: 3, of which 2 were waited for; matrix products, arithmetic and copies ran while one was open for 0% of the time, Pallas kernels for 7%

profile of v20, /device:TPU:8, one launch (start us, length us, event | category | flops | bytes accessed | tf_op | source)
XLA Modules:
  0.0 41.5 jit_solution(4398434251393011594)
XLA Ops:
  0.0 0.0 copy-start.7
  0.0 0.0 copy-start.4
  0.0 0.7 %copy-done.7 = bf16[16,128]{1,0:T(8,128)(2,1)S(1)} copy-done((bf16[16,128]{1,0:T(8,128)(2,1)S(1)}, bf16[16,128]{1,0:T(8,128)(2,1)}, u32[]{:S(2)}) %copy-start.7) | copy-done | bytes 4120
  0.7 0.2 copy-done.4
  0.9 0.0 copy-start.5
  0.9 0.0 copy-start.6
  0.9 0.0 copy-start.8
  1.0 18.3 %all_to_all.10.got_ref = bf16[32,48,128]{2,1,0:T(8,128)(2,1)S(1)} all-to-all(bf16[32,48,128]{2,1,0:T(8,128)(2,1)S(1)} %pack.1), channel_id=1, replica_groups=mesh['region'=8,'sub'=4] {'region','sub'}, dimensions={0} | all-to-all | bytes 786432 | tf_op jit(solution)/shard_map/all_to_all | solution.py:246
  19.2 0.0 copy-done.5
  19.2 0.0 copy-done.6
  19.3 0.0 copy-done.8
  19.3 0.0 copy-start
  19.3 0.0 copy-start.3
  19.3 0.3 pseudo.1
  19.6 0.0 copy-start.1
  19.6 0.0 copy-start.2
  19.6 11.9 %all_to_all.11 = bf16[8,256,128]{2,1,0:T(8,128)(2,1)S(1)} all-to-all(bf16[8,256,128]{2,1,0:T(8,128)(2,1)S(1)} %pseudo.1), channel_id=1, replica_groups={{0,2,6,4,12,14,10,8},{1,3,7,5,13,15,11,9},{16,18,22,20,28,30,26,24},{17..., dimensions={0} | all-to-all | bytes 1048576 | tf_op jit(solution)/shard_map/all_to_all | solution.py:282
  31.6 0.0 collective-permute-start
  31.6 0.0 copy-done
  31.6 0.0 copy-done.3
  31.6 1.4 %first.1 = (f32[512,128]{1,0:T(8,128)S(1)}, f32[128,128]{1,0:T(8,128)S(1)}, bf16[128,2048]{1,0:T(8,128)(2,1)S(1)}) custom-call(s32[1,128]{1,0:T(1,128)S(1)} %bitcast.7, bf16[512,4096]{1,0:T(8,128)(2,1)S(1)} %copy-done, bf16[2048,128]{1,0:T(8,128)(2,1)S(1)} %bitcast.6), custom_call_target="tpu_custom_call" | custom-call | flops 536870912 | bytes 5571072 | tf_op jit(solution)/shard_map/first/pallas_call | solution.py:196
  33.0 0.5 %collective-permute-done.pseudo_ref = bf16[2048,128]{1,0:T(8,128)(2,1)S(1)} collective-permute-done((bf16[2048,128]{1,0:T(8,128)(2,1)S(1)}, bf16[2048,128]{1,0:T(8,128)(2,1)S(1)}, u32[]{:S(2)}, u32[]{:S(2)}) %collective-permute-start) | collective-permute-done | bytes 524320 | tf_op jit(solution)/shard_map/ppermute | solution.py:284
  33.5 0.3 export.1
  33.8 3.1 %collective-permute-start.1 = (bf16[64,128]{1,0:T(8,128)(2,1)S(1)}, bf16[64,128]{1,0:T(8,128)(2,1)S(1)}, u32[]{:S(2)}, u32[]{:S(2)}) collective-permute-start(bf16[64,128]{1,0:T(8,128)(2,1)S(1)} %get-tuple-element.16), channel_id=1, source_target_pairs={{1,2},{3,4},{5,6},{7,8},{9,10},{11,12},{13,14},{15,16},{17,18},{19... | collective-permute-start | bytes 49160 | tf_op jit(solution)/shard_map/ppermute | solution.py:313
  36.9 0.1 collective-permute-start.2
  37.0 0.0 copy-done.1
  37.0 0.0 copy-done.2
  37.0 1.5 %own.1 = (f32[128,512]{1,0:T(8,128)S(1)}, bf16[256,512]{1,0:T(8,128)(2,1)S(1)}) custom-call(s32[4,512]{1,0:T(4,128)S(1)} %copy-done.1, f32[4,512]{1,0:T(4,128)S(1)} %copy-done.2, bf16[512,4096]{1,0:T(8,128)(2,1)S(1)} %copy-done, bf16[2048,128]{1,0:T(8,128)(2,1)S(1)} %collective-permute-done.pseudo_ref, f32[512,128]{1,0:T(8,128)S(1)} %get-tuple-element.12.total_ref), custom_call_target="tpu_custom_call" | custom-call | flops 402653184 | bytes 5521408 | tf_op jit(solution)/shard_map/own/pallas_call | solution.py:196
  38.5 2.2 %collective-permute-done.1.far_ref = bf16[64,128]{1,0:T(8,128)(2,1)S(1)} collective-permute-done((bf16[64,128]{1,0:T(8,128)(2,1)S(1)}, bf16[64,128]{1,0:T(8,128)(2,1)S(1)}, u32[]{:S(2)}, u32[]{:S(2)}) %collective-permute-start.1) | collective-permute-done | bytes 16416 | tf_op jit(solution)/shard_map/ppermute | solution.py:313
  40.7 0.0 collective-permute-done.2.near_ref
  40.7 0.8 %power.1 = f32[2,512]{1,0:T(2,128)} custom-call(f32[128,512]{1,0:T(8,128)S(1)} %get-tuple-element.13.stress_ref, bf16[64,128]{1,0:T(8,128)(2,1)S(1)} %collective-permute-done.1.far_ref, bf16[64,128]{1,0:T(8,128)(2,1)S(1)} %collective-permute-done.2.near_ref, bf16[256,512]{1,0:T(8,128)(2,1)S(1)} %get-tuple-element.18.rim_ref), custom_call_target="tpu_custom_call" | custom-call | flops 33554432 | bytes 561152 | tf_op jit(solution)/shard_map/power/pallas_call | solution.py:196
  (2 shorter events, 0.0 us)
Async XLA Ops:
  0.0 0.7 %copy-start.7 = (bf16[16,128]{1,0:T(8,128)(2,1)S(1)}, bf16[16,128]{1,0:T(8,128)(2,1)}, u32[]{:S(2)}) copy-start(bf16[16,128]{1,0:T(8,128)(2,1)} %factor_ref.1) | copy-start | bytes 12292
  0.0 0.9 %copy-start.4 = (bf16[16,4096]{1,0:T(8,128)(2,1)S(1)}, bf16[16,4096]{1,0:T(8,128)(2,1)}, u32[]{:S(2)}) copy-start(bf16[16,4096]{1,0:T(8,128)(2,1)} %rows_ref.1) | copy-start | bytes 393220
  0.9 18.3 %copy-start.5 = (f32[4096]{0:T(1024)S(1)}, f32[4096]{0:T(1024)}, u32[]{:S(2)}) copy-start(f32[4096]{0:T(1024)} %param.12) | copy-start | bytes 49156
  0.9 18.3 %copy-start.6 = (f32[4096]{0:T(1024)S(1)}, f32[4096]{0:T(1024)}, u32[]{:S(2)}) copy-start(f32[4096]{0:T(1024)} %param.13) | copy-start | bytes 49156
  0.9 18.3 %copy-start.8 = (f32[2]{0:T(128)S(1)}, f32[2]{0:T(128)}, u32[]{:S(2)}) copy-start(f32[2]{0:T(128)} %param.14) | copy-start | bytes 28
  19.3 12.3 %copy-start = (bf16[512,4096]{1,0:T(8,128)(2,1)S(1)}, bf16[512,4096]{1,0:T(8,128)(2,1)}, u32[]{:S(2)}) copy-start(bf16[512,4096]{1,0:T(8,128)(2,1)} %modes_ref.3) | copy-start | bytes 12582916
  19.3 12.3 %copy-start.3 = (s32[128]{0:T(128)S(1)}, s32[128]{0:T(128)}, u32[]{:S(2)}) copy-start(s32[128]{0:T(128)} %param.15) | copy-start | bytes 1540
  19.6 17.4 %copy-start.1 = (s32[4,512]{1,0:T(4,128)S(1)}, s32[4,512]{1,0:T(4,128)}, u32[]{:S(2)}) copy-start(s32[4,512]{1,0:T(4,128)} %connect_ref.1) | copy-start | bytes 24580
  19.6 17.4 %copy-start.2 = (f32[4,512]{1,0:T(4,128)S(1)}, f32[4,512]{1,0:T(4,128)}, u32[]{:S(2)}) copy-start(f32[4,512]{1,0:T(4,128)} %coef_ref.1) | copy-start | bytes 24580
  31.6 1.9 %collective-permute-start = (bf16[2048,128]{1,0:T(8,128)(2,1)S(1)}, bf16[2048,128]{1,0:T(8,128)(2,1)S(1)}, u32[]{:S(2)}, u32[]{:S(2)}) collective-permute-start(bf16[2048,128]{1,0:T(8,128)(2,1)S(1)} %bitcast.5), channel_id=1, source_target_pairs={{0,1},{1,0},{2,3},{3,2},{4,5},{5,4},{6,7},{7,6},{8,9},{9,8},{10,11... | collective-permute-start | bytes 1572872 | tf_op jit(solution)/shard_map/ppermute | solution.py:284
  33.8 6.9 %collective-permute-start.1 = (bf16[64,128]{1,0:T(8,128)(2,1)S(1)}, bf16[64,128]{1,0:T(8,128)(2,1)S(1)}, u32[]{:S(2)}, u32[]{:S(2)}) collective-permute-start(bf16[64,128]{1,0:T(8,128)(2,1)S(1)} %get-tuple-element.16), channel_id=1, source_target_pairs={{1,2},{3,4},{5,6},{7,8},{9,10},{11,12},{13,14},{15,16},{17,18},{19... | collective-permute-start | bytes 49160 | tf_op jit(solution)/shard_map/ppermute | solution.py:313
  36.9 3.7 %collective-permute-start.2 = (bf16[64,128]{1,0:T(8,128)(2,1)S(1)}, bf16[64,128]{1,0:T(8,128)(2,1)S(1)}, u32[]{:S(2)}, u32[]{:S(2)}) collective-permute-start(bf16[64,128]{1,0:T(8,128)(2,1)S(1)} %get-tuple-element.17), channel_id=1, source_target_pairs={{0,1},{1,0},{2,3},{3,2},{4,5},{5,4},{6,7},{7,6},{8,9},{9,8},{10,11... | collective-permute-start | bytes 49160 | tf_op jit(solution)/shard_map/ppermute | solution.py:312
